TPU v7x, 32 devices: a whole 2x2x4 slice. The times are simulated.
32 devices in a mesh: sub: 4 (over x, core), tile: 8 (over z, y).
Axes of the slice: x: 2, y: 2, z: 4, core: 2. Of those that a mesh axis runs over, the one named last changes fastest.
Arguments:
- modes: bfloat16 [128, 768, 512], P(('sub', 'tile')), may hold values from -0.21875 to 0.21875
- coupling: bfloat16 [128, 8, 768, 128], P(('sub', 'tile')), may hold values from -0.796875 to 0.796875
- inv_eig: float32 [128, 512], P(('sub', 'tile')), may hold values from 0.1 to 1
- sub_rows: int32 [128], P(('sub', 'tile')), may hold values from 192 to 768
- adjacency: int32 [128, 8], P(('sub', 'tile')), may hold values from 0 to 511, as said below
- base_mass: float32 [512, 128, 128], P(('sub', 'tile')), may hold values from -0.5 to 0.5
- iface_modes: bfloat16 [65536, 2048], P(('sub', 'tile')), may hold values from -0.08984375 to 0.08984375
Outputs:
- reduced_mass: float32 [2048, 2048], P('sub', 'tile')
Inputs may be any that keep to these rules, and one draw needn't show every extreme that they name: `adjacency`: interface block b is owned by device b // 16 in the order of the joined axes sub+tile. The substructures of one device link only to blocks whose owners have the same tile index; at most 8 links of one device go to blocks of one owner device, and on every device some owner receives exactly 8.
All inputs are finite; a program needn't handle non-finite values.
Results may differ from a plain program's by a relative error of at most 0.004.
Values may be sent and summed in bfloat16 or wider, within the bound.
No kernel may reach another device: no remote copies, remote signals or barrier semaphores. Data moves between devices by JAX's collectives and lax.ppermute only.
A program may use at most 128 MiB of HBM per device.

v0:
```python
import jax
import jax.numpy as jnp
from jax import lax
from jax.sharding import PartitionSpec as P

CAP = 8


def on_device(modes, coupling, inv_eig, sub_rows, adjacency, base_mass, iface_modes):
    n_sub = lax.axis_size("sub")
    n_tile = lax.axis_size("tile")
    rows = modes.shape[1]
    block = base_mass.shape[1]
    blk_dev = base_mass.shape[0]
    width = iface_modes.shape[1]
    live = (jnp.arange(rows, dtype=jnp.int32)[None, :] < sub_rows[:, None]).astype(jnp.bfloat16)
    masked = modes * live[:, :, None]
    reduced = jnp.einsum("srm,sarc->samc", masked, coupling, preferred_element_type=jnp.float32)
    reduced_b = reduced.astype(jnp.bfloat16)
    weighted = (reduced * inv_eig[:, None, :, None]).astype(jnp.bfloat16)
    contrib = jnp.einsum(
        "samc,samd->sacd", weighted, reduced_b, preferred_element_type=jnp.float32
    ).astype(jnp.bfloat16)
    link_ids = adjacency.reshape(-1)
    count = link_ids.shape[0]
    target = link_ids // blk_dev // n_tile
    same = target[:, None] == target[None, :]
    before = jnp.arange(count)[None, :] < jnp.arange(count)[:, None]
    slot = jnp.sum((same & before).astype(jnp.int32), axis=1)
    place = jnp.arange(n_sub * CAP)[:, None] == (target * CAP + slot)[None, :]
    outgoing = jnp.dot(
        place.astype(jnp.bfloat16),
        contrib.reshape(count, block * block),
        preferred_element_type=jnp.float32,
    )
    outgoing = outgoing.astype(jnp.bfloat16).reshape(n_sub, CAP, block, block)
    out_ids = (jnp.sum(place.astype(jnp.int32) * (link_ids + 1)[None, :], axis=1) - 1).reshape(
        n_sub, CAP
    )
    arrived, arrived_ids = (
        lax.all_to_all(outgoing, "sub", split_axis=0, concat_axis=0, tiled=True),
        lax.all_to_all(out_ids, "sub", split_axis=0, concat_axis=0, tiled=True),
    )
    first_block = lax.axis_index(("sub", "tile")) * blk_dev
    local_ids = arrived_ids.reshape(-1) - first_block
    select = (jnp.arange(blk_dev)[:, None] == local_ids[None, :]).astype(jnp.bfloat16)
    added = jnp.dot(
        select, arrived.reshape(n_sub * CAP, block * block), preferred_element_type=jnp.float32
    )
    assembled = base_mass + added.reshape(blk_dev, block, block)
    mass_rounded = assembled.astype(jnp.bfloat16)
    psi_blocks = iface_modes.reshape(blk_dev, block, width)
    image = jnp.einsum("bij,bjk->bik", mass_rounded, psi_blocks, preferred_element_type=jnp.float32)
    image = image.astype(jnp.bfloat16).reshape(blk_dev * block, width)
    row_band = lax.psum_scatter(
        lax.dot_general(
            iface_modes, image, (((0,), (0,)), ((), ())), preferred_element_type=jnp.float32
        ).astype(jnp.bfloat16),
        "sub",
        scatter_dimension=0,
        tiled=True,
    ).astype(jnp.float32)
    reduced_mass = lax.psum_scatter(row_band, "tile", scatter_dimension=1, tiled=True)
    return reduced_mass


def solution(mesh):
    placed = (
        P(("sub", "tile"), None, None),
        P(("sub", "tile"), None, None, None),
        P(("sub", "tile"), None),
        P(("sub", "tile")),
        P(("sub", "tile"), None),
        P(("sub", "tile"), None, None),
        P(("sub", "tile"), None),
    )
    return jax.shard_map(
        on_device, mesh=mesh, in_specs=placed, out_specs=P("sub", "tile"), check_vma=False
    )
```

profile of v0, /device:TPU:0, one launch (start us, length us, event | category | flops | bytes accessed | tf_op | source)
XLA Modules:
  0.0 243.5 jit_solution(7252992361569614249)
XLA Ops:
  6.5 0.8 reshape.172
  7.3 0.2 convert_reduce_fusion
  7.5 0.1 select_reduce_fusion
  7.6 0.7 sub.31
  8.3 4.2 %all-to-all-start = ((s32[4,1,8]{2,1,0:T(1,128)}), s32[4,1,8]{2,1,0:T(1,128)S(1)}, u32[]{:S(2)}, u32[]{:S(2)}) async-start(s32[4,1,8]{2,1,0:T(1,128)} %bitcast), calls=%async_computation | async-start | bytes 4096 | tf_op jit(solution)/shard_map/all_to_all | solution.py:42
  12.5 0.7 fusion.28
  13.2 0.0 copy-start.1
  13.2 7.3 %fusion.6 = f32[4,512,8,128]{3,1,2,0:T(8,128)S(1)} fusion(bf16[4,8,768,128]{3,2,1,0:T(8,128)(2,1)} %param.8, bf16[4,768,512]{2,1,0:T(8,128)(2,1)} %param.7, bf16[4,768]{1,0:T(4,128)(2,1)S(1)} %fusion.28), kind=kOutput, calls=%fused_computation.9 | convolution fusion | flops 3227516928 | bytes 17831936 | tf_op jit(solution)/shard_map/srm,sarc->samc/dot_general | solution.py:18
  20.5 0.0 copy-done.1
  20.5 0.0 copy-start
  20.5 2.0 fusion.15
  22.5 1.7 fusion.20
  24.2 0.0 all-to-all-done
  24.2 3.5 %all-to-all-start.1 = ((bf16[4,8,128,128]{3,1,2,0:T(8,128)(2,1)}), bf16[4,8,128,128]{3,1,2,0:T(8,128)(2,1)S(1)}, u32[]{:S(2)}, u32[]{:S(2)}) async-start(bf16[4,8,128,128]{3,1,2,0:T(8,128)(2,1)} %fusion.20), calls=%async_computation.1 | async-start | bytes 2097152 | tf_op jit(solution)/shard_map/all_to_all | solution.py:41
  27.8 0.2 reduce-scatter.3.cloned.1.call-start
  28.0 0.1 sub.34
  28.1 14.1 %all-to-all-done.1 = bf16[4,8,128,128]{3,1,2,0:T(8,128)(2,1)S(1)} async-done(((bf16[4,8,128,128]{3,1,2,0:T(8,128)(2,1)}), bf16[4,8,128,128]{3,1,2,0:T(8,128)(2,1)S(1)}, u32[]{:S(2)}, u32[]{:S(2)}) %all-to-all-start.1) | async-done | bytes 1048608 | tf_op jit(solution)/shard_map/all_to_all | solution.py:41
  42.2 0.0 copy-done
  42.2 0.0 slice-start
  42.2 0.8 fusion.21
  43.0 0.0 slice-start.1
  43.0 6.1 %convolution_convert_fusion.1 = bf16[16,128,2048]{2,1,0:T(8,128)(2,1)S(1)} fusion(bf16[16,128,2048]{2,1,0:T(8,128)(2,1)} %bitcast.49, bf16[16,128,128]{2,0,1:T(8,128)(2,1)S(1)} %fusion.21), kind=kOutput, calls=%fused_computation.3 | convolution fusion | flops 1077936128 | bytes 17301504 | tf_op jit(solution)/shard_map/bij,bjk->bik/dot_general | solution.py:53
  49.1 0.0 slice-done
  49.1 0.0 slice-done.1
  49.1 20.6 %convert_bitcast_fusion = bf16[2048,2048]{0,1:T(8,128)(2,1)} fusion(bf16[2048,2048]{1,0:T(8,128)(2,1)S(1)} %bitcast.52, bf16[2048,2048]{1,0:T(8,128)(2,1)S(1)} %bitcast.51), kind=kOutput, calls=%fused_computation.1 | convolution fusion | flops 17184063488 | bytes 25165824 | tf_op jit(solution)/shard_map/dot_general | solution.py:56
  69.8 0.0 reduce-scatter.3.cloned.1.call-update
  69.8 0.0 reduce-scatter.5.cloned.1.call-start
  69.8 72.6 %reduce-scatter.3.cloned.1.call-done = bf16[512,2048]{0,1:T(8,128)(2,1)} async-done(((bf16[2048,2048]{0,1:T(8,128)(2,1)}), bf16[512,2048]{0,1:T(8,128)(2,1)}) %reduce-scatter.3.cloned.1.call-update) | async-done | bytes 2097168 | tf_op jit(solution)/shard_map/reduce_scatter | solution.py:55
  142.4 4.1 %convert_element_type.58 = f32[512,2048]{0,1:T(8,128)} convert(bf16[512,2048]{0,1:T(8,128)(2,1)} %reduce-scatter.3.cloned.1.call-done) | non-fusion elementwise | flops 1048576 | bytes 6291456 | tf_op jit(solution)/shard_map/convert_element_type | solution.py:62
  146.5 0.0 reduce-scatter.5.cloned.1.call-update
  146.6 88.0 %reduce-scatter.5.cloned.1.call-done = f32[512,256]{0,1:T(8,128)} async-done(((f32[512,2048]{0,1:T(8,128)}), f32[512,256]{0,1:T(8,128)}) %reduce-scatter.5.cloned.1.call-update) | async-done | bytes 524304 | tf_op jit(solution)/shard_map/reduce_scatter | solution.py:63
  234.6 2.0 copy.27
  (5 shorter events, 0.1 us)
Async XLA Ops:
  8.3 15.9 %all-to-all-start = ((s32[4,1,8]{2,1,0:T(1,128)}), s32[4,1,8]{2,1,0:T(1,128)S(1)}, u32[]{:S(2)}, u32[]{:S(2)}) async-start(s32[4,1,8]{2,1,0:T(1,128)} %bitcast), calls=%async_computation | async-start | bytes 4096 | tf_op jit(solution)/shard_map/all_to_all | solution.py:42
  13.2 7.3 %copy-start.1 = (f32[4,512]{1,0:T(4,128)S(1)}, f32[4,512]{1,0:T(4,128)}, u32[]{:S(2)}) copy-start(f32[4,512]{1,0:T(4,128)} %param.9) | copy-start | bytes 24580
  20.5 21.7 %copy-start = (f32[16,128,128]{2,1,0:T(8,128)S(1)}, f32[16,128,128]{2,1,0:T(8,128)}, u32[]{:S(2)}) copy-start(f32[16,128,128]{2,1,0:T(8,128)} %param.12) | copy-start | bytes 3145732
  24.2 18.0 %all-to-all-start.1 = ((bf16[4,8,128,128]{3,1,2,0:T(8,128)(2,1)}), bf16[4,8,128,128]{3,1,2,0:T(8,128)(2,1)S(1)}, u32[]{:S(2)}, u32[]{:S(2)}) async-start(bf16[4,8,128,128]{3,1,2,0:T(8,128)(2,1)} %fusion.20), calls=%async_computation.1 | async-start | bytes 2097152 | tf_op jit(solution)/shard_map/all_to_all | solution.py:41
  27.8 114.7 %reduce-scatter.3.cloned.1.call-start = ((), (), s32[]{:S(2)}) async-start(), calls=%async_computation.4 | async-start | bytes 10485760 | tf_op jit(solution)/shard_map/reduce_scatter | solution.py:55
  42.2 6.9 %slice-start = ((s8[8388608]{0:T(1024)(128)(4,1)}), s8[4194304]{0:T(1024)(128)(4,1)S(1)}, s32[]{:S(2)}) async-start(s8[8388608]{0:T(1024)(128)(4,1)} %bitcast.50), calls=%async_computation.6 | async-start | bytes 8388608
  43.0 6.1 %slice-start.1 = ((s8[8388608]{0:T(1024)(128)(4,1)}), s8[4194304]{0:T(1024)(128)(4,1)S(1)}, s32[]{:S(2)}) async-start(s8[8388608]{0:T(1024)(128)(4,1)} %bitcast.50), calls=%async_computation.7 | async-start | bytes 8388608
  69.8 164.8 %reduce-scatter.5.cloned.1.call-start = ((), (), s32[]{:S(2)}) async-start(), calls=%async_computation.5 | async-start | bytes 4718592 | tf_op jit(solution)/shard_map/reduce_scatter | solution.py:63
Sparse Core Ops, SparseCore 0:
  69.9 72.4 reduce-scatter.2
  146.7 87.8 reduce-scatter.4
where the time goes:
time: 244 us; the launch traced here: 243 us
  waiting for transfers between devices  175 us (72%)
  matrix products  38.5 us (16%)
  between operations  13.5 us (6%)
  starting transfers between devices  7.99 us (3%)
  other arithmetic  5.19 us (2%)
  local copies, waits for them, and re-layouts  3.57 us (1%)
    reduce_scatter x1, waiting for transfers between devices, on_device(): lax.psum_scatter(row_band, 'tile', scatter_dimension=1, tiled=True)  88 us
    reduce_scatter x1, waiting for transfers between devices, on_device(): lax.psum_scatter(lax.dot_general(iface_modes, image, (((0,), (0,)), ((),...  72.6 us
    dot_general x1, matrix products, on_device(): lax.dot_general(iface_modes, image, (((0,), (0,)), ((), ())), preferred_e...  20.6 us
    all_to_all x1, waiting for transfers between devices, on_device(): lax.all_to_all(outgoing, 'sub', split_axis=0, concat_axis=0, tiled=True)  14.1 us
    dot_general x1, matrix products, on_device(): jnp.einsum('srm,sarc->samc', masked, coupling, preferred_element_type=jnp...  7.27 us
    dot_general x1, matrix products, on_device(): jnp.einsum('bij,bjk->bik', mass_rounded, psi_blocks, preferred_element_ty...  6.1 us
  transfers between devices with their start and end apart: 4, of which 3 were waited for; matrix products, arithmetic and copies ran while one was open for 5% of the time, Pallas kernels for 0%

commit v1 on v0

v1 whole, which is shorter than its diff:
```python
import functools

import jax
import jax.numpy as jnp
from jax import lax
from jax.experimental import pallas as pl
from jax.experimental.pallas import tpu as pltpu
from jax.sharding import PartitionSpec as P

CAP = 8
CORES = 2
VMEM_LIMIT = 48 * 1024 * 1024


def params():
    return pltpu.CompilerParams(vmem_limit_bytes=VMEM_LIMIT)


def contrib_kernel(n_x, blk_dev, n_tile, me_ref, rows_ref, adj_ref, modes_ref, coup_ref, inv_ref, *rest):
    outs, count_ref = rest[:n_x], rest[n_x]
    s = pl.program_id(0)
    n_sub = n_x * CORES
    links, rows, block = coup_ref.shape[1:]

    @pl.when(s == 0)
    def _():
        for i in range(n_sub):
            count_ref[i] = 0

    live = lax.broadcasted_iota(jnp.int32, (rows, 1), 0) < rows_ref[s]
    modes = jnp.where(live, modes_ref[0], jnp.zeros((), modes_ref.dtype))
    inv = inv_ref[pl.ds(s, 1), :]
    my_x = me_ref[0] // CORES
    step = 2 if links % 2 == 0 else 1
    for a in range(0, links, step):
        pair = jnp.concatenate([coup_ref[0, a + i] for i in range(step)], axis=1)
        red = lax.dot_general(
            pair, modes, (((0,), (0,)), ((), ())), preferred_element_type=jnp.float32
        )
        weighted = (red * inv).astype(jnp.bfloat16)
        red_b = red.astype(jnp.bfloat16)
        for i in range(step):
            part = slice(i * block, (i + 1) * block)
            contrib = lax.dot_general(
                weighted[part], red_b[part], (((1,), (1,)), ((), ())),
                preferred_element_type=jnp.float32,
            ).astype(jnp.bfloat16)
            target = adj_ref[s, a + i] // (blk_dev * n_tile)
            slot = count_ref[target]
            count_ref[target] = slot + 1
            x_rel = (target // CORES) ^ my_x
            place = (target % CORES) * CAP + slot
            for xr in range(n_x):
                @pl.when(x_rel == xr)
                def _(xr=xr):
                    outs[xr][place] = contrib


def make_contrib(me, modes, coupling, inv_eig, sub_rows, adjacency, n_x, n_tile, blk_dev):
    subs, rows, width = modes.shape
    links, block = coupling.shape[1], coupling.shape[3]
    smem = pl.BlockSpec(memory_space=pltpu.SMEM)
    out = jax.ShapeDtypeStruct((CORES * CAP, block, block), jnp.bfloat16)
    return pl.pallas_call(
        functools.partial(contrib_kernel, n_x, blk_dev, n_tile),
        grid=(subs,),
        in_specs=[
            smem, smem, smem,
            pl.BlockSpec((1, rows, width), lambda s: (s, 0, 0)),
            pl.BlockSpec((1, links, rows, block), lambda s: (s, 0, 0, 0)),
            pl.BlockSpec(inv_eig.shape, lambda s: (0, 0)),
        ],
        out_specs=[pl.BlockSpec(out.shape, lambda s: (0, 0, 0))] * n_x,
        out_shape=[out] * n_x,
        scratch_shapes=[pltpu.SMEM((n_x * CORES,), jnp.int32)],
        compiler_params=params(),
        name="contrib",
    )(me, sub_rows, adjacency, modes, coupling, inv_eig)


def sums_kernel(n_x, blk_dev, n_tile, me_ref, base_ref, *rest):
    adj = rest[:n_x]
    arrived = rest[n_x:2 * n_x]
    total_ref, send_ref, count_ref = rest[2 * n_x:]
    my_x, my_core = me_ref[0] // CORES, me_ref[0] % CORES
    total_ref[0] = base_ref[...]
    total_ref[1] = jnp.zeros_like(base_ref)
    links = adj[0].shape[1]
    for xr in range(n_x):
        for i in range(CORES):
            count_ref[i] = 0

        def body(link, carry, xr=xr):
            ident = adj[xr][link // links, link % links]
            owner = ident // (blk_dev * n_tile)

            @pl.when(owner // CORES == my_x)
            def _():
                core = owner % CORES
                slot = count_ref[core]
                count_ref[core] = slot + 1
                rel, local = core ^ my_core, ident % blk_dev
                total_ref[rel, local] += arrived[xr][core * CAP + slot].astype(jnp.float32)
            return carry

        lax.fori_loop(0, adj[xr].shape[0] * links, body, 0)
    send_ref[...] = total_ref[...].astype(jnp.bfloat16)


def make_sums(me, base, adjs, arrived, n_x, n_tile):
    blk_dev, block = base.shape[:2]
    smem = pl.BlockSpec(memory_space=pltpu.SMEM)
    vmem = pl.BlockSpec(memory_space=pltpu.VMEM)
    shape = (CORES, blk_dev, block, block)
    return pl.pallas_call(
        functools.partial(sums_kernel, n_x, blk_dev, n_tile),
        in_specs=[smem, vmem] + [smem] * n_x + [vmem] * n_x,
        out_specs=[vmem, vmem],
        out_shape=[
            jax.ShapeDtypeStruct(shape, jnp.float32),
            jax.ShapeDtypeStruct(shape, jnp.bfloat16),
        ],
        scratch_shapes=[pltpu.SMEM((CORES,), jnp.int32)],
        compiler_params=params(),
        name="sums",
    )(me, base, *adjs, *arrived)


def turn_kernel(cols_ref, psi_ref, out_ref):
    out_ref[0] = psi_ref[...].T


def turn(cols, psi, width):
    groups = cols.shape[0]
    depth = psi.shape[0]
    piece = min(depth, 1024)
    return pl.pallas_call(
        turn_kernel,
        grid_spec=pltpu.PrefetchScalarGridSpec(
            num_scalar_prefetch=1,
            grid=(groups, depth // piece),
            in_specs=[pl.BlockSpec((piece, width), lambda g, k, cols: (k, cols[g]))],
            out_specs=pl.BlockSpec((1, width, piece), lambda g, k, cols: (g, 0, k)),
        ),
        out_shape=jax.ShapeDtypeStruct((groups, width, depth), psi.dtype),
        compiler_params=params(),
        cost_estimate=pl.CostEstimate(
            flops=0, bytes_accessed=4 * groups * width * depth, transcendentals=0
        ),
        name="turn",
    )(cols, psi)


def left_kernel(total_ref, got_ref, own_ref, other_ref, out_ref):
    block = total_ref.shape[2]
    zero = jnp.zeros((block, block), jnp.bfloat16)
    rows = own_ref.shape[0] * own_ref.shape[1]
    for rel, psi_t in enumerate((own_ref, other_ref)):
        mass = (total_ref[rel] + got_ref[1 - rel].astype(jnp.float32)).astype(jnp.bfloat16)
        pair = jnp.concatenate(
            [
                jnp.concatenate([mass[0], zero], axis=1),
                jnp.concatenate([zero, mass[1]], axis=1),
            ],
            axis=0,
        )
        out_ref[rel] = jnp.dot(
            psi_t[...].reshape(rows, 2 * block), pair, preferred_element_type=jnp.float32
        ).astype(jnp.bfloat16)


def make_left(total, got, own_t, other_t):
    _, blk_dev, block, _ = total.shape
    groups, width, depth = own_t.shape
    rows = groups * width
    mass = pl.BlockSpec((CORES, 2, block, block), lambda j: (0, j, 0, 0))
    side = pl.BlockSpec((groups, width, 2 * block), lambda j: (0, 0, j))
    return pl.pallas_call(
        left_kernel,
        grid=(blk_dev // 2,),
        in_specs=[mass, mass, side, side],
        out_specs=pl.BlockSpec((CORES, rows, 2 * block), lambda j: (0, 0, j)),
        out_shape=jax.ShapeDtypeStruct((CORES, rows, depth), jnp.bfloat16),
        compiler_params=params(),
        cost_estimate=pl.CostEstimate(
            flops=4 * CORES * rows * depth * block, bytes_accessed=8 * rows * depth,
            transcendentals=0,
        ),
        name="left",
    )(total, got, own_t, other_t)


def product_kernel(spans, cols_ref, left_ref, own_ref, other_ref, *outs):
    y = pl.program_id(0)
    for yy, (lo, hi) in enumerate(spans):
        @pl.when(y == yy)
        def _(yy=yy, lo=lo, hi=hi):
            res = jnp.dot(left_ref[0, lo:hi], own_ref[...], preferred_element_type=jnp.float32)
            res += jnp.dot(left_ref[1, lo:hi], other_ref[...], preferred_element_type=jnp.float32)
            outs[yy][...] = res.astype(outs[yy].dtype)


def product(cols, left, own, other, width, spans, dtype):
    _, rows, depth = left.shape
    side = pl.BlockSpec((depth, width), lambda y, cols: (0, cols[y]))
    return pl.pallas_call(
        functools.partial(product_kernel, spans),
        grid_spec=pltpu.PrefetchScalarGridSpec(
            num_scalar_prefetch=1,
            grid=(2,),
            in_specs=[pl.BlockSpec((CORES, rows, depth), lambda y, cols: (0, 0, 0)), side, side],
            out_specs=[
                pl.BlockSpec((hi - lo, width), lambda y, cols: (0, 0)) for lo, hi in spans
            ],
        ),
        out_shape=[jax.ShapeDtypeStruct((hi - lo, width), dtype) for lo, hi in spans],
        compiler_params=params(),
        cost_estimate=pl.CostEstimate(
            flops=sum(4 * CORES * (hi - lo) * width * depth // 2 for lo, hi in spans),
            bytes_accessed=4 * CORES * depth * width, transcendentals=0,
        ),
        name="product",
    )(cols, left, own, other)


def on_device(modes, coupling, inv_eig, sub_rows, adjacency, base_mass, iface_modes):
    n_sub = lax.axis_size("sub")
    n_tile = lax.axis_size("tile")
    n_x = n_sub // CORES
    n_z = n_tile // 2
    blk_dev, block = base_mass.shape[:2]
    width = iface_modes.shape[1]
    band, tile = width // n_sub, width // n_tile
    half = band // 2
    sub, at = lax.axis_index("sub"), lax.axis_index("tile")
    my_x, my_core = sub // CORES, sub % CORES
    me = sub.reshape(1)

    def swap_core(v):
        return lax.ppermute(v, "sub", [(i, i ^ 1) for i in range(n_sub)])

    def swap_x(v, d):
        return lax.ppermute(v, "sub", [(i, i ^ (d * CORES)) for i in range(n_sub)])

    def swap_tile(v, d):
        return lax.ppermute(v, "tile", [(i, i ^ d) for i in range(n_tile)])

    other = swap_core(iface_modes)
    adjs = [adjacency] + [swap_x(adjacency, d) for d in range(1, n_x)]
    sent = make_contrib(
        me, modes, coupling, inv_eig, sub_rows, adjacency, n_x, n_tile, blk_dev
    )
    arrived = [sent[0]] + [swap_x(sent[d], d) for d in range(1, n_x)]
    total, share = make_sums(me, base_mass, adjs, arrived, n_x, n_tile)
    got = swap_core(share)

    order = [(d, 0) for d in range(1, n_x)] + [(d, 1) for d in range(n_x)] + [(0, 0)]
    row_cols = jnp.stack([((my_x ^ d) * CORES + my_core) * 2 + p for d, p in order])
    row_cols = row_cols.astype(jnp.int32)
    own_t = turn(row_cols, iface_modes, half)
    other_t = turn(row_cols, other, half)
    left = make_left(total, got, own_t, other_t)

    first, both = (n_x - 1) * half, (2 * n_x - 1) * half
    rows = 2 * n_x * half
    final = None
    chunks = sorted(range(n_z), key=lambda z: (-min(z, 2), z))
    for z in chunks:
        cols = jnp.stack([at ^ (2 * z + y) for y in range(2)]).astype(jnp.int32)
        out0, out1 = product(
            cols, left, iface_modes, other, tile, [(0, first), (0, both)], jnp.bfloat16
        )
        go_x = jnp.concatenate([out0, out1[:first]], axis=1)
        got_x = [swap_x(go_x[(d - 1) * half:d * half], d) for d in range(1, n_x)]
        got_y = swap_tile(out1[first:], 1)
        keep0, keep1 = product(
            cols, left, iface_modes, other, tile, [(first, rows), (both, rows)], jnp.float32
        )
        sum_a = jnp.concatenate([keep0[n_x * half:], keep1], axis=1)
        for v in got_x:
            sum_a = sum_a + v.astype(jnp.float32)
        sum_b = keep0[:n_x * half] + got_y.astype(jnp.float32)
        next_y = swap_tile(sum_a[:, tile:].astype(jnp.bfloat16), 1)
        next_x = [
            swap_x(sum_b[d * half:(d + 1) * half].astype(jnp.bfloat16), d)
            for d in range(1, n_x)
        ]
        low = sum_a[:, :tile] + next_y.astype(jnp.float32)
        high = sum_b[:half]
        for v in next_x:
            high = high + v.astype(jnp.float32)
        mine = jnp.concatenate([low, high], axis=0)
        if z:
            mine = swap_tile(mine.astype(jnp.bfloat16), 2 * z).astype(jnp.float32)
        final = mine if final is None else final + mine
    return final


def solution(mesh):
    placed = (
        P(("sub", "tile"), None, None),
        P(("sub", "tile"), None, None, None),
        P(("sub", "tile"), None),
        P(("sub", "tile")),
        P(("sub", "tile"), None),
        P(("sub", "tile"), None, None),
        P(("sub", "tile"), None),
    )
    return jax.shard_map(
        on_device, mesh=mesh, in_specs=placed, out_specs=P("sub", "tile"), check_vma=False
    )
```

time: 244 us -> 173 us (0.71)
  waiting for transfers between devices: 175 us -> 35.5 us
  Pallas kernels: 0 us -> 98.8 us
  matrix products: 38.5 us -> 0 us
  starting transfers between devices: 7.99 us -> 25.4 us
  between operations: 13.5 us -> 0.51 us
  local copies, waits for them, and re-layouts: 3.57 us -> 8.26 us
  other arithmetic: 5.19 us -> 2.15 us
    reduce_scatter x2 -> x0, waiting for transfers between devices: 161 us -> none  [the longest x1 88 us: on_device(): lax.psum_scatter(row_band, 'tile', scatter_dimension=1, tiled=True)]
    pallas_call x0 -> x13, Pallas kernels: none -> 98.8 us  [the longest x8 57.8 us: product(): pl.pallas_call(functools.partial(product_kernel, spans), grid_spec=pltpu....]
    dot_general x6 -> x0, matrix products: 38.5 us -> none  [the longest x1 20.6 us: on_device(): lax.dot_general(iface_modes, image, (((0,), (0,)), ((), ())), preferred_e...]
    ppermute x0 -> x23, waiting for transfers between devices: none -> 35.5 us  [the longest x11 22.9 us: swap_tile(): return lax.ppermute(v, 'tile', [(i, i ^ d) for i in range(n_tile)])]
    ppermute x0 -> x23, starting transfers between devices: none -> 25.4 us  [the longest x11 13.7 us: swap_tile(): return lax.ppermute(v, 'tile', [(i, i ^ d) for i in range(n_tile)])]
    all_to_all x2 -> x0, waiting for transfers between devices: 14.1 us -> none  [the longest x1 14.1 us: on_device(): lax.all_to_all(outgoing, 'sub', split_axis=0, concat_axis=0, tiled=True)]
    unnamed x8 -> x14, local copies, waits for them, and re-layouts: 0.02 us -> 7.92 us
    all_to_all x2 -> x0, starting transfers between devices: 7.72 us -> none  [the longest x1 4.21 us: on_device(): lax.all_to_all(out_ids, 'sub', split_axis=0, concat_axis=0, tiled=True)]
  transfers between devices with their start and end apart: 4 -> 23, of which waited for: 3 -> 7; matrix products, arithmetic and copies ran while one was open for 5% -> 1% of each run, Pallas kernels for 0% -> 35%
where the time goes in v1:
time: 173 us; the launch traced here: 171 us
  Pallas kernels  98.8 us (57%)
  waiting for transfers between devices  35.5 us (21%)
  starting transfers between devices  25.4 us (15%)
  local copies, waits for them, and re-layouts  8.26 us (5%)
  other arithmetic  2.15 us (1%)
    pallas_call x8, Pallas kernels, product(): pl.pallas_call(functools.partial(product_kernel, spans), grid_spec=pltpu....  57.8 us
    ppermute x11, waiting for transfers between devices, swap_tile(): return lax.ppermute(v, 'tile', [(i, i ^ d) for i in range(n_tile)])  22.9 us
    pallas_call x1, Pallas kernels, make_contrib(): pl.pallas_call(functools.partial(contrib_kernel, n_x, blk_dev, n_tile), g...  14 us
    ppermute x11, starting transfers between devices, swap_tile(): return lax.ppermute(v, 'tile', [(i, i ^ d) for i in range(n_tile)])  13.7 us
    ppermute x10, waiting for transfers between devices, swap_x(): return lax.ppermute(v, 'sub', [(i, i ^ d * CORES) for i in range(n_sub)])  12.6 us
    pallas_call x2, Pallas kernels, turn(): pl.pallas_call(turn_kernel, grid_spec=pltpu.PrefetchScalarGridSpec(num_sc...  12.3 us
    ppermute x10, starting transfers between devices, swap_x(): return lax.ppermute(v, 'sub', [(i, i ^ d * CORES) for i in range(n_sub)])  11.2 us
    pallas_call x1, Pallas kernels, make_left(): pl.pallas_call(left_kernel, grid=(blk_dev // 2,), in_specs=[mass, mass, s...  10.4 us
  transfers between devices with their start and end apart: 23, of which 7 were waited for; matrix products, arithmetic and copies ran while one was open for 1% of the time, Pallas kernels for 35%

profile of v1, /device:TPU:0, one launch (start us, length us, event | category | flops | bytes accessed | tf_op | source)
XLA Modules:
  0.0 170.6 jit_solution(14669734854610566401)
XLA Ops:
  0.0 0.5 collective-permute-start.3
  0.5 1.9 %copy-done.2 = bf16[4,768,512]{2,1,0:T(8,128)(2,1)S(1)} copy-done((bf16[4,768,512]{2,1,0:T(8,128)(2,1)S(1)}, bf16[4,768,512]{2,1,0:T(8,128)(2,1)}, u32[]{:S(2)}) %copy-start.2) | copy-done | bytes 3145752
  2.3 0.7 copy-done.4
  3.0 0.7 copy-done.5
  3.7 0.7 copy-done.6
  4.4 14.0 %contrib.1 = (bf16[16,128,128]{2,1,0:T(8,128)(2,1)S(1)}, bf16[16,128,128]{2,1,0:T(8,128)(2,1)S(1)}) custom-call(s32[1]{0:T(128)} %bitcast.2.me_ref, s32[4]{0:T(128)S(1)} %copy-done.6, s32[4,8]{1,0:T(4,128)S(1)} %copy-done.5, bf16[4,768,512]{2,1,0:T(8,128)(2,1)S(1)} %copy-done.2, bf16[4,8,768,128]{3,2,1,0:T(8,128)(2,1)} %coup_ref.1, f32[4,512]{1,0:T(4,128)S(1)} %copy-done.4), custom_call_target="tpu_custom_call" | custom-call | tf_op jit(solution)/shard_map/contrib/pallas_call | solution.py:64
  18.4 2.6 %collective-permute-start.1 = (bf16[16,128,128]{2,1,0:T(8,128)(2,1)S(1)}, bf16[16,128,128]{2,1,0:T(8,128)(2,1)S(1)}, u32[]{:S(2)}, u32[]{:S(2)}) collective-permute-start(bf16[16,128,128]{2,1,0:T(8,128)(2,1)S(1)} %get-tuple-element.26), channel_id=1, source_target_pairs={{0,16},{8,24},{16,0},{24,8},{1,17},{9,25},{17,1},{25,9},{2,18},{10... | collective-permute-start | bytes 1572872 | tf_op jit(solution)/shard_map/ppermute | solution.py:243
  21.0 0.1 collective-permute-start
  21.0 12.5 %collective-permute-done.rest_1_ = s32[4,8]{1,0:T(4,128)S(1)} collective-permute-done((s32[4,8]{1,0:T(4,128)S(1)}, s32[4,8]{1,0:T(4,128)S(1)}, u32[]{:S(2)}, u32[]{:S(2)}) %collective-permute-start) | collective-permute-done | bytes 160 | tf_op jit(solution)/shard_map/ppermute | solution.py:243
  33.6 4.3 %sums.1 = (f32[2,16,128,128]{3,2,1,0:T(8,128)S(1)}, bf16[2,16,128,128]{3,2,1,0:T(8,128)(2,1)}) custom-call(s32[1]{0:T(128)} %bitcast.2.me_ref, f32[16,128,128]{2,1,0:T(8,128)S(1)} %copy-done.3, s32[4,8]{1,0:T(4,128)S(1)} %copy-done.5, s32[4,8]{1,0:T(4,128)S(1)} %collective-permute-done.rest_1_, bf16[16,128,128]{2,1,0:T(8,128)(2,1)S(1)} %get-tuple-element.25.rest_2_, ...), custom_call_target="tpu_custom_call" | custom-call | tf_op jit(solution)/shard_map/sums/pallas_call | solution.py:115
  38.0 6.1 %turn.2.own_ref = bf16[4,256,2048]{2,1,0:T(8,128)(2,1)S(1)} custom-call(s32[4]{0:T(128)S(1)} %pad_add_fusion.1.cols_ref, bf16[2048,2048]{1,0:T(8,128)(2,1)} %own_ref.15), custom_call_target="tpu_custom_call" | custom-call | bytes 8388608 | tf_op jit(solution)/shard_map/turn/pallas_call | solution.py:137
  44.1 2.0 %copy-done = bf16[4,256,2048]{2,1,0:T(8,128)(2,1)} copy-done((bf16[4,256,2048]{2,1,0:T(8,128)(2,1)}, bf16[4,256,2048]{2,1,0:T(8,128)(2,1)S(1)}, u32[]{:S(2)}) %copy-start) | copy-done | bytes 4194328
  46.4 6.1 %turn.3.other_ref = bf16[4,256,2048]{2,1,0:T(8,128)(2,1)S(1)} custom-call(s32[4]{0:T(128)S(1)} %pad_add_fusion.1.cols_ref, bf16[2048,2048]{1,0:T(8,128)(2,1)} %collective-permute-done.3.psi_ref.other_ref), custom_call_target="tpu_custom_call" | custom-call | bytes 8388608 | tf_op jit(solution)/shard_map/turn/pallas_call | solution.py:137
  52.6 2.0 %copy-done.1 = bf16[4,256,2048]{2,1,0:T(8,128)(2,1)} copy-done((bf16[4,256,2048]{2,1,0:T(8,128)(2,1)}, bf16[4,256,2048]{2,1,0:T(8,128)(2,1)S(1)}, u32[]{:S(2)}) %copy-start.1) | copy-done | bytes 4194328
  54.6 10.4 %left.1.left_ref = bf16[2,1024,2048]{2,1,0:T(8,128)(2,1)} custom-call(f32[2,16,128,128]{3,2,1,0:T(8,128)S(1)} %get-tuple-element.27.total_ref, bf16[2,16,128,128]{3,2,1,0:T(8,128)(2,1)S(1)} %collective-permute-done.2.got_ref, bf16[4,256,2048]{2,1,0:T(8,128)(2,1)} %copy-done, bf16[4,256,2048]{2,1,0:T(8,128)(2,1)} %copy-done.1), custom_call_target="tpu_custom_call" | custom-call | flops 2147483648 | bytes 16777216 | tf_op jit(solution)/shard_map/left/pallas_call | solution.py:178
  65.0 7.2 %product.9 = (bf16[256,256]{1,0:T(8,128)(2,1)S(1)}, bf16[768,256]{1,0:T(8,128)(2,1)S(1)}) custom-call(s32[2]{0:T(128)S(1)} %pad_add_fusion.cols_ref, bf16[2,1024,2048]{2,1,0:T(8,128)(2,1)} %left.1.left_ref, bf16[2048,2048]{1,0:T(8,128)(2,1)} %own_ref.15, bf16[2048,2048]{1,0:T(8,128)(2,1)} %collective-permute-done.3.psi_ref.other_ref), custom_call_target="tpu_custom_call" | custom-call | flops 2147483648 | bytes 4194304 | tf_op jit(solution)/shard_map/product/pallas_call | solution.py:206
  72.2 7.2 %product.11 = (bf16[256,256]{1,0:T(8,128)(2,1)S(1)}, bf16[768,256]{1,0:T(8,128)(2,1)S(1)}) custom-call(s32[2]{0:T(128)S(1)} %pad_add_fusion.2.cols_ref, bf16[2,1024,2048]{2,1,0:T(8,128)(2,1)} %left.1.left_ref, bf16[2048,2048]{1,0:T(8,128)(2,1)} %own_ref.15, bf16[2048,2048]{1,0:T(8,128)(2,1)} %collective-permute-done.3.psi_ref.other_ref), custom_call_target="tpu_custom_call" | custom-call | flops 2147483648 | bytes 4194304 | tf_op jit(solution)/shard_map/product/pallas_call | solution.py:206
  79.5 7.2 %product.13 = (bf16[256,256]{1,0:T(8,128)(2,1)S(1)}, bf16[768,256]{1,0:T(8,128)(2,1)S(1)}) custom-call(s32[2]{0:T(128)S(1)} %pad_add_fusion.3.cols_ref, bf16[2,1024,2048]{2,1,0:T(8,128)(2,1)} %left.1.left_ref, bf16[2048,2048]{1,0:T(8,128)(2,1)} %own_ref.15, bf16[2048,2048]{1,0:T(8,128)(2,1)} %collective-permute-done.3.psi_ref.other_ref), custom_call_target="tpu_custom_call" | custom-call | flops 2147483648 | bytes 4194304 | tf_op jit(solution)/shard_map/product/pallas_call | solution.py:206
  86.8 7.2 %product.15 = (bf16[256,256]{1,0:T(8,128)(2,1)S(1)}, bf16[768,256]{1,0:T(8,128)(2,1)S(1)}) custom-call(s32[2]{0:T(128)S(1)} %pad_add_fusion.4.cols_ref, bf16[2,1024,2048]{2,1,0:T(8,128)(2,1)} %left.1.left_ref, bf16[2048,2048]{1,0:T(8,128)(2,1)} %own_ref.15, bf16[2048,2048]{1,0:T(8,128)(2,1)} %collective-permute-done.3.psi_ref.other_ref), custom_call_target="tpu_custom_call" | custom-call | flops 2147483648 | bytes 4194304 | tf_op jit(solution)/shard_map/product/pallas_call | solution.py:206
  94.0 1.8 %collective-permute-start.4 = (bf16[256,512]{1,0:T(8,128)(2,1)S(1)}, bf16[256,512]{1,0:T(8,128)(2,1)S(1)}, u32[]{:S(2)}, u32[]{:S(2)}) collective-permute-start(bf16[256,512]{1,0:T(8,128)(2,1)S(1)} %pad_maximum_fusion), channel_id=1, source_target_pairs={{0,16},{8,24},{16,0},{24,8},{1,17},{9,25},{17,1},{25,9},{2,18},{10... | collective-permute-start | bytes 786440 | tf_op jit(solution)/shard_map/ppermute | solution.py:243
  95.9 7.4 %product.8 = (f32[768,256]{1,0:T(8,128)S(1)}, f32[256,256]{1,0:T(8,128)S(1)}) custom-call(s32[2]{0:T(128)S(1)} %pad_add_fusion.cols_ref, bf16[2,1024,2048]{2,1,0:T(8,128)(2,1)} %left.1.left_ref, bf16[2048,2048]{1,0:T(8,128)(2,1)} %own_ref.15, bf16[2048,2048]{1,0:T(8,128)(2,1)} %collective-permute-done.3.psi_ref.other_ref), custom_call_target="tpu_custom_call" | custom-call | flops 2147483648 | bytes 4194304 | tf_op jit(solution)/shard_map/product/pallas_call | solution.py:206
  103.3 1.6 collective-permute-start.6
  104.9 0.6 collective-permute-start.9
  105.5 7.2 %product.10 = (f32[768,256]{1,0:T(8,128)S(1)}, f32[256,256]{1,0:T(8,128)S(1)}) custom-call(s32[2]{0:T(128)S(1)} %pad_add_fusion.2.cols_ref, bf16[2,1024,2048]{2,1,0:T(8,128)(2,1)} %left.1.left_ref, bf16[2048,2048]{1,0:T(8,128)(2,1)} %own_ref.15, bf16[2048,2048]{1,0:T(8,128)(2,1)} %collective-permute-done.3.psi_ref.other_ref), custom_call_target="tpu_custom_call" | custom-call | flops 2147483648 | bytes 4194304 | tf_op jit(solution)/shard_map/product/pallas_call | solution.py:206
  112.7 0.3 collective-permute-start.11
  113.1 1.8 %collective-permute-start.14 = (bf16[256,512]{1,0:T(8,128)(2,1)S(1)}, bf16[256,512]{1,0:T(8,128)(2,1)S(1)}, u32[]{:S(2)}, u32[]{:S(2)}) collective-permute-start(bf16[256,512]{1,0:T(8,128)(2,1)S(1)} %pad_maximum_fusion.4), channel_id=1, source_target_pairs={{0,16},{8,24},{16,0},{24,8},{1,17},{9,25},{17,1},{25,9},{2,18},{10... | collective-permute-start | bytes 786440 | tf_op jit(solution)/shard_map/ppermute | solution.py:243
  114.9 7.2 %product.14 = (f32[768,256]{1,0:T(8,128)S(1)}, f32[256,256]{1,0:T(8,128)S(1)}) custom-call(s32[2]{0:T(128)S(1)} %pad_add_fusion.4.cols_ref, bf16[2,1024,2048]{2,1,0:T(8,128)(2,1)} %left.1.left_ref, bf16[2048,2048]{1,0:T(8,128)(2,1)} %own_ref.15, bf16[2048,2048]{1,0:T(8,128)(2,1)} %collective-permute-done.3.psi_ref.other_ref), custom_call_target="tpu_custom_call" | custom-call | flops 2147483648 | bytes 4194304 | tf_op jit(solution)/shard_map/product/pallas_call | solution.py:206
  122.1 7.2 %product.12 = (f32[768,256]{1,0:T(8,128)S(1)}, f32[256,256]{1,0:T(8,128)S(1)}) custom-call(s32[2]{0:T(128)S(1)} %pad_add_fusion.3.cols_ref, bf16[2,1024,2048]{2,1,0:T(8,128)(2,1)} %left.1.left_ref, bf16[2048,2048]{1,0:T(8,128)(2,1)} %own_ref.15, bf16[2048,2048]{1,0:T(8,128)(2,1)} %collective-permute-done.3.psi_ref.other_ref), custom_call_target="tpu_custom_call" | custom-call | flops 2147483648 | bytes 4194304 | tf_op jit(solution)/shard_map/product/pallas_call | solution.py:206
  129.4 1.6 collective-permute-start.16
  131.0 0.6 collective-permute-start.19
  131.7 0.3 collective-permute-start.21
  132.1 6.6 %collective-permute-done.16 = bf16[512,256]{1,0:T(8,128)(2,1)S(1)} collective-permute-done((bf16[512,256]{1,0:T(8,128)(2,1)S(1)}, bf16[512,256]{1,0:T(8,128)(2,1)S(1)}, u32[]{:S(2)}, u32[]{:S(2)}) %collective-permute-start.16) | collective-permute-done | bytes 262176 | tf_op jit(solution)/shard_map/ppermute | solution.py:246
  138.7 1.5 collective-permute-start.5
  140.3 0.6 collective-permute-start.7
  141.0 0.3 collective-permute-start.10
  141.5 1.8 %collective-permute-start.12 = (bf16[256,256]{1,0:T(8,128)(2,1)S(1)}, bf16[256,256]{1,0:T(8,128)(2,1)S(1)}, u32[]{:S(2)}, u32[]{:S(2)}) collective-permute-start(bf16[256,256]{1,0:T(8,128)(2,1)S(1)} %slice.188), channel_id=1, source_target_pairs={{0,16},{8,24},{16,0},{24,8},{1,17},{9,25},{17,1},{25,9},{2,18},{10... | collective-permute-start | bytes 393224 | tf_op jit(solution)/shard_map/ppermute | solution.py:243
  143.4 0.9 collective-permute-done.21
  144.3 1.5 collective-permute-start.15
  145.9 1.2 collective-permute-done.5
  147.1 0.3 collective-permute-start.17
  147.5 1.9 %collective-permute-start.20 = (bf16[256,256]{1,0:T(8,128)(2,1)S(1)}, bf16[256,256]{1,0:T(8,128)(2,1)S(1)}, u32[]{:S(2)}, u32[]{:S(2)}) collective-permute-start(bf16[256,256]{1,0:T(8,128)(2,1)S(1)} %slice.185), channel_id=1, source_target_pairs={{0,1},{1,0},{2,3},{3,2},{4,5},{5,4},{6,7},{7,6},{8,9},{9,8},{10,11... | collective-permute-start | bytes 393224 | tf_op jit(solution)/shard_map/ppermute | solution.py:246
  149.3 0.6 collective-permute-done.10
  150.0 0.9 collective-permute-start.22
  151.0 2.7 %collective-permute-start.8 = (bf16[512,256]{1,0:T(8,128)(2,1)S(1)}, bf16[512,256]{1,0:T(8,128)(2,1)S(1)}, u32[]{:S(2)}, u32[]{:S(2)}) collective-permute-start(bf16[512,256]{1,0:T(8,128)(2,1)S(1)} %pad_maximum_fusion.1), channel_id=1, source_target_pairs={{0,4},{1,5},{2,6},{3,7},{4,0},{5,1},{6,2},{7,3},{8,12},{9,13},{10,... | collective-permute-start | bytes 786440 | tf_op jit(solution)/shard_map/ppermute | solution.py:246
  153.7 2.1 %collective-permute-start.13 = (bf16[512,256]{1,0:T(8,128)(2,1)S(1)}, bf16[512,256]{1,0:T(8,128)(2,1)S(1)}, u32[]{:S(2)}, u32[]{:S(2)}) collective-permute-start(bf16[512,256]{1,0:T(8,128)(2,1)S(1)} %pad_maximum_fusion.3), channel_id=1, source_target_pairs={{0,6},{1,7},{2,4},{3,5},{4,2},{5,3},{6,0},{7,1},{8,14},{9,15},{10,... | collective-permute-start | bytes 786440 | tf_op jit(solution)/shard_map/ppermute | solution.py:246
  156.2 12.0 %collective-permute-done.8 = bf16[512,256]{1,0:T(8,128)(2,1)S(1)} collective-permute-done((bf16[512,256]{1,0:T(8,128)(2,1)S(1)}, bf16[512,256]{1,0:T(8,128)(2,1)S(1)}, u32[]{:S(2)}, u32[]{:S(2)}) %collective-permute-start.8) | collective-permute-done | bytes 262176 | tf_op jit(solution)/shard_map/ppermute | solution.py:246
  168.1 1.6 collective-permute-done.18
  169.7 0.9 maximum_add_fusion.4
  (74 shorter events, 1.7 us)
Async XLA Ops:
  0.0 46.4 %collective-permute-start.3 = (bf16[2048,2048]{1,0:T(8,128)(2,1)}, bf16[2048,2048]{1,0:T(8,128)(2,1)}, u32[]{:S(2)}, u32[]{:S(2)}) collective-permute-start(bf16[2048,2048]{1,0:T(8,128)(2,1)} %own_ref.15), channel_id=1, source_target_pairs={{0,8},{8,0},{16,24},{24,16},{1,9},{9,1},{17,25},{25,17},{2,10},{10... | collective-permute-start | bytes 25165832 | tf_op jit(solution)/shard_map/ppermute | solution.py:240
  0.5 1.9 %copy-start.2 = (bf16[4,768,512]{2,1,0:T(8,128)(2,1)S(1)}, bf16[4,768,512]{2,1,0:T(8,128)(2,1)}, u32[]{:S(2)}) copy-start(bf16[4,768,512]{2,1,0:T(8,128)(2,1)} %modes_ref.1) | copy-start | bytes 9437188
  2.3 0.7 copy-start.4
  3.0 0.7 copy-start.5
  3.7 0.7 copy-start.6
  4.4 29.2 %copy-start.3 = (f32[16,128,128]{2,1,0:T(8,128)S(1)}, f32[16,128,128]{2,1,0:T(8,128)}, u32[]{:S(2)}) copy-start(f32[16,128,128]{2,1,0:T(8,128)} %base_ref.1) | copy-start | bytes 3145732
  18.4 15.2 %collective-permute-start.1 = (bf16[16,128,128]{2,1,0:T(8,128)(2,1)S(1)}, bf16[16,128,128]{2,1,0:T(8,128)(2,1)S(1)}, u32[]{:S(2)}, u32[]{:S(2)}) collective-permute-start(bf16[16,128,128]{2,1,0:T(8,128)(2,1)S(1)} %get-tuple-element.26), channel_id=1, source_target_pairs={{0,16},{8,24},{16,0},{24,8},{1,17},{9,25},{17,1},{25,9},{2,18},{10... | collective-permute-start | bytes 1572872 | tf_op jit(solution)/shard_map/ppermute | solution.py:243
  21.0 12.6 %collective-permute-start = (s32[4,8]{1,0:T(4,128)S(1)}, s32[4,8]{1,0:T(4,128)S(1)}, u32[]{:S(2)}, u32[]{:S(2)}) collective-permute-start(s32[4,8]{1,0:T(4,128)S(1)} %copy-done.5), channel_id=1, source_target_pairs={{0,16},{8,24},{16,0},{24,8},{1,17},{9,25},{17,1},{25,9},{2,18},{10... | collective-permute-start | bytes 392 | tf_op jit(solution)/shard_map/ppermute | solution.py:243
  37.9 16.7 %collective-permute-start.2 = (bf16[2,16,128,128]{3,2,1,0:T(8,128)(2,1)}, bf16[2,16,128,128]{3,2,1,0:T(8,128)(2,1)S(1)}, u32[]{:S(2)}, u32[]{:S(2)}) collective-permute-start(bf16[2,16,128,128]{3,2,1,0:T(8,128)(2,1)} %get-tuple-element.28), channel_id=1, source_target_pairs={{0,8},{8,0},{16,24},{24,16},{1,9},{9,1},{17,25},{25,17},{2,10},{10... | collective-permute-start | bytes 3145736 | tf_op jit(solution)/shard_map/ppermute | solution.py:240
  44.1 2.0 %copy-start = (bf16[4,256,2048]{2,1,0:T(8,128)(2,1)}, bf16[4,256,2048]{2,1,0:T(8,128)(2,1)S(1)}, u32[]{:S(2)}) copy-start(bf16[4,256,2048]{2,1,0:T(8,128)(2,1)S(1)} %turn.2.own_ref) | copy-start | bytes 12582916
  52.5 2.0 %copy-start.1 = (bf16[4,256,2048]{2,1,0:T(8,128)(2,1)}, bf16[4,256,2048]{2,1,0:T(8,128)(2,1)S(1)}, u32[]{:S(2)}) copy-start(bf16[4,256,2048]{2,1,0:T(8,128)(2,1)S(1)} %turn.3.other_ref) | copy-start | bytes 12582916
  94.0 37.7 %collective-permute-start.4 = (bf16[256,512]{1,0:T(8,128)(2,1)S(1)}, bf16[256,512]{1,0:T(8,128)(2,1)S(1)}, u32[]{:S(2)}, u32[]{:S(2)}) collective-permute-start(bf16[256,512]{1,0:T(8,128)(2,1)S(1)} %pad_maximum_fusion), channel_id=1, source_target_pairs={{0,16},{8,24},{16,0},{24,8},{1,17},{9,25},{17,1},{25,9},{2,18},{10... | collective-permute-start | bytes 786440 | tf_op jit(solution)/shard_map/ppermute | solution.py:243
  103.3 26.1 %collective-permute-start.6 = (bf16[512,256]{1,0:T(8,128)(2,1)S(1)}, bf16[512,256]{1,0:T(8,128)(2,1)S(1)}, u32[]{:S(2)}, u32[]{:S(2)}) collective-permute-start(bf16[512,256]{1,0:T(8,128)(2,1)S(1)} %slice.109), channel_id=1, source_target_pairs={{0,1},{1,0},{2,3},{3,2},{4,5},{5,4},{6,7},{7,6},{8,9},{9,8},{10,11... | collective-permute-start | bytes 786440 | tf_op jit(solution)/shard_map/ppermute | solution.py:246
  104.9 35.4 %collective-permute-start.9 = (bf16[256,512]{1,0:T(8,128)(2,1)S(1)}, bf16[256,512]{1,0:T(8,128)(2,1)S(1)}, u32[]{:S(2)}, u32[]{:S(2)}) collective-permute-start(bf16[256,512]{1,0:T(8,128)(2,1)S(1)} %pad_maximum_fusion.2), channel_id=1, source_target_pairs={{0,16},{8,24},{16,0},{24,8},{1,17},{9,25},{17,1},{25,9},{2,18},{10... | collective-permute-start | bytes 786440 | tf_op jit(solution)/shard_map/ppermute | solution.py:243
  112.7 18.3 %collective-permute-start.11 = (bf16[512,256]{1,0:T(8,128)(2,1)S(1)}, bf16[512,256]{1,0:T(8,128)(2,1)S(1)}, u32[]{:S(2)}, u32[]{:S(2)}) collective-permute-start(bf16[512,256]{1,0:T(8,128)(2,1)S(1)} %slice.117), channel_id=1, source_target_pairs={{0,1},{1,0},{2,3},{3,2},{4,5},{5,4},{6,7},{7,6},{8,9},{9,8},{10,11... | collective-permute-start | bytes 786440 | tf_op jit(solution)/shard_map/ppermute | solution.py:246
  113.1 28.0 %collective-permute-start.14 = (bf16[256,512]{1,0:T(8,128)(2,1)S(1)}, bf16[256,512]{1,0:T(8,128)(2,1)S(1)}, u32[]{:S(2)}, u32[]{:S(2)}) collective-permute-start(bf16[256,512]{1,0:T(8,128)(2,1)S(1)} %pad_maximum_fusion.4), channel_id=1, source_target_pairs={{0,16},{8,24},{16,0},{24,8},{1,17},{9,25},{17,1},{25,9},{2,18},{10... | collective-permute-start | bytes 786440 | tf_op jit(solution)/shard_map/ppermute | solution.py:243
  129.4 9.3 %collective-permute-start.16 = (bf16[512,256]{1,0:T(8,128)(2,1)S(1)}, bf16[512,256]{1,0:T(8,128)(2,1)S(1)}, u32[]{:S(2)}, u32[]{:S(2)}) collective-permute-start(bf16[512,256]{1,0:T(8,128)(2,1)S(1)} %slice.125), channel_id=1, source_target_pairs={{0,1},{1,0},{2,3},{3,2},{4,5},{5,4},{6,7},{7,6},{8,9},{9,8},{10,11... | collective-permute-start | bytes 786440 | tf_op jit(solution)/shard_map/ppermute | solution.py:246
  131.0 10.5 %collective-permute-start.19 = (bf16[256,512]{1,0:T(8,128)(2,1)S(1)}, bf16[256,512]{1,0:T(8,128)(2,1)S(1)}, u32[]{:S(2)}, u32[]{:S(2)}) collective-permute-start(bf16[256,512]{1,0:T(8,128)(2,1)S(1)} %pad_maximum_fusion.6), channel_id=1, source_target_pairs={{0,16},{8,24},{16,0},{24,8},{1,17},{9,25},{17,1},{25,9},{2,18},{10... | collective-permute-start | bytes 786440 | tf_op jit(solution)/shard_map/ppermute | solution.py:243
  131.7 12.6 %collective-permute-start.21 = (bf16[512,256]{1,0:T(8,128)(2,1)S(1)}, bf16[512,256]{1,0:T(8,128)(2,1)S(1)}, u32[]{:S(2)}, u32[]{:S(2)}) collective-permute-start(bf16[512,256]{1,0:T(8,128)(2,1)S(1)} %slice.133), channel_id=1, source_target_pairs={{0,1},{1,0},{2,3},{3,2},{4,5},{5,4},{6,7},{7,6},{8,9},{9,8},{10,11... | collective-permute-start | bytes 786440 | tf_op jit(solution)/shard_map/ppermute | solution.py:246
  138.7 8.4 %collective-permute-start.5 = (bf16[256,256]{1,0:T(8,128)(2,1)S(1)}, bf16[256,256]{1,0:T(8,128)(2,1)S(1)}, u32[]{:S(2)}, u32[]{:S(2)}) collective-permute-start(bf16[256,256]{1,0:T(8,128)(2,1)S(1)} %slice.191), channel_id=1, source_target_pairs={{0,1},{1,0},{2,3},{3,2},{4,5},{5,4},{6,7},{7,6},{8,9},{9,8},{10,11... | collective-permute-start | bytes 393224 | tf_op jit(solution)/shard_map/ppermute | solution.py:246
  140.3 7.2 %collective-permute-start.7 = (bf16[256,256]{1,0:T(8,128)(2,1)S(1)}, bf16[256,256]{1,0:T(8,128)(2,1)S(1)}, u32[]{:S(2)}, u32[]{:S(2)}) collective-permute-start(bf16[256,256]{1,0:T(8,128)(2,1)S(1)} %slice.190), channel_id=1, source_target_pairs={{0,16},{8,24},{16,0},{24,8},{1,17},{9,25},{17,1},{25,9},{2,18},{10... | collective-permute-start | bytes 393224 | tf_op jit(solution)/shard_map/ppermute | solution.py:243
  141.0 8.9 %collective-permute-start.10 = (bf16[256,256]{1,0:T(8,128)(2,1)S(1)}, bf16[256,256]{1,0:T(8,128)(2,1)S(1)}, u32[]{:S(2)}, u32[]{:S(2)}) collective-permute-start(bf16[256,256]{1,0:T(8,128)(2,1)S(1)} %slice.189), channel_id=1, source_target_pairs={{0,1},{1,0},{2,3},{3,2},{4,5},{5,4},{6,7},{7,6},{8,9},{9,8},{10,11... | collective-permute-start | bytes 393224 | tf_op jit(solution)/shard_map/ppermute | solution.py:246
  141.5 9.5 %collective-permute-start.12 = (bf16[256,256]{1,0:T(8,128)(2,1)S(1)}, bf16[256,256]{1,0:T(8,128)(2,1)S(1)}, u32[]{:S(2)}, u32[]{:S(2)}) collective-permute-start(bf16[256,256]{1,0:T(8,128)(2,1)S(1)} %slice.188), channel_id=1, source_target_pairs={{0,16},{8,24},{16,0},{24,8},{1,17},{9,25},{17,1},{25,9},{2,18},{10... | collective-permute-start | bytes 393224 | tf_op jit(solution)/shard_map/ppermute | solution.py:243
  144.3 9.4 %collective-permute-start.15 = (bf16[256,256]{1,0:T(8,128)(2,1)S(1)}, bf16[256,256]{1,0:T(8,128)(2,1)S(1)}, u32[]{:S(2)}, u32[]{:S(2)}) collective-permute-start(bf16[256,256]{1,0:T(8,128)(2,1)S(1)} %slice.187), channel_id=1, source_target_pairs={{0,1},{1,0},{2,3},{3,2},{4,5},{5,4},{6,7},{7,6},{8,9},{9,8},{10,11... | collective-permute-start | bytes 393224 | tf_op jit(solution)/shard_map/ppermute | solution.py:246
  147.1 8.8 %collective-permute-start.17 = (bf16[256,256]{1,0:T(8,128)(2,1)S(1)}, bf16[256,256]{1,0:T(8,128)(2,1)S(1)}, u32[]{:S(2)}, u32[]{:S(2)}) collective-permute-start(bf16[256,256]{1,0:T(8,128)(2,1)S(1)} %slice.186), channel_id=1, source_target_pairs={{0,16},{8,24},{16,0},{24,8},{1,17},{9,25},{17,1},{25,9},{2,18},{10... | collective-permute-start | bytes 393224 | tf_op jit(solution)/shard_map/ppermute | solution.py:243
  147.5 8.6 %collective-permute-start.20 = (bf16[256,256]{1,0:T(8,128)(2,1)S(1)}, bf16[256,256]{1,0:T(8,128)(2,1)S(1)}, u32[]{:S(2)}, u32[]{:S(2)}) collective-permute-start(bf16[256,256]{1,0:T(8,128)(2,1)S(1)} %slice.185), channel_id=1, source_target_pairs={{0,1},{1,0},{2,3},{3,2},{4,5},{5,4},{6,7},{7,6},{8,9},{9,8},{10,11... | collective-permute-start | bytes 393224 | tf_op jit(solution)/shard_map/ppermute | solution.py:246
  150.0 6.2 %collective-permute-start.22 = (bf16[256,256]{1,0:T(8,128)(2,1)S(1)}, bf16[256,256]{1,0:T(8,128)(2,1)S(1)}, u32[]{:S(2)}, u32[]{:S(2)}) collective-permute-start(bf16[256,256]{1,0:T(8,128)(2,1)S(1)} %slice.184), channel_id=1, source_target_pairs={{0,16},{8,24},{16,0},{24,8},{1,17},{9,25},{17,1},{25,9},{2,18},{10... | collective-permute-start | bytes 393224 | tf_op jit(solution)/shard_map/ppermute | solution.py:243
  151.0 17.2 %collective-permute-start.8 = (bf16[512,256]{1,0:T(8,128)(2,1)S(1)}, bf16[512,256]{1,0:T(8,128)(2,1)S(1)}, u32[]{:S(2)}, u32[]{:S(2)}) collective-permute-start(bf16[512,256]{1,0:T(8,128)(2,1)S(1)} %pad_maximum_fusion.1), channel_id=1, source_target_pairs={{0,4},{1,5},{2,6},{3,7},{4,0},{5,1},{6,2},{7,3},{8,12},{9,13},{10,... | collective-permute-start | bytes 786440 | tf_op jit(solution)/shard_map/ppermute | solution.py:246
  153.7 14.4 %collective-permute-start.13 = (bf16[512,256]{1,0:T(8,128)(2,1)S(1)}, bf16[512,256]{1,0:T(8,128)(2,1)S(1)}, u32[]{:S(2)}, u32[]{:S(2)}) collective-permute-start(bf16[512,256]{1,0:T(8,128)(2,1)S(1)} %pad_maximum_fusion.3), channel_id=1, source_target_pairs={{0,6},{1,7},{2,4},{3,5},{4,2},{5,3},{6,0},{7,1},{8,14},{9,15},{10,... | collective-permute-start | bytes 786440 | tf_op jit(solution)/shard_map/ppermute | solution.py:246
  156.0 13.7 %collective-permute-start.18 = (bf16[512,256]{1,0:T(8,128)(2,1)S(1)}, bf16[512,256]{1,0:T(8,128)(2,1)S(1)}, u32[]{:S(2)}, u32[]{:S(2)}) collective-permute-start(bf16[512,256]{1,0:T(8,128)(2,1)S(1)} %pad_maximum_fusion.5), channel_id=1, source_target_pairs={{0,2},{1,3},{2,0},{3,1},{4,6},{5,7},{6,4},{7,5},{8,10},{9,11},{10,... | collective-permute-start | bytes 786440 | tf_op jit(solution)/shard_map/ppermute | solution.py:246

commit v2 on v0

v2 whole, which is shorter than its diff:
```python
import functools

import jax
import jax.numpy as jnp
from jax import lax
from jax.experimental import pallas as pl
from jax.experimental.pallas import tpu as pltpu
from jax.sharding import PartitionSpec as P

CAP = 8
CORES = 2
MIB = 1024 * 1024
SMEM = pl.BlockSpec(memory_space=pltpu.SMEM)
VMEM = pl.BlockSpec(memory_space=pltpu.VMEM)


def params(mib):
    return pltpu.CompilerParams(vmem_limit_bytes=mib * MIB)


def cheap():
    return pl.CostEstimate(flops=1, bytes_accessed=1, transcendentals=0)


ANY = pl.BlockSpec(memory_space=pl.ANY)


def contrib_kernel(
    owner_links, spot_ref, rows_ref, adj_ref, modes_ref, coup_ref, inv_ref, *refs
):
    outs, (part_ref, all_ref, count_ref) = refs[:-3], refs[-3:]
    s = pl.program_id(0)
    links, rows, block = coup_ref.shape[1:]

    @pl.when(s == 0)
    def _():
        for i in range(count_ref.shape[0]):
            count_ref[i] = 0

    live = lax.broadcasted_iota(jnp.int32, (rows, 1), 0) < rows_ref[s]
    modes = jnp.where(live, modes_ref[0], jnp.zeros((), modes_ref.dtype))
    inv = inv_ref[pl.ds(s, 1), :]
    wide = jnp.concatenate([coup_ref[0, a] for a in range(links)], axis=1)
    red = lax.dot_general(
        wide, modes, (((0,), (0,)), ((), ())), preferred_element_type=jnp.float32
    )
    weighted = (red * inv).astype(jnp.bfloat16)
    red_b = red.astype(jnp.bfloat16)
    for a in range(links):
        part = slice(a * block, (a + 1) * block)
        part_ref[a] = lax.dot_general(
            weighted[part], red_b[part], (((1,), (1,)), ((), ())),
            preferred_element_type=jnp.float32,
        ).astype(jnp.bfloat16)
    for a in range(links):
        target = adj_ref[s, a] // owner_links
        slot = count_ref[target]
        count_ref[target] = slot + 1
        all_ref[(target ^ spot_ref[0]) * CAP + slot] = part_ref[a]

    @pl.when(s == pl.num_programs(0) - 1)
    def _():
        for d, out in enumerate(outs):
            out[...] = all_ref[d * CAP:(d + 1) * CAP]


def make_contrib(spot, modes, coupling, inv_eig, sub_rows, adjacency, n_sub, owner_links):
    subs, rows, width = modes.shape
    links, block = coupling.shape[1], coupling.shape[3]
    out = jax.ShapeDtypeStruct((CAP, block, block), jnp.bfloat16)
    return pl.pallas_call(
        functools.partial(contrib_kernel, owner_links),
        grid=(subs,),
        in_specs=[
            SMEM, SMEM, SMEM,
            pl.BlockSpec((1, rows, width), lambda s: (s, 0, 0)),
            pl.BlockSpec((1, links, rows, block), lambda s: (s, 0, 0, 0)),
            pl.BlockSpec(inv_eig.shape, lambda s: (0, 0)),
        ],
        out_specs=[pl.BlockSpec(out.shape, lambda s: (0, 0, 0))] * n_sub,
        out_shape=[out] * n_sub,
        scratch_shapes=[
            pltpu.VMEM((links, block, block), jnp.bfloat16),
            pltpu.VMEM((n_sub * CAP, block, block), jnp.bfloat16),
            pltpu.SMEM((n_sub,), jnp.int32),
        ],
        compiler_params=params(60),
        cost_estimate=cheap(),
        name="contrib",
    )(spot, sub_rows, adjacency, modes, coupling, inv_eig)


def near_kernel(n_sub, base_ref, *rest):
    lists = rest[:n_sub]
    own_ref, pair_ref, total_ref, place_ref = rest[n_sub:]
    spare = base_ref.shape[0]
    total_ref[:spare] = base_ref[...]
    subs, links = lists[0].shape
    for i in range(n_sub * CAP):
        place_ref[i] = spare
    for d in range(n_sub):
        def body(link, slot, d=d):
            local = lists[d][link // links, link % links]

            @pl.when(local >= 0)
            def _():
                place_ref[d * CAP + slot] = local

            return slot + (local >= 0).astype(jnp.int32)

        lax.fori_loop(0, subs * links, body, jnp.int32(0))
    for d, group in enumerate((own_ref, pair_ref)):
        for i in range(CAP):
            total_ref[place_ref[d * CAP + i]] += group[i].astype(jnp.float32)


def make_near(base, lists, own, pair):
    blk_dev, block = base.shape[:2]
    n_sub = len(lists)
    return pl.pallas_call(
        functools.partial(near_kernel, n_sub),
        in_specs=[VMEM] + [SMEM] * n_sub + [VMEM] * 2,
        out_specs=[VMEM, SMEM],
        out_shape=[
            jax.ShapeDtypeStruct((blk_dev + 1, block, block), jnp.float32),
            jax.ShapeDtypeStruct((n_sub * CAP,), jnp.int32),
        ],
        compiler_params=params(12),
        cost_estimate=cheap(),
        name="near",
    )(base, *lists, own, pair)


def far_kernel(groups, place_ref, near_ref, *rest):
    mass_ref, total_ref = rest[-2:]
    total_ref[...] = near_ref[...]
    for d, group in enumerate(rest[:groups]):
        for i in range(CAP):
            total_ref[place_ref[(d + CORES) * CAP + i]] += group[i].astype(jnp.float32)
    mass_ref[...] = total_ref[:mass_ref.shape[0]].astype(jnp.bfloat16)


def make_far(place, near, groups, behind):
    count, block = near.shape[:2]
    return pl.pallas_call(
        functools.partial(far_kernel, len(groups)),
        in_specs=[SMEM, VMEM] + [VMEM] * len(groups) + [ANY] * len(behind),
        out_specs=VMEM,
        out_shape=jax.ShapeDtypeStruct((count - 1, block, block), jnp.bfloat16),
        scratch_shapes=[pltpu.VMEM(near.shape, jnp.float32)],
        compiler_params=params(12),
        cost_estimate=cheap(),
        name="far",
    )(place, near, *groups, *behind)


def turn_kernel(spot_ref, psi_ref, out_ref):
    groups, half, _ = out_ref.shape
    n_x = groups // 2
    x = pl.program_id(0)
    out_ref[jnp.where(x == 0, groups - 1, x - 1)] = psi_ref[:, :half].T
    out_ref[n_x - 1 + x] = psi_ref[:, half:].T


def turn(spot, psi, n_x, band):
    depth = psi.shape[0]
    shape = (2 * n_x, band // 2, depth)
    return pl.pallas_call(
        turn_kernel,
        grid_spec=pltpu.PrefetchScalarGridSpec(
            num_scalar_prefetch=1,
            grid=(n_x,),
            in_specs=[pl.BlockSpec((depth, band), lambda x, spot: (0, spot[0] ^ (x * CORES)))],
            out_specs=pl.BlockSpec(shape, lambda x, spot: (0, 0, 0)),
        ),
        out_shape=jax.ShapeDtypeStruct(shape, psi.dtype),
        compiler_params=params(16),
        cost_estimate=cheap(),
        name="turn",
    )(spot, psi)


def left_kernel(mass_ref, turned_ref, out_ref):
    block = mass_ref.shape[1]
    zero = jnp.zeros((block, block), jnp.bfloat16)
    groups, half, _ = turned_ref.shape
    for j in range(0, mass_ref.shape[0], 2):
        pair = jnp.concatenate(
            [
                jnp.concatenate([mass_ref[j], zero], axis=1),
                jnp.concatenate([zero, mass_ref[j + 1]], axis=1),
            ],
            axis=0,
        )
        cols = slice(j * block, (j + 2) * block)
        out_ref[:, cols] = jnp.dot(
            turned_ref[:, :, cols].reshape(groups * half, 2 * block), pair,
            preferred_element_type=jnp.float32,
        ).astype(jnp.bfloat16)


def make_left(mass, turned):
    groups, half, depth = turned.shape
    return pl.pallas_call(
        left_kernel,
        in_specs=[VMEM, VMEM],
        out_specs=VMEM,
        out_shape=jax.ShapeDtypeStruct((groups * half, depth), jnp.bfloat16),
        compiler_params=params(16),
        cost_estimate=cheap(),
        name="left",
    )(mass, turned)


def product_kernel(z, n_x, pairs, acc_in, go, keep, behind, spot_ref, *refs):
    lefts, psis, refs = refs[:pairs], refs[pairs:2 * pairs], refs[2 * pairs:]
    acc_x, acc_y = (refs[:n_x - 1], refs[n_x - 1]) if acc_in else (None, None)
    outs = refs[(n_x if acc_in else 0) + behind:]
    go_x, go_y = (outs[:n_x - 1], outs[n_x - 1]) if go else (None, None)
    keep_a, keep_b = outs[-2:] if keep else (None, None)
    rows = lefts[0].shape[0]
    half = rows // (2 * n_x)
    first, both = (n_x - 1) * half, (2 * n_x - 1) * half
    width = (go_y if go else keep_b).shape[1]
    for y in range(2):
        lo = 0 if go else (both if y else first)
        hi = rows if keep else (both if y else first)
        tile = spot_ref[1] ^ (2 * z + y)
        at = pl.ds(pl.multiple_of(tile * width, width), width)
        res = None
        for left, psi in zip(lefts, psis):
            term = jnp.dot(left[lo:hi], psi[:, at], preferred_element_type=jnp.float32)
            res = term if res is None else res + term
        here = slice(y * width, (y + 1) * width)
        if go:
            for d in range(n_x - 1):
                head = res[d * half:(d + 1) * half]
                if acc_in:
                    head += acc_x[d][:, here]
                go_x[d][:, here] = head.astype(go_x[d].dtype)
            if y:
                head = res[first:both]
                if acc_in:
                    head += acc_y[...]
                go_y[...] = head.astype(go_y.dtype)
        if keep:
            if not y:
                keep_b[...] = res[first - lo:both - lo]
            keep_a[:, here] = res[both - lo:]


def product(z, spot, lefts, psis, width, n_x, go=None, keep=False, accs=(), behind=()):
    rows = lefts[0].shape[0]
    half = rows // (2 * n_x)
    shapes = []
    if go is not None:
        shapes += [(half, 2 * width, go)] * (n_x - 1) + [(n_x * half, width, go)]
    if keep:
        shapes += [(half, 2 * width, jnp.float32), (n_x * half, width, jnp.float32)]
    return pl.pallas_call(
        functools.partial(
            product_kernel, z, n_x, len(lefts), bool(accs), go is not None, keep, len(behind)
        ),
        in_specs=[SMEM] + [VMEM] * (2 * len(lefts) + len(accs)) + [ANY] * len(behind),
        out_specs=[VMEM] * len(shapes),
        out_shape=[jax.ShapeDtypeStruct((r, c), t) for r, c, t in shapes],
        compiler_params=params(24),
        cost_estimate=cheap(),
        name="product",
    )(spot, *lefts, *psis, *accs, *behind)


def first_kernel(n_x, a_ref, b_ref, *refs):
    got_x, got_y, outs = refs[:n_x - 1], refs[n_x - 1], refs[n_x:]
    low, high, go_y, go_x = outs[0], outs[1], outs[2], outs[3:]
    half, width = low.shape
    total = a_ref[...]
    for v in got_x:
        total += v[...].astype(jnp.float32)
    low[...] = total[:, :width]
    go_y[...] = total[:, width:].astype(jnp.bfloat16)
    for d in range(n_x):
        rows = slice(d * half, (d + 1) * half)
        total = b_ref[rows] + got_y[rows].astype(jnp.float32)
        if d == 0:
            high[...] = total
        else:
            go_x[d - 1][...] = total.astype(jnp.bfloat16)


def add_first(keep_a, keep_b, got_x, got_y):
    half, width = keep_a.shape[0], keep_b.shape[1]
    n_x = len(got_x) + 1
    types = [jnp.float32] * 2 + [jnp.bfloat16] * n_x
    low, high, go_y, *go_x = pl.pallas_call(
        functools.partial(first_kernel, n_x),
        in_specs=[VMEM] * (n_x + 2),
        out_specs=[VMEM] * len(types),
        out_shape=[jax.ShapeDtypeStruct((half, width), t) for t in types],
        compiler_params=params(12),
        cost_estimate=cheap(),
        name="add_first",
    )(keep_a, keep_b, *got_x, got_y)
    return low, high, go_y, go_x


def second_kernel(n_x, low_ref, high_ref, got_y, *refs):
    got_x, tails, out = refs[:n_x - 1], refs[n_x - 1:-1], refs[-1]
    half = low_ref.shape[0]
    low = low_ref[...] + got_y[...].astype(jnp.float32)
    high = high_ref[...]
    for v in got_x:
        high += v[...].astype(jnp.float32)
    for v in tails:
        low += v[:half].astype(jnp.float32)
        high += v[half:].astype(jnp.float32)
    out[:half] = low.astype(out.dtype)
    out[half:] = high.astype(out.dtype)


def add_second(low, high, got_y, got_x, dtype, tails=()):
    half, width = low.shape
    return pl.pallas_call(
        functools.partial(second_kernel, len(got_x) + 1),
        in_specs=[VMEM] * (3 + len(got_x) + len(tails)),
        out_specs=VMEM,
        out_shape=jax.ShapeDtypeStruct((2 * half, width), dtype),
        compiler_params=params(12),
        cost_estimate=cheap(),
        name="add_second",
    )(low, high, got_y, *got_x, *tails)


def on_device(modes, coupling, inv_eig, sub_rows, adjacency, base_mass, iface_modes):
    n_sub = lax.axis_size("sub")
    n_tile = lax.axis_size("tile")
    n_x = n_sub // CORES
    n_z = n_tile // 2
    blk_dev = base_mass.shape[0]
    owner_links = blk_dev * n_tile
    width = iface_modes.shape[1]
    band, tile = width // n_sub, width // n_tile
    sub, at = lax.axis_index("sub"), lax.axis_index("tile")
    spot = jnp.stack([sub, at]).astype(jnp.int32)

    def swap_sub(v, d):
        return lax.ppermute(v, "sub", [(i, i ^ d) for i in range(n_sub)])

    def swap_x(v, d):
        return swap_sub(v, d * CORES)

    def swap_tile(v, d):
        return lax.ppermute(v, "tile", [(i, i ^ d) for i in range(n_tile)])

    owner, local = adjacency // owner_links, adjacency % blk_dev
    lists = [jnp.where(owner == (sub ^ d), local, -1) for d in range(n_sub)]
    lists = [swap_sub(v, d) if d else v for d, v in enumerate(lists)]
    other = swap_sub(iface_modes, 1)
    sent = make_contrib(
        spot, modes, coupling, inv_eig, sub_rows, adjacency, n_sub, owner_links
    )
    far = [swap_sub(sent[d], d) for d in range(CORES, n_sub)]
    near, place = make_near(base_mass, lists, sent[0], swap_sub(sent[1], 1))
    own_t = turn(spot, iface_modes, n_x, band)
    other_t = turn(spot, other, n_x, band)
    mass = make_far(place, near, far, [own_t, other_t])
    mass_other = swap_sub(mass, 1)
    left = make_left(mass, own_t)

    chunks = sorted(range(1, n_z), key=lambda z: (-min(z, 2), z)) + [0]
    head = product(chunks[0], spot, [left], [iface_modes], tile, n_x, go=jnp.float32)
    left_other = make_left(mass_other, other_t)
    lefts, psis = [left, left_other], [iface_modes, other]

    def send_first(go):
        *go_x, go_y = go
        return [swap_x(v, d + 1) for d, v in enumerate(go_x)], swap_tile(go_y, 1)

    def send_second(low, high, go_y, go_x):
        return low, high, swap_tile(go_y, 1), [swap_x(v, d + 1) for d, v in enumerate(go_x)]

    keep, first, second, third = {}, {}, {}, []
    last = len(chunks) - 1
    for i in range(last + 3):
        if i == 0:
            go = product(
                chunks[0], spot, [left_other], [other], tile, n_x, go=jnp.bfloat16, accs=head
            )
            first[0] = send_first(go)
            keep[0] = product(chunks[0], spot, lefts, psis, tile, n_x, keep=True, behind=go[:1])
        elif i <= last:
            behind = [keep[0][0]] if i == 1 else [second[i - 2][0]]
            *go, keep_a, keep_b = product(
                chunks[i], spot, lefts, psis, tile, n_x, go=jnp.bfloat16, keep=True,
                behind=behind,
            )
            keep[i] = keep_a, keep_b
            first[i] = send_first(go)
        if 0 < i <= last + 1:
            second[i - 1] = send_second(*add_first(*keep[i - 1], *first[i - 1]))
        if 1 < i < last + 2:
            mine = add_second(*second[i - 2], jnp.bfloat16)
            third.append(swap_tile(mine, 2 * chunks[i - 2]))
    return add_second(*second[last], jnp.float32, third)


def solution(mesh):
    placed = (
        P(("sub", "tile"), None, None),
        P(("sub", "tile"), None, None, None),
        P(("sub", "tile"), None),
        P(("sub", "tile")),
        P(("sub", "tile"), None),
        P(("sub", "tile"), None, None),
        P(("sub", "tile"), None),
    )
    return jax.shard_map(
        on_device, mesh=mesh, in_specs=placed, out_specs=P("sub", "tile"), check_vma=False
    )
```

time: 244 us -> 120 us (0.49)
  waiting for transfers between devices: 175 us -> 24 us
  Pallas kernels: 0 us -> 58.5 us
  matrix products: 38.5 us -> 0 us
  starting transfers between devices: 7.99 us -> 31 us
  between operations: 13.5 us -> 0.28 us
  other arithmetic: 5.19 us -> 0.67 us
    reduce_scatter x2 -> x0, waiting for transfers between devices: 161 us -> none  [the longest x1 88 us: on_device(): lax.psum_scatter(row_band, 'tile', scatter_dimension=1, tiled=True)]
    pallas_call x0 -> x21, Pallas kernels: none -> 58.5 us  [the longest x6 36.2 us: product(): pl.pallas_call(functools.partial(product_kernel, z, n_x, len(lefts), bool...]
    dot_general x6 -> x0, matrix products: 38.5 us -> none  [the longest x1 20.6 us: on_device(): lax.dot_general(iface_modes, image, (((0,), (0,)), ((), ())), preferred_e...]
    ppermute x0 -> x27, starting transfers between devices: none -> 31 us  [the longest x16 16.5 us: swap_sub(): return lax.ppermute(v, 'sub', [(i, i ^ d) for i in range(n_sub)])]
    ppermute x0 -> x27, waiting for transfers between devices: none -> 24 us  [the longest x16 12.9 us: swap_sub(): return lax.ppermute(v, 'sub', [(i, i ^ d) for i in range(n_sub)])]
    all_to_all x2 -> x0, waiting for transfers between devices: 14.1 us -> none  [the longest x1 14.1 us: on_device(): lax.all_to_all(outgoing, 'sub', split_axis=0, concat_axis=0, tiled=True)]
    all_to_all x2 -> x0, starting transfers between devices: 7.72 us -> none  [the longest x1 4.21 us: on_device(): lax.all_to_all(out_ids, 'sub', split_axis=0, concat_axis=0, tiled=True)]
    convert_element_type x2 -> x0, other arithmetic: 4.85 us -> none  [the longest x1 4.12 us: on_device(): row_band = lax.psum_scatter(lax.dot_general(iface_modes, image, (((0,), (...]
  transfers between devices with their start and end apart: 4 -> 27, of which waited for: 3 -> 6; matrix products, arithmetic and copies ran while one was open for 5% -> 1% of each run, Pallas kernels for 0% -> 43%
where the time goes in v2:
time: 120 us; the launch traced here: 119 us
  Pallas kernels  58.5 us (49%)
  starting transfers between devices  31 us (26%)
  waiting for transfers between devices  24 us (20%)
  local copies, waits for them, and re-layouts  4.21 us (4%)
    pallas_call x6, Pallas kernels, product(): pl.pallas_call(functools.partial(product_kernel, z, n_x, len(lefts), bool...  36.2 us
    ppermute x16, starting transfers between devices, swap_sub(): return lax.ppermute(v, 'sub', [(i, i ^ d) for i in range(n_sub)])  16.5 us
    ppermute x11, starting transfers between devices, swap_tile(): return lax.ppermute(v, 'tile', [(i, i ^ d) for i in range(n_tile)])  14.5 us
    ppermute x16, waiting for transfers between devices, swap_sub(): return lax.ppermute(v, 'sub', [(i, i ^ d) for i in range(n_sub)])  12.9 us
    ppermute x11, waiting for transfers between devices, swap_tile(): return lax.ppermute(v, 'tile', [(i, i ^ d) for i in range(n_tile)])  11.1 us
    pallas_call x1, Pallas kernels, make_contrib(): pl.pallas_call(functools.partial(contrib_kernel, owner_links), grid=(subs...  8.47 us
    pallas_call x2, Pallas kernels, turn(): pl.pallas_call(turn_kernel, grid_spec=pltpu.PrefetchScalarGridSpec(num_sc...  5.81 us
    unnamed x14, local copies, waits for them, and re-layouts  4.21 us
  transfers between devices with their start and end apart: 27, of which 6 were waited for; matrix products, arithmetic and copies ran while one was open for 1% of the time, Pallas kernels for 43%

profile of v2, /device:TPU:0, one launch (start us, length us, event | category | flops | bytes accessed | tf_op | source)
XLA Modules:
  0.0 118.8 jit_solution(5669322932220132644)
XLA Ops:
  0.0 0.5 collective-permute-start.6
  0.5 0.7 pad_add_fusion.spot_ref
  1.1 8.5 %contrib.1 = (bf16[8,128,128]{2,1,0:T(8,128)(2,1)}, bf16[8,128,128]{2,1,0:T(8,128)(2,1)}, bf16[8,128,128]{2,1,0:T(8,128)(2,1)}, bf16[8,128,128]{2,1,0:T(8,128)(2,1)}) custom-call(s32[2]{0:T(128)} %pad_add_fusion.spot_ref, s32[4]{0:T(128)} %rows_ref.1, s32[4,8]{1,0:T(4,128)} %adj_ref.1, bf16[4,768,512]{2,1,0:T(8,128)(2,1)} %modes_ref.1, ...), custom_call_target="tpu_custom_call" | custom-call | flops 1 | bytes 1 | tf_op jit(solution)/shard_map/contrib/pallas_call | solution.py:71
  9.6 2.9 %collective-permute-start.4 = (bf16[8,128,128]{2,1,0:T(8,128)(2,1)}, bf16[8,128,128]{2,1,0:T(8,128)(2,1)S(1)}, u32[]{:S(2)}, u32[]{:S(2)}) collective-permute-start(bf16[8,128,128]{2,1,0:T(8,128)(2,1)} %get-tuple-element.49), channel_id=1, source_target_pairs={{0,16},{8,24},{16,0},{24,8},{1,17},{9,25},{17,1},{25,9},{2,18},{10... | collective-permute-start | bytes 786440 | tf_op jit(solution)/shard_map/ppermute | solution.py:347
  12.6 1.8 %collective-permute-start.2 = (s32[4,8]{1,0:T(4,128)S(1)}, s32[4,8]{1,0:T(4,128)S(1)}, u32[]{:S(2)}, u32[]{:S(2)}) collective-permute-start(s32[4,8]{1,0:T(4,128)S(1)} %get-tuple-element.85), channel_id=1, source_target_pairs={{0,24},{8,16},{16,8},{24,0},{1,25},{9,17},{17,9},{25,1},{2,26},{10... | collective-permute-start | bytes 392 | tf_op jit(solution)/shard_map/ppermute | solution.py:347
  14.4 10.0 %collective-permute-done.2.rest_3_ = s32[4,8]{1,0:T(4,128)S(1)} collective-permute-done((s32[4,8]{1,0:T(4,128)S(1)}, s32[4,8]{1,0:T(4,128)S(1)}, u32[]{:S(2)}, u32[]{:S(2)}) %collective-permute-start.2) | collective-permute-done | bytes 160 | tf_op jit(solution)/shard_map/ppermute | solution.py:347
  24.4 1.4 %collective-permute-start.1 = (s32[4,8]{1,0:T(4,128)S(1)}, s32[4,8]{1,0:T(4,128)S(1)}, u32[]{:S(2)}, u32[]{:S(2)}) collective-permute-start(s32[4,8]{1,0:T(4,128)S(1)} %get-tuple-element.86), channel_id=1, source_target_pairs={{0,16},{8,24},{16,0},{24,8},{1,17},{9,25},{17,1},{25,9},{2,18},{10... | collective-permute-start | bytes 392 | tf_op jit(solution)/shard_map/ppermute | solution.py:347
  25.8 2.2 %collective-permute-done.1.rest_2_ = s32[4,8]{1,0:T(4,128)S(1)} collective-permute-done((s32[4,8]{1,0:T(4,128)S(1)}, s32[4,8]{1,0:T(4,128)S(1)}, u32[]{:S(2)}, u32[]{:S(2)}) %collective-permute-start.1) | collective-permute-done | bytes 160 | tf_op jit(solution)/shard_map/ppermute | solution.py:347
  28.0 3.4 %copy-done = bf16[2048,2048]{1,0:T(8,128)(2,1)S(1)} copy-done((bf16[2048,2048]{1,0:T(8,128)(2,1)S(1)}, bf16[2048,2048]{1,0:T(8,128)(2,1)}, u32[]{:S(2)}) %copy-start) | copy-done | bytes 8388632
  31.4 2.2 %turn.2.rest_2_.turned_ref = bf16[4,256,2048]{2,1,0:T(8,128)(2,1)S(1)} custom-call(s32[2]{0:T(128)S(1)} %copy-done.3, bf16[2048,2048]{1,0:T(8,128)(2,1)S(1)} %copy-done), custom_call_target="tpu_custom_call" | custom-call | flops 1 | bytes 1 | tf_op jit(solution)/shard_map/turn/pallas_call | solution.py:168
  33.7 3.2 %near.1 = (f32[17,128,128]{2,1,0:T(8,128)S(1)}, s32[32]{0:T(128)S(1)}) custom-call(f32[16,128,128]{2,1,0:T(8,128)S(1)} %copy-done.1, s32[4,8]{1,0:T(4,128)S(1)} %get-tuple-element.88.rest_0_, s32[4,8]{1,0:T(4,128)S(1)} %collective-permute-done.rest_1_, s32[4,8]{1,0:T(4,128)S(1)} %collective-permute-done.1.rest_2_, ...), custom_call_target="tpu_custom_call" | custom-call | flops 1 | bytes 1 | tf_op jit(solution)/shard_map/near/pallas_call | solution.py:120
  36.9 3.6 %turn.3.rest_3_.turned_ref = bf16[4,256,2048]{2,1,0:T(8,128)(2,1)S(1)} custom-call(s32[2]{0:T(128)S(1)} %copy-done.3, bf16[2048,2048]{1,0:T(8,128)(2,1)} %collective-permute-done.6.psi_ref.refs_1_.refs_3_), custom_call_target="tpu_custom_call" | custom-call | flops 1 | bytes 1 | tf_op jit(solution)/shard_map/turn/pallas_call | solution.py:168
  40.6 0.8 far.1.mass_ref
  41.4 0.6 collective-permute-start.7
  42.0 1.3 %left.2.refs_0_ = bf16[1024,2048]{1,0:T(8,128)(2,1)S(1)} custom-call(bf16[16,128,128]{2,1,0:T(8,128)(2,1)S(1)} %far.1.mass_ref, bf16[4,256,2048]{2,1,0:T(8,128)(2,1)S(1)} %turn.2.rest_2_.turned_ref), custom_call_target="tpu_custom_call" | custom-call | flops 1 | bytes 1 | tf_op jit(solution)/shard_map/left/pallas_call | solution.py:204
  43.2 0.8 slice-done.1
  44.0 1.8 %product.6 = (f32[256,512]{1,0:T(8,128)S(1)}, f32[512,256]{1,0:T(8,128)S(1)}) custom-call(s32[2]{0:T(128)S(1)} %copy-done.3, bf16[1024,2048]{1,0:T(8,128)(2,1)S(1)} %left.2.refs_0_, bf16[2048,2048]{1,0:T(8,128)(2,1)S(1)} %bitcast.3), custom_call_target="tpu_custom_call" | custom-call | flops 1 | bytes 1 | tf_op jit(solution)/shard_map/product/pallas_call | solution.py:260
  45.9 1.3 %left.3.refs_0_.refs_1_ = bf16[1024,2048]{1,0:T(8,128)(2,1)S(1)} custom-call(bf16[16,128,128]{2,1,0:T(8,128)(2,1)S(1)} %collective-permute-done.7.mass_ref, bf16[4,256,2048]{2,1,0:T(8,128)(2,1)S(1)} %turn.3.rest_3_.turned_ref), custom_call_target="tpu_custom_call" | custom-call | flops 1 | bytes 1 | tf_op jit(solution)/shard_map/left/pallas_call | solution.py:204
  47.1 4.7 %product.7 = (bf16[256,512]{1,0:T(8,128)(2,1)S(1)}, bf16[512,256]{1,0:T(8,128)(2,1)S(1)}) custom-call(s32[2]{0:T(128)S(1)} %copy-done.3, bf16[1024,2048]{1,0:T(8,128)(2,1)S(1)} %left.3.refs_0_.refs_1_, bf16[2048,2048]{1,0:T(8,128)(2,1)} %collective-permute-done.6.psi_ref.refs_1_.refs_3_, f32[256,512]{1,0:T(8,128)S(1)} %get-tuple-element.51.refs_2_, ...), custom_call_target="tpu_custom_call" | custom-call | flops 1 | bytes 1 | tf_op jit(solution)/shard_map/product/pallas_call | solution.py:260
  51.8 1.5 %collective-permute-start.15 = (bf16[512,256]{1,0:T(8,128)(2,1)S(1)}, bf16[512,256]{1,0:T(8,128)(2,1)S(1)}, u32[]{:S(2)}, u32[]{:S(2)}) collective-permute-start(bf16[512,256]{1,0:T(8,128)(2,1)S(1)} %get-tuple-element.69), channel_id=1, source_target_pairs={{0,1},{1,0},{2,3},{3,2},{4,5},{5,4},{6,7},{7,6},{8,9},{9,8},{10,11... | collective-permute-start | bytes 786440 | tf_op jit(solution)/shard_map/ppermute | solution.py:353
  53.3 1.5 %collective-permute-start.14 = (bf16[256,512]{1,0:T(8,128)(2,1)S(1)}, bf16[256,512]{1,0:T(8,128)(2,1)S(1)}, u32[]{:S(2)}, u32[]{:S(2)}) collective-permute-start(bf16[256,512]{1,0:T(8,128)(2,1)S(1)} %get-tuple-element.53.refs_4_), channel_id=1, source_target_pairs={{0,16},{8,24},{16,0},{24,8},{1,17},{9,25},{17,1},{25,9},{2,18},{10... | collective-permute-start | bytes 786440 | tf_op jit(solution)/shard_map/ppermute | solution.py:347
  54.8 5.8 %product.8 = (f32[256,512]{1,0:T(8,128)S(1)}, f32[512,256]{1,0:T(8,128)S(1)}) custom-call(s32[2]{0:T(128)S(1)} %copy-done.3, bf16[1024,2048]{1,0:T(8,128)(2,1)S(1)} %left.2.refs_0_, bf16[1024,2048]{1,0:T(8,128)(2,1)S(1)} %left.3.refs_0_.refs_1_, bf16[2048,2048]{1,0:T(8,128)(2,1)S(1)} %bitcast.3, ...), custom_call_target="tpu_custom_call" | custom-call | flops 1 | bytes 1 | tf_op jit(solution)/shard_map/product/pallas_call | solution.py:260
  60.6 7.9 %product.9 = (bf16[256,512]{1,0:T(8,128)(2,1)S(1)}, bf16[512,256]{1,0:T(8,128)(2,1)S(1)}, f32[256,512]{1,0:T(8,128)S(1)}, f32[512,256]{1,0:T(8,128)S(1)}) custom-call(s32[2]{0:T(128)S(1)} %copy-done.3, bf16[1024,2048]{1,0:T(8,128)(2,1)S(1)} %left.2.refs_0_, bf16[1024,2048]{1,0:T(8,128)(2,1)S(1)} %left.3.refs_0_.refs_1_, bf16[2048,2048]{1,0:T(8,128)(2,1)S(1)} %bitcast.3, ...), custom_call_target="tpu_custom_call" | custom-call | flops 1 | bytes 1 | tf_op jit(solution)/shard_map/product/pallas_call | solution.py:260
  68.5 0.6 collective-permute-start.8
  69.1 0.6 collective-permute-start.9
  69.7 0.1 add_first.6
  69.8 8.1 %product.11 = (bf16[256,512]{1,0:T(8,128)(2,1)S(1)}, bf16[512,256]{1,0:T(8,128)(2,1)S(1)}, f32[256,512]{1,0:T(8,128)S(1)}, f32[512,256]{1,0:T(8,128)S(1)}) custom-call(s32[2]{0:T(128)S(1)} %copy-done.3, bf16[1024,2048]{1,0:T(8,128)(2,1)S(1)} %left.2.refs_0_, bf16[1024,2048]{1,0:T(8,128)(2,1)S(1)} %left.3.refs_0_.refs_1_, bf16[2048,2048]{1,0:T(8,128)(2,1)S(1)} %bitcast.3, ...), custom_call_target="tpu_custom_call" | custom-call | flops 1 | bytes 1 | tf_op jit(solution)/shard_map/product/pallas_call | solution.py:260
  78.0 1.5 %collective-permute-start.22 = (bf16[256,512]{1,0:T(8,128)(2,1)S(1)}, bf16[256,512]{1,0:T(8,128)(2,1)S(1)}, u32[]{:S(2)}, u32[]{:S(2)}) collective-permute-start(bf16[256,512]{1,0:T(8,128)(2,1)S(1)} %get-tuple-element.79), channel_id=1, source_target_pairs={{0,16},{8,24},{16,0},{24,8},{1,17},{9,25},{17,1},{25,9},{2,18},{10... | collective-permute-start | bytes 786440 | tf_op jit(solution)/shard_map/ppermute | solution.py:347
  79.4 1.5 %collective-permute-start.23 = (bf16[512,256]{1,0:T(8,128)(2,1)S(1)}, bf16[512,256]{1,0:T(8,128)(2,1)S(1)}, u32[]{:S(2)}, u32[]{:S(2)}) collective-permute-start(bf16[512,256]{1,0:T(8,128)(2,1)S(1)} %get-tuple-element.80), channel_id=1, source_target_pairs={{0,1},{1,0},{2,3},{3,2},{4,5},{5,4},{6,7},{7,6},{8,9},{9,8},{10,11... | collective-permute-start | bytes 786440 | tf_op jit(solution)/shard_map/ppermute | solution.py:353
  80.9 0.5 collective-permute-start.16
  81.4 0.6 collective-permute-start.17
  82.2 1.5 %collective-permute-start.19 = (bf16[256,256]{1,0:T(8,128)(2,1)S(1)}, bf16[256,256]{1,0:T(8,128)(2,1)S(1)}, u32[]{:S(2)}, u32[]{:S(2)}) collective-permute-start(bf16[256,256]{1,0:T(8,128)(2,1)S(1)} %get-tuple-element.75), channel_id=1, source_target_pairs={{0,1},{1,0},{2,3},{3,2},{4,5},{5,4},{6,7},{7,6},{8,9},{9,8},{10,11... | collective-permute-start | bytes 393224 | tf_op jit(solution)/shard_map/ppermute | solution.py:353
  83.7 7.9 %product.10 = (bf16[256,512]{1,0:T(8,128)(2,1)S(1)}, bf16[512,256]{1,0:T(8,128)(2,1)S(1)}, f32[256,512]{1,0:T(8,128)S(1)}, f32[512,256]{1,0:T(8,128)S(1)}) custom-call(s32[2]{0:T(128)S(1)} %copy-done.3, bf16[1024,2048]{1,0:T(8,128)(2,1)S(1)} %left.2.refs_0_, bf16[1024,2048]{1,0:T(8,128)(2,1)S(1)} %left.3.refs_0_.refs_1_, bf16[2048,2048]{1,0:T(8,128)(2,1)S(1)} %bitcast.3, ...), custom_call_target="tpu_custom_call" | custom-call | flops 1 | bytes 1 | tf_op jit(solution)/shard_map/product/pallas_call | solution.py:260
  91.6 1.6 %collective-permute-start.20 = (bf16[256,256]{1,0:T(8,128)(2,1)S(1)}, bf16[256,256]{1,0:T(8,128)(2,1)S(1)}, u32[]{:S(2)}, u32[]{:S(2)}) collective-permute-start(bf16[256,256]{1,0:T(8,128)(2,1)S(1)} %get-tuple-element.76), channel_id=1, source_target_pairs={{0,16},{8,24},{16,0},{24,8},{1,17},{9,25},{17,1},{25,9},{2,18},{10... | collective-permute-start | bytes 393224 | tf_op jit(solution)/shard_map/ppermute | solution.py:347
  93.1 0.5 collective-permute-start.10
  93.8 0.7 collective-permute-start.11
  94.4 1.4 %collective-permute-start.24 = (bf16[256,256]{1,0:T(8,128)(2,1)S(1)}, bf16[256,256]{1,0:T(8,128)(2,1)S(1)}, u32[]{:S(2)}, u32[]{:S(2)}) collective-permute-start(bf16[256,256]{1,0:T(8,128)(2,1)S(1)} %get-tuple-element.83), channel_id=1, source_target_pairs={{0,1},{1,0},{2,3},{3,2},{4,5},{5,4},{6,7},{7,6},{8,9},{9,8},{10,11... | collective-permute-start | bytes 393224 | tf_op jit(solution)/shard_map/ppermute | solution.py:353
  95.9 1.5 %collective-permute-start.25 = (bf16[256,256]{1,0:T(8,128)(2,1)S(1)}, bf16[256,256]{1,0:T(8,128)(2,1)S(1)}, u32[]{:S(2)}, u32[]{:S(2)}) collective-permute-start(bf16[256,256]{1,0:T(8,128)(2,1)S(1)} %get-tuple-element.84), channel_id=1, source_target_pairs={{0,16},{8,24},{16,0},{24,8},{1,17},{9,25},{17,1},{25,9},{2,18},{10... | collective-permute-start | bytes 393224 | tf_op jit(solution)/shard_map/ppermute | solution.py:347
  97.4 0.7 collective-permute-done.20.refs_0_
  98.1 2.6 %collective-permute-start.18 = (bf16[512,256]{1,0:T(8,128)(2,1)S(1)}, bf16[512,256]{1,0:T(8,128)(2,1)S(1)}, u32[]{:S(2)}, u32[]{:S(2)}) collective-permute-start(bf16[512,256]{1,0:T(8,128)(2,1)S(1)} %add_second.4), channel_id=1, source_target_pairs={{0,4},{1,5},{2,6},{3,7},{4,0},{5,1},{6,2},{7,3},{8,12},{9,13},{10,... | collective-permute-start | bytes 786440 | tf_op jit(solution)/shard_map/ppermute | solution.py:353
  100.7 1.6 %collective-permute-done.24.got_y = bf16[256,256]{1,0:T(8,128)(2,1)S(1)} collective-permute-done((bf16[256,256]{1,0:T(8,128)(2,1)S(1)}, bf16[256,256]{1,0:T(8,128)(2,1)S(1)}, u32[]{:S(2)}, u32[]{:S(2)}) %collective-permute-start.24) | collective-permute-done | bytes 131104 | tf_op jit(solution)/shard_map/ppermute | solution.py:353
  102.3 3.6 %collective-permute-start.21 = (bf16[512,256]{1,0:T(8,128)(2,1)S(1)}, bf16[512,256]{1,0:T(8,128)(2,1)S(1)}, u32[]{:S(2)}, u32[]{:S(2)}) collective-permute-start(bf16[512,256]{1,0:T(8,128)(2,1)S(1)} %add_second.5), channel_id=1, source_target_pairs={{0,6},{1,7},{2,4},{3,5},{4,2},{5,3},{6,0},{7,1},{8,14},{9,15},{10,... | collective-permute-start | bytes 786440 | tf_op jit(solution)/shard_map/ppermute | solution.py:353
  106.0 0.1 add_first.5
  106.1 0.6 collective-permute-start.12
  106.7 1.5 %collective-permute-start.13 = (bf16[256,256]{1,0:T(8,128)(2,1)S(1)}, bf16[256,256]{1,0:T(8,128)(2,1)S(1)}, u32[]{:S(2)}, u32[]{:S(2)}) collective-permute-start(bf16[256,256]{1,0:T(8,128)(2,1)S(1)} %get-tuple-element.67), channel_id=1, source_target_pairs={{0,16},{8,24},{16,0},{24,8},{1,17},{9,25},{17,1},{25,9},{2,18},{10... | collective-permute-start | bytes 393224 | tf_op jit(solution)/shard_map/ppermute | solution.py:347
  108.2 8.4 %collective-permute-done.18.refs_1_ = bf16[512,256]{1,0:T(8,128)(2,1)S(1)} collective-permute-done((bf16[512,256]{1,0:T(8,128)(2,1)S(1)}, bf16[512,256]{1,0:T(8,128)(2,1)S(1)}, u32[]{:S(2)}, u32[]{:S(2)}) %collective-permute-start.18) | collective-permute-done | bytes 262176 | tf_op jit(solution)/shard_map/ppermute | solution.py:353
  116.6 1.2 collective-permute-done.26.refs_3_
  117.8 1.0 add_second.7
  (44 shorter events, 0.6 us)
Async XLA Ops:
  0.0 36.9 %collective-permute-start.6 = (bf16[2048,2048]{1,0:T(8,128)(2,1)}, bf16[2048,2048]{1,0:T(8,128)(2,1)}, u32[]{:S(2)}, u32[]{:S(2)}) collective-permute-start(bf16[2048,2048]{1,0:T(8,128)(2,1)} %refs_2_.7), channel_id=1, source_target_pairs={{0,8},{8,0},{16,24},{24,16},{1,9},{9,1},{17,25},{25,17},{2,10},{10... | collective-permute-start | bytes 25165832 | tf_op jit(solution)/shard_map/ppermute | solution.py:347
  1.1 11.5 %copy-start.4 = (s32[4,8]{1,0:T(4,128)S(1)}, s32[4,8]{1,0:T(4,128)}, u32[]{:S(2)}) copy-start(s32[4,8]{1,0:T(4,128)} %adj_ref.1) | copy-start | bytes 388
  1.1 26.9 %copy-start.3 = (s32[2]{0:T(128)S(1)}, s32[2]{0:T(128)}, u32[]{:S(2)}) copy-start(s32[2]{0:T(128)} %pad_add_fusion.spot_ref) | copy-start | bytes 28
  9.6 24.0 %collective-permute-start.3 = (bf16[8,128,128]{2,1,0:T(8,128)(2,1)}, bf16[8,128,128]{2,1,0:T(8,128)(2,1)S(1)}, u32[]{:S(2)}, u32[]{:S(2)}) collective-permute-start(bf16[8,128,128]{2,1,0:T(8,128)(2,1)} %get-tuple-element.46), channel_id=1, source_target_pairs={{0,8},{8,0},{16,24},{24,16},{1,9},{9,1},{17,25},{25,17},{2,10},{10... | collective-permute-start | bytes 786440 | tf_op jit(solution)/shard_map/ppermute | solution.py:347
  9.6 30.9 %collective-permute-start.4 = (bf16[8,128,128]{2,1,0:T(8,128)(2,1)}, bf16[8,128,128]{2,1,0:T(8,128)(2,1)S(1)}, u32[]{:S(2)}, u32[]{:S(2)}) collective-permute-start(bf16[8,128,128]{2,1,0:T(8,128)(2,1)} %get-tuple-element.49), channel_id=1, source_target_pairs={{0,16},{8,24},{16,0},{24,8},{1,17},{9,25},{17,1},{25,9},{2,18},{10... | collective-permute-start | bytes 786440 | tf_op jit(solution)/shard_map/ppermute | solution.py:347
  12.6 28.0 %collective-permute-start.5 = (bf16[8,128,128]{2,1,0:T(8,128)(2,1)}, bf16[8,128,128]{2,1,0:T(8,128)(2,1)S(1)}, u32[]{:S(2)}, u32[]{:S(2)}) collective-permute-start(bf16[8,128,128]{2,1,0:T(8,128)(2,1)} %get-tuple-element.50), channel_id=1, source_target_pairs={{0,24},{8,16},{16,8},{24,0},{1,25},{9,17},{17,9},{25,1},{2,26},{10... | collective-permute-start | bytes 786440 | tf_op jit(solution)/shard_map/ppermute | solution.py:347
  12.6 11.8 %collective-permute-start.2 = (s32[4,8]{1,0:T(4,128)S(1)}, s32[4,8]{1,0:T(4,128)S(1)}, u32[]{:S(2)}, u32[]{:S(2)}) collective-permute-start(s32[4,8]{1,0:T(4,128)S(1)} %get-tuple-element.85), channel_id=1, source_target_pairs={{0,24},{8,16},{16,8},{24,0},{1,25},{9,17},{17,9},{25,1},{2,26},{10... | collective-permute-start | bytes 392 | tf_op jit(solution)/shard_map/ppermute | solution.py:347
  24.4 3.6 %collective-permute-start.1 = (s32[4,8]{1,0:T(4,128)S(1)}, s32[4,8]{1,0:T(4,128)S(1)}, u32[]{:S(2)}, u32[]{:S(2)}) collective-permute-start(s32[4,8]{1,0:T(4,128)S(1)} %get-tuple-element.86), channel_id=1, source_target_pairs={{0,16},{8,24},{16,0},{24,8},{1,17},{9,25},{17,1},{25,9},{2,18},{10... | collective-permute-start | bytes 392 | tf_op jit(solution)/shard_map/ppermute | solution.py:347
  28.0 5.6 %collective-permute-start = (s32[4,8]{1,0:T(4,128)S(1)}, s32[4,8]{1,0:T(4,128)S(1)}, u32[]{:S(2)}, u32[]{:S(2)}) collective-permute-start(s32[4,8]{1,0:T(4,128)S(1)} %get-tuple-element.87), channel_id=1, source_target_pairs={{0,8},{8,0},{16,24},{24,16},{1,9},{9,1},{17,25},{25,17},{2,10},{10... | collective-permute-start | bytes 392 | tf_op jit(solution)/shard_map/ppermute | solution.py:347
  28.0 3.4 %copy-start = (bf16[2048,2048]{1,0:T(8,128)(2,1)S(1)}, bf16[2048,2048]{1,0:T(8,128)(2,1)}, u32[]{:S(2)}) copy-start(bf16[2048,2048]{1,0:T(8,128)(2,1)} %refs_2_.7) | copy-start | bytes 25165828
  31.4 2.2 %copy-start.1 = (f32[16,128,128]{2,1,0:T(8,128)S(1)}, f32[16,128,128]{2,1,0:T(8,128)}, u32[]{:S(2)}) copy-start(f32[16,128,128]{2,1,0:T(8,128)} %base_ref.1) | copy-start | bytes 3145732
  31.4 2.2 %copy-start.2 = (bf16[8,128,128]{2,1,0:T(8,128)(2,1)S(1)}, bf16[8,128,128]{2,1,0:T(8,128)(2,1)}, u32[]{:S(2)}) copy-start(bf16[8,128,128]{2,1,0:T(8,128)(2,1)} %get-tuple-element.45.rest_4_) | copy-start | bytes 786436
  40.6 2.7 %slice-start = ((s8[8388608]{0:T(1024)(128)(4,1)}), s8[4194304]{0:T(1024)(128)(4,1)S(1)}, s32[]{:S(2)}) async-start(s8[8388608]{0:T(1024)(128)(4,1)} %bitcast.2), calls=%async_computation | async-start | bytes 8388608
  40.6 3.5 %slice-start.1 = ((s8[8388608]{0:T(1024)(128)(4,1)}), s8[4194304]{0:T(1024)(128)(4,1)S(1)}, s32[]{:S(2)}) async-start(s8[8388608]{0:T(1024)(128)(4,1)} %bitcast.2), calls=%async_computation.1 | async-start | bytes 8388608
  41.4 4.5 %collective-permute-start.7 = (bf16[16,128,128]{2,1,0:T(8,128)(2,1)S(1)}, bf16[16,128,128]{2,1,0:T(8,128)(2,1)S(1)}, u32[]{:S(2)}, u32[]{:S(2)}) collective-permute-start(bf16[16,128,128]{2,1,0:T(8,128)(2,1)S(1)} %far.1.mass_ref), channel_id=1, source_target_pairs={{0,8},{8,0},{16,24},{24,16},{1,9},{9,1},{17,25},{25,17},{2,10},{10... | collective-permute-start | bytes 1572872 | tf_op jit(solution)/shard_map/ppermute | solution.py:347
  51.8 17.9 %collective-permute-start.15 = (bf16[512,256]{1,0:T(8,128)(2,1)S(1)}, bf16[512,256]{1,0:T(8,128)(2,1)S(1)}, u32[]{:S(2)}, u32[]{:S(2)}) collective-permute-start(bf16[512,256]{1,0:T(8,128)(2,1)S(1)} %get-tuple-element.69), channel_id=1, source_target_pairs={{0,1},{1,0},{2,3},{3,2},{4,5},{5,4},{6,7},{7,6},{8,9},{9,8},{10,11... | collective-permute-start | bytes 786440 | tf_op jit(solution)/shard_map/ppermute | solution.py:353
  53.3 16.4 %collective-permute-start.14 = (bf16[256,512]{1,0:T(8,128)(2,1)S(1)}, bf16[256,512]{1,0:T(8,128)(2,1)S(1)}, u32[]{:S(2)}, u32[]{:S(2)}) collective-permute-start(bf16[256,512]{1,0:T(8,128)(2,1)S(1)} %get-tuple-element.53.refs_4_), channel_id=1, source_target_pairs={{0,16},{8,24},{16,0},{24,8},{1,17},{9,25},{17,1},{25,9},{2,18},{10... | collective-permute-start | bytes 786440 | tf_op jit(solution)/shard_map/ppermute | solution.py:347
  68.5 13.0 %collective-permute-start.8 = (bf16[256,512]{1,0:T(8,128)(2,1)S(1)}, bf16[256,512]{1,0:T(8,128)(2,1)S(1)}, u32[]{:S(2)}, u32[]{:S(2)}) collective-permute-start(bf16[256,512]{1,0:T(8,128)(2,1)S(1)} %get-tuple-element.57), channel_id=1, source_target_pairs={{0,16},{8,24},{16,0},{24,8},{1,17},{9,25},{17,1},{25,9},{2,18},{10... | collective-permute-start | bytes 786440 | tf_op jit(solution)/shard_map/ppermute | solution.py:347
  69.1 13.0 %collective-permute-start.9 = (bf16[512,256]{1,0:T(8,128)(2,1)S(1)}, bf16[512,256]{1,0:T(8,128)(2,1)S(1)}, u32[]{:S(2)}, u32[]{:S(2)}) collective-permute-start(bf16[512,256]{1,0:T(8,128)(2,1)S(1)} %get-tuple-element.58), channel_id=1, source_target_pairs={{0,1},{1,0},{2,3},{3,2},{4,5},{5,4},{6,7},{7,6},{8,9},{9,8},{10,11... | collective-permute-start | bytes 786440 | tf_op jit(solution)/shard_map/ppermute | solution.py:353
  78.0 13.6 %collective-permute-start.22 = (bf16[256,512]{1,0:T(8,128)(2,1)S(1)}, bf16[256,512]{1,0:T(8,128)(2,1)S(1)}, u32[]{:S(2)}, u32[]{:S(2)}) collective-permute-start(bf16[256,512]{1,0:T(8,128)(2,1)S(1)} %get-tuple-element.79), channel_id=1, source_target_pairs={{0,16},{8,24},{16,0},{24,8},{1,17},{9,25},{17,1},{25,9},{2,18},{10... | collective-permute-start | bytes 786440 | tf_op jit(solution)/shard_map/ppermute | solution.py:347
  79.4 13.7 %collective-permute-start.23 = (bf16[512,256]{1,0:T(8,128)(2,1)S(1)}, bf16[512,256]{1,0:T(8,128)(2,1)S(1)}, u32[]{:S(2)}, u32[]{:S(2)}) collective-permute-start(bf16[512,256]{1,0:T(8,128)(2,1)S(1)} %get-tuple-element.80), channel_id=1, source_target_pairs={{0,1},{1,0},{2,3},{3,2},{4,5},{5,4},{6,7},{7,6},{8,9},{9,8},{10,11... | collective-permute-start | bytes 786440 | tf_op jit(solution)/shard_map/ppermute | solution.py:353
  80.9 12.8 %collective-permute-start.16 = (bf16[256,256]{1,0:T(8,128)(2,1)S(1)}, bf16[256,256]{1,0:T(8,128)(2,1)S(1)}, u32[]{:S(2)}, u32[]{:S(2)}) collective-permute-start(bf16[256,256]{1,0:T(8,128)(2,1)S(1)} %get-tuple-element.72), channel_id=1, source_target_pairs={{0,1},{1,0},{2,3},{3,2},{4,5},{5,4},{6,7},{7,6},{8,9},{9,8},{10,11... | collective-permute-start | bytes 393224 | tf_op jit(solution)/shard_map/ppermute | solution.py:353
  81.4 13.0 %collective-permute-start.17 = (bf16[256,256]{1,0:T(8,128)(2,1)S(1)}, bf16[256,256]{1,0:T(8,128)(2,1)S(1)}, u32[]{:S(2)}, u32[]{:S(2)}) collective-permute-start(bf16[256,256]{1,0:T(8,128)(2,1)S(1)} %get-tuple-element.73), channel_id=1, source_target_pairs={{0,16},{8,24},{16,0},{24,8},{1,17},{9,25},{17,1},{25,9},{2,18},{10... | collective-permute-start | bytes 393224 | tf_op jit(solution)/shard_map/ppermute | solution.py:347
  82.2 13.7 %collective-permute-start.19 = (bf16[256,256]{1,0:T(8,128)(2,1)S(1)}, bf16[256,256]{1,0:T(8,128)(2,1)S(1)}, u32[]{:S(2)}, u32[]{:S(2)}) collective-permute-start(bf16[256,256]{1,0:T(8,128)(2,1)S(1)} %get-tuple-element.75), channel_id=1, source_target_pairs={{0,1},{1,0},{2,3},{3,2},{4,5},{5,4},{6,7},{7,6},{8,9},{9,8},{10,11... | collective-permute-start | bytes 393224 | tf_op jit(solution)/shard_map/ppermute | solution.py:353
  91.6 6.5 %collective-permute-start.20 = (bf16[256,256]{1,0:T(8,128)(2,1)S(1)}, bf16[256,256]{1,0:T(8,128)(2,1)S(1)}, u32[]{:S(2)}, u32[]{:S(2)}) collective-permute-start(bf16[256,256]{1,0:T(8,128)(2,1)S(1)} %get-tuple-element.76), channel_id=1, source_target_pairs={{0,16},{8,24},{16,0},{24,8},{1,17},{9,25},{17,1},{25,9},{2,18},{10... | collective-permute-start | bytes 393224 | tf_op jit(solution)/shard_map/ppermute | solution.py:347
  93.1 12.9 %collective-permute-start.10 = (bf16[256,512]{1,0:T(8,128)(2,1)S(1)}, bf16[256,512]{1,0:T(8,128)(2,1)S(1)}, u32[]{:S(2)}, u32[]{:S(2)}) collective-permute-start(bf16[256,512]{1,0:T(8,128)(2,1)S(1)} %get-tuple-element.62), channel_id=1, source_target_pairs={{0,16},{8,24},{16,0},{24,8},{1,17},{9,25},{17,1},{25,9},{2,18},{10... | collective-permute-start | bytes 786440 | tf_op jit(solution)/shard_map/ppermute | solution.py:347
  93.8 12.3 %collective-permute-start.11 = (bf16[512,256]{1,0:T(8,128)(2,1)S(1)}, bf16[512,256]{1,0:T(8,128)(2,1)S(1)}, u32[]{:S(2)}, u32[]{:S(2)}) collective-permute-start(bf16[512,256]{1,0:T(8,128)(2,1)S(1)} %get-tuple-element.63), channel_id=1, source_target_pairs={{0,1},{1,0},{2,3},{3,2},{4,5},{5,4},{6,7},{7,6},{8,9},{9,8},{10,11... | collective-permute-start | bytes 786440 | tf_op jit(solution)/shard_map/ppermute | solution.py:353
  94.4 7.8 %collective-permute-start.24 = (bf16[256,256]{1,0:T(8,128)(2,1)S(1)}, bf16[256,256]{1,0:T(8,128)(2,1)S(1)}, u32[]{:S(2)}, u32[]{:S(2)}) collective-permute-start(bf16[256,256]{1,0:T(8,128)(2,1)S(1)} %get-tuple-element.83), channel_id=1, source_target_pairs={{0,1},{1,0},{2,3},{3,2},{4,5},{5,4},{6,7},{7,6},{8,9},{9,8},{10,11... | collective-permute-start | bytes 393224 | tf_op jit(solution)/shard_map/ppermute | solution.py:353
  95.9 10.0 %collective-permute-start.25 = (bf16[256,256]{1,0:T(8,128)(2,1)S(1)}, bf16[256,256]{1,0:T(8,128)(2,1)S(1)}, u32[]{:S(2)}, u32[]{:S(2)}) collective-permute-start(bf16[256,256]{1,0:T(8,128)(2,1)S(1)} %get-tuple-element.84), channel_id=1, source_target_pairs={{0,16},{8,24},{16,0},{24,8},{1,17},{9,25},{17,1},{25,9},{2,18},{10... | collective-permute-start | bytes 393224 | tf_op jit(solution)/shard_map/ppermute | solution.py:347
  98.1 18.6 %collective-permute-start.18 = (bf16[512,256]{1,0:T(8,128)(2,1)S(1)}, bf16[512,256]{1,0:T(8,128)(2,1)S(1)}, u32[]{:S(2)}, u32[]{:S(2)}) collective-permute-start(bf16[512,256]{1,0:T(8,128)(2,1)S(1)} %add_second.4), channel_id=1, source_target_pairs={{0,4},{1,5},{2,6},{3,7},{4,0},{5,1},{6,2},{7,3},{8,12},{9,13},{10,... | collective-permute-start | bytes 786440 | tf_op jit(solution)/shard_map/ppermute | solution.py:353
  102.3 14.4 %collective-permute-start.21 = (bf16[512,256]{1,0:T(8,128)(2,1)S(1)}, bf16[512,256]{1,0:T(8,128)(2,1)S(1)}, u32[]{:S(2)}, u32[]{:S(2)}) collective-permute-start(bf16[512,256]{1,0:T(8,128)(2,1)S(1)} %add_second.5), channel_id=1, source_target_pairs={{0,6},{1,7},{2,4},{3,5},{4,2},{5,3},{6,0},{7,1},{8,14},{9,15},{10,... | collective-permute-start | bytes 786440 | tf_op jit(solution)/shard_map/ppermute | solution.py:353
  105.9 11.9 %collective-permute-start.26 = (bf16[512,256]{1,0:T(8,128)(2,1)S(1)}, bf16[512,256]{1,0:T(8,128)(2,1)S(1)}, u32[]{:S(2)}, u32[]{:S(2)}) collective-permute-start(bf16[512,256]{1,0:T(8,128)(2,1)S(1)} %add_second.6), channel_id=1, source_target_pairs={{0,2},{1,3},{2,0},{3,1},{4,6},{5,7},{6,4},{7,5},{8,10},{9,11},{10,... | collective-permute-start | bytes 786440 | tf_op jit(solution)/shard_map/ppermute | solution.py:353
  106.1 10.5 %collective-permute-start.12 = (bf16[256,256]{1,0:T(8,128)(2,1)S(1)}, bf16[256,256]{1,0:T(8,128)(2,1)S(1)}, u32[]{:S(2)}, u32[]{:S(2)}) collective-permute-start(bf16[256,256]{1,0:T(8,128)(2,1)S(1)} %get-tuple-element.66), channel_id=1, source_target_pairs={{0,1},{1,0},{2,3},{3,2},{4,5},{5,4},{6,7},{7,6},{8,9},{9,8},{10,11... | collective-permute-start | bytes 393224 | tf_op jit(solution)/shard_map/ppermute | solution.py:353
  106.7 9.9 %collective-permute-start.13 = (bf16[256,256]{1,0:T(8,128)(2,1)S(1)}, bf16[256,256]{1,0:T(8,128)(2,1)S(1)}, u32[]{:S(2)}, u32[]{:S(2)}) collective-permute-start(bf16[256,256]{1,0:T(8,128)(2,1)S(1)} %get-tuple-element.67), channel_id=1, source_target_pairs={{0,16},{8,24},{16,0},{24,8},{1,17},{9,25},{17,1},{25,9},{2,18},{10... | collective-permute-start | bytes 393224 | tf_op jit(solution)/shard_map/ppermute | solution.py:347

commit v3 on v0

v3 whole, which is shorter than its diff:
```python
import functools

import jax
import jax.numpy as jnp
from jax import lax
from jax.experimental import pallas as pl
from jax.experimental.pallas import tpu as pltpu
from jax.sharding import PartitionSpec as P

CAP = 8
CORES = 2
MIB = 1024 * 1024
SMEM = pl.BlockSpec(memory_space=pltpu.SMEM)
VMEM = pl.BlockSpec(memory_space=pltpu.VMEM)


def params(mib):
    return pltpu.CompilerParams(vmem_limit_bytes=mib * MIB)


def cheap():
    return pl.CostEstimate(flops=1, bytes_accessed=1, transcendentals=0)


ANY = pl.BlockSpec(memory_space=pl.ANY)


def prep_kernel(owner_links, blk_dev, n_sub, adj_ref, spot_ref, dest_ref, *refs):
    lists, (flat_ref, count_ref) = refs[:n_sub], refs[n_sub:]
    sub = lax.axis_index("sub")
    spot_ref[0] = sub
    spot_ref[1] = lax.axis_index("tile")
    subs, links = adj_ref.shape
    for d in range(n_sub):
        count_ref[d] = 0
        for i in range(CAP):
            flat_ref[d * CAP + i] = blk_dev
    for s in range(subs):
        for a in range(links):
            ident = adj_ref[s, a]
            rel = (ident // owner_links) ^ sub
            slot = count_ref[rel]
            count_ref[rel] = slot + 1
            flat_ref[rel * CAP + slot] = ident % blk_dev
            dest_ref[s, a] = rel * CAP + slot
    for d in range(n_sub):
        for i in range(CAP):
            lists[d][i] = flat_ref[d * CAP + i]


def make_prep(adjacency, n_sub, owner_links, blk_dev):
    int_of = lambda *shape: jax.ShapeDtypeStruct(shape, jnp.int32)
    return pl.pallas_call(
        functools.partial(prep_kernel, owner_links, blk_dev, n_sub),
        in_specs=[SMEM],
        out_specs=[SMEM] * (2 + n_sub),
        out_shape=[int_of(2), int_of(*adjacency.shape)] + [int_of(CAP)] * n_sub,
        scratch_shapes=[pltpu.SMEM((n_sub * CAP,), jnp.int32), pltpu.SMEM((n_sub,), jnp.int32)],
        compiler_params=params(60),
        cost_estimate=cheap(),
        name="prep",
    )(adjacency)


def contrib_kernel(rows_ref, dest_ref, modes_ref, coup_ref, inv_ref, *refs):
    outs, (part_ref, all_ref) = refs[:-2], refs[-2:]
    s = pl.program_id(0)
    links, rows, block = coup_ref.shape[1:]
    live = lax.broadcasted_iota(jnp.int32, (rows, 1), 0) < rows_ref[s]
    modes = jnp.where(live, modes_ref[0], jnp.zeros((), modes_ref.dtype))
    inv = inv_ref[pl.ds(s, 1), :]
    wide = jnp.concatenate([coup_ref[0, a] for a in range(links)], axis=1)
    red = lax.dot_general(
        wide, modes, (((0,), (0,)), ((), ())), preferred_element_type=jnp.float32
    )
    weighted = (red * inv).astype(jnp.bfloat16)
    red_b = red.astype(jnp.bfloat16)
    for a in range(links):
        part = slice(a * block, (a + 1) * block)
        part_ref[a] = lax.dot_general(
            weighted[part], red_b[part], (((1,), (1,)), ((), ())),
            preferred_element_type=jnp.float32,
        ).astype(jnp.bfloat16)
    for a in range(links):
        all_ref[dest_ref[s, a]] = part_ref[a]

    @pl.when(s == pl.num_programs(0) - 1)
    def _():
        for d, out in enumerate(outs):
            out[...] = all_ref[d * CAP:(d + 1) * CAP]


def make_contrib(dest, modes, coupling, inv_eig, sub_rows, n_sub):
    subs, rows, width = modes.shape
    links, block = coupling.shape[1], coupling.shape[3]
    out = jax.ShapeDtypeStruct((CAP, block, block), jnp.bfloat16)
    return pl.pallas_call(
        contrib_kernel,
        grid=(subs,),
        in_specs=[
            SMEM, SMEM,
            pl.BlockSpec((1, rows, width), lambda s: (s, 0, 0)),
            pl.BlockSpec((1, links, rows, block), lambda s: (s, 0, 0, 0)),
            pl.BlockSpec(inv_eig.shape, lambda s: (0, 0)),
        ],
        out_specs=[pl.BlockSpec(out.shape, lambda s: (0, 0, 0))] * n_sub,
        out_shape=[out] * n_sub,
        scratch_shapes=[
            pltpu.VMEM((links, block, block), jnp.bfloat16),
            pltpu.VMEM((n_sub * CAP, block, block), jnp.bfloat16),
        ],
        compiler_params=params(55),
        cost_estimate=cheap(),
        name="contrib",
    )(sub_rows, dest, modes, coupling, inv_eig)


def near_kernel(base_ref, own_at, pair_at, own_ref, pair_ref, total_ref):
    total_ref[:base_ref.shape[0]] = base_ref[...]
    for place, group in ((own_at, own_ref), (pair_at, pair_ref)):
        for i in range(CAP):
            total_ref[place[i]] += group[i].astype(jnp.float32)


def make_near(base, places, groups):
    blk_dev, block = base.shape[:2]
    return pl.pallas_call(
        near_kernel,
        in_specs=[VMEM] + [SMEM] * 2 + [VMEM] * 2,
        out_specs=VMEM,
        out_shape=jax.ShapeDtypeStruct((blk_dev + 1, block, block), jnp.float32),
        compiler_params=params(12),
        cost_estimate=cheap(),
        name="near",
    )(base, *places, *groups)


def far_kernel(count, near_ref, *rest):
    mass_ref, total_ref = rest[-2:]
    total_ref[...] = near_ref[...]
    for place, group in zip(rest[:count], rest[count:2 * count]):
        for i in range(CAP):
            total_ref[place[i]] += group[i].astype(jnp.float32)
    mass_ref[...] = total_ref[:mass_ref.shape[0]].astype(jnp.bfloat16)


def make_far(near, places, groups, behind):
    count, block = near.shape[:2]
    return pl.pallas_call(
        functools.partial(far_kernel, len(groups)),
        in_specs=[VMEM] + [SMEM] * len(places) + [VMEM] * len(groups) + [ANY] * len(behind),
        out_specs=VMEM,
        out_shape=jax.ShapeDtypeStruct((count - 1, block, block), jnp.bfloat16),
        scratch_shapes=[pltpu.VMEM(near.shape, jnp.float32)],
        compiler_params=params(12),
        cost_estimate=cheap(),
        name="far",
    )(near, *places, *groups, *behind)


def turn_kernel(spot_ref, psi_ref, out_ref, copy_ref, sems):
    band, n_sub = out_ref.shape[1], sems.shape[0]

    def bring(j):
        at = pl.ds(pl.multiple_of((spot_ref[0] ^ j) * band, band), band)
        return pltpu.make_async_copy(psi_ref.at[:, at], copy_ref.at[:, at], sems.at[j])

    order = list(range(0, n_sub, CORES)) + [j for j in range(n_sub) if j % CORES]
    for j in order:
        bring(j).start()
    for j in order:
        bring(j).wait()
        if j % CORES == 0:
            at = pl.multiple_of((spot_ref[0] ^ j) * band, band)
            out_ref[j // CORES] = copy_ref[:, pl.ds(at, band)].T


def turn(spot, psi, n_sub):
    depth, width = psi.shape
    shape = (n_sub // CORES, width // n_sub, depth)
    return pl.pallas_call(
        turn_kernel,
        in_specs=[SMEM, ANY],
        out_specs=[VMEM, VMEM],
        out_shape=[
            jax.ShapeDtypeStruct(shape, psi.dtype), jax.ShapeDtypeStruct(psi.shape, psi.dtype)
        ],
        scratch_shapes=[pltpu.SemaphoreType.DMA((n_sub,))],
        compiler_params=params(16),
        cost_estimate=cheap(),
        name="turn",
    )(spot, psi)


def left_kernel(mass_ref, turned_ref, out_ref):
    block = mass_ref.shape[1]
    zero = jnp.zeros((block, block), jnp.bfloat16)
    groups, half, _ = turned_ref.shape
    for j in range(0, mass_ref.shape[0], 2):
        pair = jnp.concatenate(
            [
                jnp.concatenate([mass_ref[j], zero], axis=1),
                jnp.concatenate([zero, mass_ref[j + 1]], axis=1),
            ],
            axis=0,
        )
        cols = slice(j * block, (j + 2) * block)
        out_ref[:, cols] = jnp.dot(
            turned_ref[:, :, cols].reshape(groups * half, 2 * block), pair,
            preferred_element_type=jnp.float32,
        ).astype(jnp.bfloat16)


def make_left(mass, turned):
    groups, half, depth = turned.shape
    return pl.pallas_call(
        left_kernel,
        in_specs=[VMEM, VMEM],
        out_specs=VMEM,
        out_shape=jax.ShapeDtypeStruct((groups * half, depth), jnp.bfloat16),
        compiler_params=params(16),
        cost_estimate=cheap(),
        name="left",
    )(mass, turned)


def product_kernel(chunk, pairs, acc_in, go, keep, behind, spot_ref, *refs):
    lefts, psis, refs = refs[:pairs], refs[pairs:2 * pairs], refs[2 * pairs:]
    acc = refs[0] if acc_in else None
    outs = list(refs[int(acc_in) + behind:])
    high, z = chunk
    core = spot_ref[0] % CORES

    def block(x, y):
        band, width = outs[0].shape[1:]
        rows = pl.ds(pl.multiple_of((2 * high + x) * band, band), band)
        tile = spot_ref[1] ^ (2 * z + y)
        cols = pl.ds(pl.multiple_of(tile * width, width), width)
        res = None
        for left, psi in zip(lefts, psis):
            term = jnp.dot(left[rows], psi[:, cols], preferred_element_type=jnp.float32)
            res = term if res is None else res + term
        return res

    places = []
    if go:
        places += [(outs[0], 0, 1, 1), (outs[0], 1, 1 - core, core)]
    if keep:
        places += [(outs[-1], 0, 0, 0), (outs[-1], 1, core, 1 - core)]
    for out, i, x, y in places:
        res = block(x, y)
        if acc_in:
            res += acc[i]
        out[i] = res.astype(out.dtype)


def product(chunk, spot, lefts, psis, band, width, go=None, keep=False, acc=(), behind=()):
    depth = lefts[0].shape[1]
    types = ([go] if go is not None else []) + ([jnp.float32] if keep else [])
    flops = len(types) * 4 * band * width * depth * len(lefts)
    return pl.pallas_call(
        functools.partial(
            product_kernel, chunk, len(lefts), bool(acc), go is not None, keep, len(behind)
        ),
        in_specs=[SMEM] + [VMEM] * (2 * len(lefts) + len(acc)) + [ANY] * len(behind),
        out_specs=[VMEM] * len(types),
        out_shape=[jax.ShapeDtypeStruct((2, band, width), t) for t in types],
        compiler_params=params(16),
        cost_estimate=pl.CostEstimate(
            flops=flops, bytes_accessed=flops // 512, transcendentals=0
        ),
        name="product",
    )(spot, *lefts, *psis, *acc, *behind)


def first_kernel(keep_ref, got_ref, *refs):
    low_ref, go_ref = refs[-2:]
    low_ref[...] = keep_ref[0] + got_ref[1].astype(jnp.float32)
    go_ref[...] = (keep_ref[1] + got_ref[0].astype(jnp.float32)).astype(jnp.bfloat16)


def add_first(keep, got, behind=()):
    shape = keep.shape[1:]
    return pl.pallas_call(
        first_kernel,
        in_specs=[VMEM] * 2 + [ANY] * len(behind),
        out_specs=[VMEM] * 2,
        out_shape=[jax.ShapeDtypeStruct(shape, t) for t in (jnp.float32, jnp.bfloat16)],
        compiler_params=params(12),
        cost_estimate=cheap(),
        name="add_first",
    )(keep, got, *behind)


def second_kernel(low_ref, got_ref, *refs):
    total = low_ref[...] + got_ref[...].astype(jnp.float32)
    for v in refs[:-1]:
        total += v[...].astype(jnp.float32)
    refs[-1][...] = total.astype(refs[-1].dtype)


def add_second(low, got, dtype, tails=()):
    return pl.pallas_call(
        second_kernel,
        in_specs=[VMEM] * (2 + len(tails)),
        out_specs=VMEM,
        out_shape=jax.ShapeDtypeStruct(low.shape, dtype),
        compiler_params=params(12),
        cost_estimate=cheap(),
        name="add_second",
    )(low, got, *tails)


def on_device(modes, coupling, inv_eig, sub_rows, adjacency, base_mass, iface_modes):
    n_sub = lax.axis_size("sub")
    n_tile = lax.axis_size("tile")
    blk_dev = base_mass.shape[0]
    owner_links = blk_dev * n_tile
    width = iface_modes.shape[1]
    band, tile = width // n_sub, width // n_tile
    def swap_sub(v, d):
        return lax.ppermute(v, "sub", [(i, i ^ d) for i in range(n_sub)])

    def swap(v, partner):
        pairs = []
        for i in range(n_sub):
            for j in range(n_tile):
                k, m = partner(i, j)
                pairs.append((i * n_tile + j, k * n_tile + m))
        return lax.ppermute(v, ("sub", "tile"), pairs)

    def swap_first(v):
        return swap(v, lambda i, j: (i, j ^ 1) if i % CORES else (i ^ CORES, j))

    def swap_second(v):
        return swap(v, lambda i, j: (i ^ CORES, j) if i % CORES else (i, j ^ 1))

    def swap_third(v, chunk):
        high, z = chunk
        bit = z & -z if z else 0
        step = 0 if z else (high & -high) * 2 * CORES
        return swap(v, lambda i, j: (i ^ step, j ^ (2 * bit)))

    spot, dest, *lists = make_prep(adjacency, n_sub, owner_links, blk_dev)
    lists = [swap_sub(v, d) if d else v for d, v in enumerate(lists)]
    other = swap_sub(iface_modes, 1)
    sent = make_contrib(dest, modes, coupling, inv_eig, sub_rows, n_sub)
    far = [swap_sub(sent[d], d) for d in range(CORES, n_sub)]
    near = make_near(base_mass, lists[:CORES], [sent[0], swap_sub(sent[1], 1)])
    own_t, own = turn(spot, iface_modes, n_sub)
    other_t, other = turn(spot, other, n_sub)
    mass = make_far(near, lists[CORES:], far, [own_t, other_t])
    mass_other = swap_sub(mass, 1)
    left = make_left(mass, own_t)

    chunks = [(h, z) for h in range(n_sub // (2 * CORES)) for z in range(n_tile // 2)][::-1]
    goes_to = {(h, z): (h, z & (z - 1)) if z else (h & (h - 1), 0) for h, z in chunks[:-1]}
    head = product(chunks[0], spot, [left], [own], band, tile, go=jnp.float32)
    left_other = make_left(mass_other, other_t)
    lefts, psis = [left, left_other], [own, other]

    keep, first, second, third = {}, {}, {}, []
    tails = {c: [] for c in chunks}
    last = len(chunks) - 1
    for i in range(last + 2):
        if i == 0:
            go, = product(
                chunks[0], spot, [left_other], [other], band, tile, go=jnp.bfloat16, acc=head
            )
            keep[0], = product(
                chunks[0], spot, lefts, psis, band, tile, keep=True, behind=[go]
            )
            first[0] = swap_first(go)
        elif i <= last:
            behind = [keep[0]] if i == 1 else [second[i - 2][0]]
            go, keep[i] = product(
                chunks[i], spot, lefts, psis, band, tile, go=jnp.bfloat16, keep=True,
                behind=behind,
            )
            first[i] = swap_first(go)
        if i > 1:
            chunk = chunks[i - 2]
            third.append(add_second(*second[i - 2], jnp.bfloat16, tails[chunk]))
            tails[goes_to[chunk]].append(swap_third(third[-1], chunk))
        if i:
            low, go = add_first(keep[i - 1], first[i - 1], third[i - 2:])
            second[i - 1] = low, swap_second(go)
    low, got = second[last]
    early, late = tails[chunks[-1]][:-1], tails[chunks[-1]][-1:]
    if early:
        low = add_second(low, early[0], jnp.float32, early[1:])
    return add_second(low, got, jnp.float32, late)


def solution(mesh):
    placed = (
        P(("sub", "tile"), None, None),
        P(("sub", "tile"), None, None, None),
        P(("sub", "tile"), None),
        P(("sub", "tile")),
        P(("sub", "tile"), None),
        P(("sub", "tile"), None, None),
        P(("sub", "tile"), None),
    )
    return jax.shard_map(
        on_device, mesh=mesh, in_specs=placed, out_specs=P("sub", "tile"), check_vma=False
    )
```

time: 244 us -> 86.3 us (0.35)
  waiting for transfers between devices: 175 us -> 17.3 us
  Pallas kernels: 0 us -> 45.7 us
  matrix products: 38.5 us -> 0 us
  starting transfers between devices: 7.99 us -> 22.8 us
  between operations: 13.5 us -> 0.28 us
  other arithmetic: 5.19 us -> 0 us
  local copies, waits for them, and re-layouts: 3.57 us -> 0.04 us
    reduce_scatter x2 -> x0, waiting for transfers between devices: 161 us -> none  [the longest x1 88 us: on_device(): lax.psum_scatter(row_band, 'tile', scatter_dimension=1, tiled=True)]
    pallas_call x0 -> x23, Pallas kernels: none -> 45.7 us  [the longest x6 22.2 us: product(): pl.pallas_call(functools.partial(product_kernel, chunk, len(lefts), bool(...]
    dot_general x6 -> x0, matrix products: 38.5 us -> none  [the longest x1 20.6 us: on_device(): lax.dot_general(iface_modes, image, (((0,), (0,)), ((), ())), preferred_e...]
    ppermute x0 -> x19, starting transfers between devices: none -> 22.8 us  [the longest x11 17 us: swap(): return lax.ppermute(v, ('sub', 'tile'), pairs)]
    ppermute x0 -> x19, waiting for transfers between devices: none -> 17.3 us  [the longest x11 15.3 us: swap(): return lax.ppermute(v, ('sub', 'tile'), pairs)]
    all_to_all x2 -> x0, waiting for transfers between devices: 14.1 us -> none  [the longest x1 14.1 us: on_device(): lax.all_to_all(outgoing, 'sub', split_axis=0, concat_axis=0, tiled=True)]
    all_to_all x2 -> x0, starting transfers between devices: 7.72 us -> none  [the longest x1 4.21 us: on_device(): lax.all_to_all(out_ids, 'sub', split_axis=0, concat_axis=0, tiled=True)]
    convert_element_type x2 -> x0, other arithmetic: 4.85 us -> none  [the longest x1 4.12 us: on_device(): row_band = lax.psum_scatter(lax.dot_general(iface_modes, image, (((0,), (...]
  transfers between devices with their start and end apart: 4 -> 19, of which waited for: 3 -> 7; matrix products, arithmetic and copies ran while one was open for 5% -> 0% of each run, Pallas kernels for 0% -> 48%
where the time goes in v3:
time: 86.3 us; the launch traced here: 86.1 us
  Pallas kernels  45.7 us (53%)
  starting transfers between devices  22.8 us (26%)
  waiting for transfers between devices  17.3 us (20%)
    pallas_call x6, Pallas kernels, product(): pl.pallas_call(functools.partial(product_kernel, chunk, len(lefts), bool(...  22.2 us
    ppermute x11, starting transfers between devices, swap(): return lax.ppermute(v, ('sub', 'tile'), pairs)  17 us
    ppermute x11, waiting for transfers between devices, swap(): return lax.ppermute(v, ('sub', 'tile'), pairs)  15.3 us
    pallas_call x1, Pallas kernels, make_contrib(): pl.pallas_call(contrib_kernel, grid=(subs,), in_specs=[SMEM, SMEM, pl.Blo...  9.2 us
    pallas_call x2, Pallas kernels, turn(): pl.pallas_call(turn_kernel, in_specs=[SMEM, ANY], out_specs=[VMEM, VMEM],...  7.29 us
    ppermute x8, starting transfers between devices, swap_sub(): return lax.ppermute(v, 'sub', [(i, i ^ d) for i in range(n_sub)])  5.73 us
    pallas_call x2, Pallas kernels, make_left(): pl.pallas_call(left_kernel, in_specs=[VMEM, VMEM], out_specs=VMEM, out_sh...  2.52 us
    ppermute x8, waiting for transfers between devices, swap_sub(): return lax.ppermute(v, 'sub', [(i, i ^ d) for i in range(n_sub)])  1.98 us
  transfers between devices with their start and end apart: 19, of which 7 were waited for; matrix products, arithmetic and copies ran while one was open for 0% of the time, Pallas kernels for 48%

profile of v3, /device:TPU:0, one launch (start us, length us, event | category | flops | bytes accessed | tf_op | source)
XLA Modules:
  0.0 86.1 jit_solution(18415000147111399896)
XLA Ops:
  0.0 0.5 collective-permute-start.6
  0.5 1.6 %prep.1 = (s32[2]{0:T(128)}, s32[4,8]{1,0:T(4,128)}, s32[8]{0:T(128)}, s32[8]{0:T(128)}, s32[8]{0:T(128)}, /*index=5*/s32[8]{0:T(128)}) custom-call(s32[4,8]{1,0:T(4,128)} %adj_ref.1), custom_call_target="tpu_custom_call" | custom-call | flops 1 | bytes 1 | tf_op jit(solution)/shard_map/prep/pallas_call | solution.py:53
  2.1 0.0 copy-start
  2.1 9.2 %contrib.1 = (bf16[8,128,128]{2,1,0:T(8,128)(2,1)}, bf16[8,128,128]{2,1,0:T(8,128)(2,1)}, bf16[8,128,128]{2,1,0:T(8,128)(2,1)}, bf16[8,128,128]{2,1,0:T(8,128)(2,1)}) custom-call(s32[4]{0:T(128)} %rows_ref.1, s32[4,8]{1,0:T(4,128)} %get-tuple-element.36.dest_ref, bf16[4,768,512]{2,1,0:T(8,128)(2,1)} %modes_ref.1, bf16[4,8,768,128]{3,2,1,0:T(8,128)(2,1)} %coup_ref.1, ...), custom_call_target="tpu_custom_call" | custom-call | flops 1 | bytes 1 | tf_op jit(solution)/shard_map/contrib/pallas_call | solution.py:97
  11.3 0.1 collective-permute-start.1
  11.3 2.9 %collective-permute-start.4 = (bf16[8,128,128]{2,1,0:T(8,128)(2,1)}, bf16[8,128,128]{2,1,0:T(8,128)(2,1)S(1)}, u32[]{:S(2)}, u32[]{:S(2)}) collective-permute-start(bf16[8,128,128]{2,1,0:T(8,128)(2,1)} %get-tuple-element.41), channel_id=1, source_target_pairs={{0,16},{8,24},{16,0},{24,8},{1,17},{9,25},{17,1},{25,9},{2,18},{10... | collective-permute-start | bytes 786440 | tf_op jit(solution)/shard_map/ppermute | solution.py:322
  14.3 0.0 collective-permute-start.5
  14.3 0.1 collective-permute-start
  14.4 0.0 copy-start.1
  14.5 0.0 copy-start.2
  14.5 3.2 %turn.2 = (bf16[2,512,2048]{2,1,0:T(8,128)(2,1)S(1)}, bf16[2048,2048]{1,0:T(8,128)(2,1)S(1)}) custom-call(s32[2]{0:T(128)S(1)} %copy-done.3, bf16[2048,2048]{1,0:T(8,128)(2,1)S(1)} %copy-done), custom_call_target="tpu_custom_call" | custom-call | flops 1 | bytes 1 | tf_op jit(solution)/shard_map/turn/pallas_call | solution.py:181
  17.7 2.1 %collective-permute-start.2 = (s32[8]{0:T(128)S(1)}, s32[8]{0:T(128)S(1)}, u32[]{:S(2)}, u32[]{:S(2)}) collective-permute-start(s32[8]{0:T(128)S(1)} %copy-done.6), channel_id=1, source_target_pairs={{0,16},{8,24},{16,0},{24,8},{1,17},{9,25},{17,1},{25,9},{2,18},{10... | collective-permute-start | bytes 104 | tf_op jit(solution)/shard_map/ppermute | solution.py:322
  19.8 0.7 near.1.near_ref
  20.6 4.1 %turn.3 = (bf16[2,512,2048]{2,1,0:T(8,128)(2,1)S(1)}, bf16[2048,2048]{1,0:T(8,128)(2,1)S(1)}) custom-call(s32[2]{0:T(128)S(1)} %copy-done.3, bf16[2048,2048]{1,0:T(8,128)(2,1)} %collective-permute-done.6.psi_ref), custom_call_target="tpu_custom_call" | custom-call | flops 1 | bytes 1 | tf_op jit(solution)/shard_map/turn/pallas_call | solution.py:181
  24.7 2.0 %collective-permute-done.2.rest_0_ = s32[8]{0:T(128)S(1)} collective-permute-done((s32[8]{0:T(128)S(1)}, s32[8]{0:T(128)S(1)}, u32[]{:S(2)}, u32[]{:S(2)}) %collective-permute-start.2) | collective-permute-done | bytes 64 | tf_op jit(solution)/shard_map/ppermute | solution.py:322
  26.6 0.8 far.1.mass_ref
  27.4 0.1 collective-permute-start.7
  27.5 1.3 %left.2.refs_0_ = bf16[1024,2048]{1,0:T(8,128)(2,1)S(1)} custom-call(bf16[16,128,128]{2,1,0:T(8,128)(2,1)S(1)} %far.1.mass_ref, bf16[2,512,2048]{2,1,0:T(8,128)(2,1)S(1)} %get-tuple-element.43.rest_4_.turned_ref), custom_call_target="tpu_custom_call" | custom-call | flops 1 | bytes 1 | tf_op jit(solution)/shard_map/left/pallas_call | solution.py:216
  28.8 1.8 %product.6.refs_2_ = f32[2,512,256]{2,1,0:T(8,128)S(1)} custom-call(s32[2]{0:T(128)S(1)} %copy-done.3, bf16[1024,2048]{1,0:T(8,128)(2,1)S(1)} %left.2.refs_0_, bf16[2048,2048]{1,0:T(8,128)(2,1)S(1)} %get-tuple-element.45.refs_1_.refs_2_), custom_call_target="tpu_custom_call" | custom-call | flops 1073741824 | bytes 2097152 | tf_op jit(solution)/shard_map/product/pallas_call | solution.py:261
  30.6 1.3 %left.3.refs_0_.refs_1_ = bf16[1024,2048]{1,0:T(8,128)(2,1)S(1)} custom-call(bf16[16,128,128]{2,1,0:T(8,128)(2,1)S(1)} %collective-permute-done.7.mass_ref, bf16[2,512,2048]{2,1,0:T(8,128)(2,1)S(1)} %get-tuple-element.44.rest_5_.turned_ref), custom_call_target="tpu_custom_call" | custom-call | flops 1 | bytes 1 | tf_op jit(solution)/shard_map/left/pallas_call | solution.py:216
  31.9 1.8 %product.7.refs_4_ = bf16[2,512,256]{2,1,0:T(8,128)(2,1)S(1)} custom-call(s32[2]{0:T(128)S(1)} %copy-done.3, bf16[1024,2048]{1,0:T(8,128)(2,1)S(1)} %left.3.refs_0_.refs_1_, bf16[2048,2048]{1,0:T(8,128)(2,1)S(1)} %get-tuple-element.46.refs_1_.refs_3_, f32[2,512,256]{2,1,0:T(8,128)S(1)} %product.6.refs_2_), custom_call_target="tpu_custom_call" | custom-call | flops 1073741824 | bytes 2097152 | tf_op jit(solution)/shard_map/product/pallas_call | solution.py:261
  33.7 1.8 %collective-permute-start.9 = (bf16[2,512,256]{2,1,0:T(8,128)(2,1)S(1)}, bf16[2,512,256]{2,1,0:T(8,128)(2,1)S(1)}, u32[]{:S(2)}, u32[]{:S(2)}) collective-permute-start(bf16[2,512,256]{2,1,0:T(8,128)(2,1)S(1)} %product.7.refs_4_), channel_id=1, source_target_pairs={{0,16},{1,17},{2,18},{3,19},{4,20},{5,21},{6,22},{7,23},{8,9},{9,8... | collective-permute-start | bytes 1572872 | tf_op jit(solution)/shard_map/ppermute | solution.py:330
  35.6 2.9 %product.8.refs_4_.keep_ref = f32[2,512,256]{2,1,0:T(8,128)S(1)} custom-call(s32[2]{0:T(128)S(1)} %copy-done.3, bf16[1024,2048]{1,0:T(8,128)(2,1)S(1)} %left.2.refs_0_, bf16[1024,2048]{1,0:T(8,128)(2,1)S(1)} %left.3.refs_0_.refs_1_, bf16[2048,2048]{1,0:T(8,128)(2,1)S(1)} %get-tuple-element.45.refs_1_.refs_2_, ...), custom_call_target="tpu_custom_call" | custom-call | flops 2147483648 | bytes 4194304 | tf_op jit(solution)/shard_map/product/pallas_call | solution.py:261
  38.5 5.3 %product.9 = (bf16[2,512,256]{2,1,0:T(8,128)(2,1)S(1)}, f32[2,512,256]{2,1,0:T(8,128)S(1)}) custom-call(s32[2]{0:T(128)S(1)} %copy-done.3, bf16[1024,2048]{1,0:T(8,128)(2,1)S(1)} %left.2.refs_0_, bf16[1024,2048]{1,0:T(8,128)(2,1)S(1)} %left.3.refs_0_.refs_1_, bf16[2048,2048]{1,0:T(8,128)(2,1)S(1)} %get-tuple-element.45.refs_1_.refs_2_, ...), custom_call_target="tpu_custom_call" | custom-call | flops 4294967296 | bytes 8388608 | tf_op jit(solution)/shard_map/product/pallas_call | solution.py:261
  43.8 0.3 collective-permute-start.8
  44.2 0.1 add_first.4
  44.3 1.8 %collective-permute-start.10 = (bf16[512,256]{1,0:T(8,128)(2,1)S(1)}, bf16[512,256]{1,0:T(8,128)(2,1)S(1)}, u32[]{:S(2)}, u32[]{:S(2)}) collective-permute-start(bf16[512,256]{1,0:T(8,128)(2,1)S(1)} %get-tuple-element.50), channel_id=1, source_target_pairs={{0,1},{1,0},{2,3},{3,2},{4,5},{5,4},{6,7},{7,6},{8,24},{9,25},{10,... | collective-permute-start | bytes 786440 | tf_op jit(solution)/shard_map/ppermute | solution.py:330
  46.1 5.1 %product.11 = (bf16[2,512,256]{2,1,0:T(8,128)(2,1)S(1)}, f32[2,512,256]{2,1,0:T(8,128)S(1)}) custom-call(s32[2]{0:T(128)S(1)} %copy-done.3, bf16[1024,2048]{1,0:T(8,128)(2,1)S(1)} %left.2.refs_0_, bf16[1024,2048]{1,0:T(8,128)(2,1)S(1)} %left.3.refs_0_.refs_1_, bf16[2048,2048]{1,0:T(8,128)(2,1)S(1)} %get-tuple-element.45.refs_1_.refs_2_, ...), custom_call_target="tpu_custom_call" | custom-call | flops 4294967296 | bytes 8388608 | tf_op jit(solution)/shard_map/product/pallas_call | solution.py:261
  51.2 1.6 %collective-permute-start.12 = (bf16[2,512,256]{2,1,0:T(8,128)(2,1)S(1)}, bf16[2,512,256]{2,1,0:T(8,128)(2,1)S(1)}, u32[]{:S(2)}, u32[]{:S(2)}) collective-permute-start(bf16[2,512,256]{2,1,0:T(8,128)(2,1)S(1)} %get-tuple-element.55), channel_id=1, source_target_pairs={{0,16},{1,17},{2,18},{3,19},{4,20},{5,21},{6,22},{7,23},{8,9},{9,8... | collective-permute-start | bytes 1572872 | tf_op jit(solution)/shard_map/ppermute | solution.py:330
  52.8 0.7 collective-permute-done.10.got_ref
  53.6 1.9 %collective-permute-start.14 = (bf16[512,256]{1,0:T(8,128)(2,1)S(1)}, bf16[512,256]{1,0:T(8,128)(2,1)S(1)}, u32[]{:S(2)}, u32[]{:S(2)}) collective-permute-start(bf16[512,256]{1,0:T(8,128)(2,1)S(1)} %add_second.5.refs_0_), channel_id=1, source_target_pairs={{0,2},{1,3},{2,0},{3,1},{4,6},{5,7},{6,4},{7,5},{8,10},{9,11},{10,... | collective-permute-start | bytes 786440 | tf_op jit(solution)/shard_map/ppermute | solution.py:330
  55.5 0.1 add_first.5
  55.6 1.6 %collective-permute-start.13 = (bf16[512,256]{1,0:T(8,128)(2,1)S(1)}, bf16[512,256]{1,0:T(8,128)(2,1)S(1)}, u32[]{:S(2)}, u32[]{:S(2)}) collective-permute-start(bf16[512,256]{1,0:T(8,128)(2,1)S(1)} %get-tuple-element.56), channel_id=1, source_target_pairs={{0,1},{1,0},{2,3},{3,2},{4,5},{5,4},{6,7},{7,6},{8,24},{9,25},{10,... | collective-permute-start | bytes 786440 | tf_op jit(solution)/shard_map/ppermute | solution.py:330
  57.2 5.1 %product.10 = (bf16[2,512,256]{2,1,0:T(8,128)(2,1)S(1)}, f32[2,512,256]{2,1,0:T(8,128)S(1)}) custom-call(s32[2]{0:T(128)S(1)} %copy-done.3, bf16[1024,2048]{1,0:T(8,128)(2,1)S(1)} %left.2.refs_0_, bf16[1024,2048]{1,0:T(8,128)(2,1)S(1)} %left.3.refs_0_.refs_1_, bf16[2048,2048]{1,0:T(8,128)(2,1)S(1)} %get-tuple-element.45.refs_1_.refs_2_, ...), custom_call_target="tpu_custom_call" | custom-call | flops 4294967296 | bytes 8388608 | tf_op jit(solution)/shard_map/product/pallas_call | solution.py:261
  62.3 1.5 %collective-permute-start.11 = (bf16[2,512,256]{2,1,0:T(8,128)(2,1)S(1)}, bf16[2,512,256]{2,1,0:T(8,128)(2,1)S(1)}, u32[]{:S(2)}, u32[]{:S(2)}) collective-permute-start(bf16[2,512,256]{2,1,0:T(8,128)(2,1)S(1)} %get-tuple-element.53), channel_id=1, source_target_pairs={{0,16},{1,17},{2,18},{3,19},{4,20},{5,21},{6,22},{7,23},{8,9},{9,8... | collective-permute-start | bytes 1572872 | tf_op jit(solution)/shard_map/ppermute | solution.py:330
  63.9 0.1 add_second.6.refs_0_
  64.0 0.1 add_first.6
  64.1 1.6 %collective-permute-start.15 = (bf16[512,256]{1,0:T(8,128)(2,1)S(1)}, bf16[512,256]{1,0:T(8,128)(2,1)S(1)}, u32[]{:S(2)}, u32[]{:S(2)}) collective-permute-start(bf16[512,256]{1,0:T(8,128)(2,1)S(1)} %get-tuple-element.58), channel_id=1, source_target_pairs={{0,1},{1,0},{2,3},{3,2},{4,5},{5,4},{6,7},{7,6},{8,24},{9,25},{10,... | collective-permute-start | bytes 786440 | tf_op jit(solution)/shard_map/ppermute | solution.py:330
  65.7 2.6 %collective-permute-start.16 = (bf16[512,256]{1,0:T(8,128)(2,1)S(1)}, bf16[512,256]{1,0:T(8,128)(2,1)S(1)}, u32[]{:S(2)}, u32[]{:S(2)}) collective-permute-start(bf16[512,256]{1,0:T(8,128)(2,1)S(1)} %add_second.6.refs_0_), channel_id=1, source_target_pairs={{0,4},{1,5},{2,6},{3,7},{4,0},{5,1},{6,2},{7,3},{8,12},{9,13},{10,... | collective-permute-start | bytes 786440 | tf_op jit(solution)/shard_map/ppermute | solution.py:330
  68.2 4.6 %collective-permute-done.15.got_ref = bf16[512,256]{1,0:T(8,128)(2,1)S(1)} collective-permute-done((bf16[512,256]{1,0:T(8,128)(2,1)S(1)}, bf16[512,256]{1,0:T(8,128)(2,1)S(1)}, u32[]{:S(2)}, u32[]{:S(2)}) %collective-permute-start.15) | collective-permute-done | bytes 262176 | tf_op jit(solution)/shard_map/ppermute | solution.py:330
  72.9 1.5 %collective-permute-done.11.got_ref = bf16[2,512,256]{2,1,0:T(8,128)(2,1)S(1)} collective-permute-done((bf16[2,512,256]{2,1,0:T(8,128)(2,1)S(1)}, bf16[2,512,256]{2,1,0:T(8,128)(2,1)S(1)}, u32[]{:S(2)}, u32[]{:S(2)}) %collective-permute-start.11) | collective-permute-done | bytes 524320 | tf_op jit(solution)/shard_map/ppermute | solution.py:330
  74.4 0.1 add_first.7
  74.5 0.5 collective-permute-start.17
  75.0 1.7 %collective-permute-start.18 = (bf16[512,256]{1,0:T(8,128)(2,1)S(1)}, bf16[512,256]{1,0:T(8,128)(2,1)S(1)}, u32[]{:S(2)}, u32[]{:S(2)}) collective-permute-start(bf16[512,256]{1,0:T(8,128)(2,1)S(1)} %add_second.7.refs_0_), channel_id=1, source_target_pairs={{0,2},{1,3},{2,0},{3,1},{4,6},{5,7},{6,4},{7,5},{8,10},{9,11},{10,... | collective-permute-start | bytes 786440 | tf_op jit(solution)/shard_map/ppermute | solution.py:330
  76.7 3.0 %collective-permute-done.16.got_ref = bf16[512,256]{1,0:T(8,128)(2,1)S(1)} collective-permute-done((bf16[512,256]{1,0:T(8,128)(2,1)S(1)}, bf16[512,256]{1,0:T(8,128)(2,1)S(1)}, u32[]{:S(2)}, u32[]{:S(2)}) %collective-permute-start.16) | collective-permute-done | bytes 262176 | tf_op jit(solution)/shard_map/ppermute | solution.py:330
  79.8 1.2 %collective-permute-done.17.got_ref = bf16[512,256]{1,0:T(8,128)(2,1)S(1)} collective-permute-done((bf16[512,256]{1,0:T(8,128)(2,1)S(1)}, bf16[512,256]{1,0:T(8,128)(2,1)S(1)}, u32[]{:S(2)}, u32[]{:S(2)}) %collective-permute-start.17) | collective-permute-done | bytes 262176 | tf_op jit(solution)/shard_map/ppermute | solution.py:330
  80.9 4.3 %collective-permute-done.18.refs_0_ = bf16[512,256]{1,0:T(8,128)(2,1)S(1)} collective-permute-done((bf16[512,256]{1,0:T(8,128)(2,1)S(1)}, bf16[512,256]{1,0:T(8,128)(2,1)S(1)}, u32[]{:S(2)}, u32[]{:S(2)}) %collective-permute-start.18) | collective-permute-done | bytes 262176 | tf_op jit(solution)/shard_map/ppermute | solution.py:330
  85.2 0.9 %add_second.9 = f32[512,256]{1,0:T(8,128)} custom-call(f32[512,256]{1,0:T(8,128)S(1)} %add_second.8.low_ref, bf16[512,256]{1,0:T(8,128)(2,1)S(1)} %collective-permute-done.17.got_ref, bf16[512,256]{1,0:T(8,128)(2,1)S(1)} %collective-permute-done.18.refs_0_), custom_call_target="tpu_custom_call" | custom-call | flops 1 | bytes 1 | tf_op jit(solution)/shard_map/add_second/pallas_call | solution.py:303
  (29 shorter events, 0.2 us)
Async XLA Ops:
  0.0 20.5 %collective-permute-start.6 = (bf16[2048,2048]{1,0:T(8,128)(2,1)}, bf16[2048,2048]{1,0:T(8,128)(2,1)}, u32[]{:S(2)}, u32[]{:S(2)}) collective-permute-start(bf16[2048,2048]{1,0:T(8,128)(2,1)} %psi_ref.1), channel_id=1, source_target_pairs={{0,8},{8,0},{16,24},{24,16},{1,9},{9,1},{17,25},{25,17},{2,10},{10... | collective-permute-start | bytes 25165832 | tf_op jit(solution)/shard_map/ppermute | solution.py:322
  2.0 12.2 %copy-start.7 = (s32[8]{0:T(128)S(1)}, s32[8]{0:T(128)}, u32[]{:S(2)}) copy-start(s32[8]{0:T(128)} %get-tuple-element.35) | copy-start | bytes 100
  2.1 12.4 %copy-start = (bf16[2048,2048]{1,0:T(8,128)(2,1)S(1)}, bf16[2048,2048]{1,0:T(8,128)(2,1)}, u32[]{:S(2)}) copy-start(bf16[2048,2048]{1,0:T(8,128)(2,1)} %psi_ref.1) | copy-start | bytes 25165828
  2.1 12.4 %copy-start.3 = (s32[2]{0:T(128)S(1)}, s32[2]{0:T(128)}, u32[]{:S(2)}) copy-start(s32[2]{0:T(128)} %get-tuple-element.33.spot_ref) | copy-start | bytes 28
  11.3 8.5 %collective-permute-start.1 = (bf16[8,128,128]{2,1,0:T(8,128)(2,1)}, bf16[8,128,128]{2,1,0:T(8,128)(2,1)S(1)}, u32[]{:S(2)}, u32[]{:S(2)}) collective-permute-start(bf16[8,128,128]{2,1,0:T(8,128)(2,1)} %get-tuple-element.38), channel_id=1, source_target_pairs={{0,8},{8,0},{16,24},{24,16},{1,9},{9,1},{17,25},{25,17},{2,10},{10... | collective-permute-start | bytes 786440 | tf_op jit(solution)/shard_map/ppermute | solution.py:322
  11.3 15.3 %collective-permute-start.4 = (bf16[8,128,128]{2,1,0:T(8,128)(2,1)}, bf16[8,128,128]{2,1,0:T(8,128)(2,1)S(1)}, u32[]{:S(2)}, u32[]{:S(2)}) collective-permute-start(bf16[8,128,128]{2,1,0:T(8,128)(2,1)} %get-tuple-element.41), channel_id=1, source_target_pairs={{0,16},{8,24},{16,0},{24,8},{1,17},{9,25},{17,1},{25,9},{2,18},{10... | collective-permute-start | bytes 786440 | tf_op jit(solution)/shard_map/ppermute | solution.py:322
  14.3 12.4 %collective-permute-start.5 = (bf16[8,128,128]{2,1,0:T(8,128)(2,1)}, bf16[8,128,128]{2,1,0:T(8,128)(2,1)S(1)}, u32[]{:S(2)}, u32[]{:S(2)}) collective-permute-start(bf16[8,128,128]{2,1,0:T(8,128)(2,1)} %get-tuple-element.42), channel_id=1, source_target_pairs={{0,24},{8,16},{16,8},{24,0},{1,25},{9,17},{17,9},{25,1},{2,26},{10... | collective-permute-start | bytes 786440 | tf_op jit(solution)/shard_map/ppermute | solution.py:322
  14.3 3.4 %collective-permute-start = (s32[8]{0:T(128)S(1)}, s32[8]{0:T(128)S(1)}, u32[]{:S(2)}, u32[]{:S(2)}) collective-permute-start(s32[8]{0:T(128)S(1)} %copy-done.7), channel_id=1, source_target_pairs={{0,8},{8,0},{16,24},{24,16},{1,9},{9,1},{17,25},{25,17},{2,10},{10... | collective-permute-start | bytes 104 | tf_op jit(solution)/shard_map/ppermute | solution.py:322
  14.4 3.3 %copy-start.6 = (s32[8]{0:T(128)S(1)}, s32[8]{0:T(128)}, u32[]{:S(2)}) copy-start(s32[8]{0:T(128)} %get-tuple-element.39) | copy-start | bytes 100
  14.4 5.3 %copy-start.5 = (s32[8]{0:T(128)S(1)}, s32[8]{0:T(128)}, u32[]{:S(2)}) copy-start(s32[8]{0:T(128)} %get-tuple-element.40) | copy-start | bytes 100
  14.4 5.3 %copy-start.1 = (f32[16,128,128]{2,1,0:T(8,128)S(1)}, f32[16,128,128]{2,1,0:T(8,128)}, u32[]{:S(2)}) copy-start(f32[16,128,128]{2,1,0:T(8,128)} %base_ref.1) | copy-start | bytes 3145732
  14.5 5.3 %copy-start.2 = (bf16[8,128,128]{2,1,0:T(8,128)(2,1)S(1)}, bf16[8,128,128]{2,1,0:T(8,128)(2,1)}, u32[]{:S(2)}) copy-start(bf16[8,128,128]{2,1,0:T(8,128)(2,1)} %get-tuple-element.37.own_ref) | copy-start | bytes 786436
  14.5 5.3 %copy-start.4 = (s32[8]{0:T(128)S(1)}, s32[8]{0:T(128)}, u32[]{:S(2)}) copy-start(s32[8]{0:T(128)} %get-tuple-element.34.own_at) | copy-start | bytes 100
  17.7 8.9 %collective-permute-start.2 = (s32[8]{0:T(128)S(1)}, s32[8]{0:T(128)S(1)}, u32[]{:S(2)}, u32[]{:S(2)}) collective-permute-start(s32[8]{0:T(128)S(1)} %copy-done.6), channel_id=1, source_target_pairs={{0,16},{8,24},{16,0},{24,8},{1,17},{9,25},{17,1},{25,9},{2,18},{10... | collective-permute-start | bytes 104 | tf_op jit(solution)/shard_map/ppermute | solution.py:322
  19.8 6.9 %collective-permute-start.3 = (s32[8]{0:T(128)S(1)}, s32[8]{0:T(128)S(1)}, u32[]{:S(2)}, u32[]{:S(2)}) collective-permute-start(s32[8]{0:T(128)S(1)} %copy-done.5), channel_id=1, source_target_pairs={{0,24},{8,16},{16,8},{24,0},{1,25},{9,17},{17,9},{25,1},{2,26},{10... | collective-permute-start | bytes 104 | tf_op jit(solution)/shard_map/ppermute | solution.py:322
  27.4 3.2 %collective-permute-start.7 = (bf16[16,128,128]{2,1,0:T(8,128)(2,1)S(1)}, bf16[16,128,128]{2,1,0:T(8,128)(2,1)S(1)}, u32[]{:S(2)}, u32[]{:S(2)}) collective-permute-start(bf16[16,128,128]{2,1,0:T(8,128)(2,1)S(1)} %far.1.mass_ref), channel_id=1, source_target_pairs={{0,8},{8,0},{16,24},{24,16},{1,9},{9,1},{17,25},{25,17},{2,10},{10... | collective-permute-start | bytes 1572872 | tf_op jit(solution)/shard_map/ppermute | solution.py:322
  33.7 10.4 %collective-permute-start.9 = (bf16[2,512,256]{2,1,0:T(8,128)(2,1)S(1)}, bf16[2,512,256]{2,1,0:T(8,128)(2,1)S(1)}, u32[]{:S(2)}, u32[]{:S(2)}) collective-permute-start(bf16[2,512,256]{2,1,0:T(8,128)(2,1)S(1)} %product.7.refs_4_), channel_id=1, source_target_pairs={{0,16},{1,17},{2,18},{3,19},{4,20},{5,21},{6,22},{7,23},{8,9},{9,8... | collective-permute-start | bytes 1572872 | tf_op jit(solution)/shard_map/ppermute | solution.py:330
  43.8 11.7 %collective-permute-start.8 = (bf16[2,512,256]{2,1,0:T(8,128)(2,1)S(1)}, bf16[2,512,256]{2,1,0:T(8,128)(2,1)S(1)}, u32[]{:S(2)}, u32[]{:S(2)}) collective-permute-start(bf16[2,512,256]{2,1,0:T(8,128)(2,1)S(1)} %get-tuple-element.48), channel_id=1, source_target_pairs={{0,16},{1,17},{2,18},{3,19},{4,20},{5,21},{6,22},{7,23},{8,9},{9,8... | collective-permute-start | bytes 1572872 | tf_op jit(solution)/shard_map/ppermute | solution.py:330
  44.3 9.3 %collective-permute-start.10 = (bf16[512,256]{1,0:T(8,128)(2,1)S(1)}, bf16[512,256]{1,0:T(8,128)(2,1)S(1)}, u32[]{:S(2)}, u32[]{:S(2)}) collective-permute-start(bf16[512,256]{1,0:T(8,128)(2,1)S(1)} %get-tuple-element.50), channel_id=1, source_target_pairs={{0,1},{1,0},{2,3},{3,2},{4,5},{5,4},{6,7},{7,6},{8,24},{9,25},{10,... | collective-permute-start | bytes 786440 | tf_op jit(solution)/shard_map/ppermute | solution.py:330
  51.2 12.7 %collective-permute-start.12 = (bf16[2,512,256]{2,1,0:T(8,128)(2,1)S(1)}, bf16[2,512,256]{2,1,0:T(8,128)(2,1)S(1)}, u32[]{:S(2)}, u32[]{:S(2)}) collective-permute-start(bf16[2,512,256]{2,1,0:T(8,128)(2,1)S(1)} %get-tuple-element.55), channel_id=1, source_target_pairs={{0,16},{1,17},{2,18},{3,19},{4,20},{5,21},{6,22},{7,23},{8,9},{9,8... | collective-permute-start | bytes 1572872 | tf_op jit(solution)/shard_map/ppermute | solution.py:330
  53.6 10.3 %collective-permute-start.14 = (bf16[512,256]{1,0:T(8,128)(2,1)S(1)}, bf16[512,256]{1,0:T(8,128)(2,1)S(1)}, u32[]{:S(2)}, u32[]{:S(2)}) collective-permute-start(bf16[512,256]{1,0:T(8,128)(2,1)S(1)} %add_second.5.refs_0_), channel_id=1, source_target_pairs={{0,2},{1,3},{2,0},{3,1},{4,6},{5,7},{6,4},{7,5},{8,10},{9,11},{10,... | collective-permute-start | bytes 786440 | tf_op jit(solution)/shard_map/ppermute | solution.py:330
  55.6 8.3 %collective-permute-start.13 = (bf16[512,256]{1,0:T(8,128)(2,1)S(1)}, bf16[512,256]{1,0:T(8,128)(2,1)S(1)}, u32[]{:S(2)}, u32[]{:S(2)}) collective-permute-start(bf16[512,256]{1,0:T(8,128)(2,1)S(1)} %get-tuple-element.56), channel_id=1, source_target_pairs={{0,1},{1,0},{2,3},{3,2},{4,5},{5,4},{6,7},{7,6},{8,24},{9,25},{10,... | collective-permute-start | bytes 786440 | tf_op jit(solution)/shard_map/ppermute | solution.py:330
  62.3 12.1 %collective-permute-start.11 = (bf16[2,512,256]{2,1,0:T(8,128)(2,1)S(1)}, bf16[2,512,256]{2,1,0:T(8,128)(2,1)S(1)}, u32[]{:S(2)}, u32[]{:S(2)}) collective-permute-start(bf16[2,512,256]{2,1,0:T(8,128)(2,1)S(1)} %get-tuple-element.53), channel_id=1, source_target_pairs={{0,16},{1,17},{2,18},{3,19},{4,20},{5,21},{6,22},{7,23},{8,9},{9,8... | collective-permute-start | bytes 1572872 | tf_op jit(solution)/shard_map/ppermute | solution.py:330
  64.1 8.7 %collective-permute-start.15 = (bf16[512,256]{1,0:T(8,128)(2,1)S(1)}, bf16[512,256]{1,0:T(8,128)(2,1)S(1)}, u32[]{:S(2)}, u32[]{:S(2)}) collective-permute-start(bf16[512,256]{1,0:T(8,128)(2,1)S(1)} %get-tuple-element.58), channel_id=1, source_target_pairs={{0,1},{1,0},{2,3},{3,2},{4,5},{5,4},{6,7},{7,6},{8,24},{9,25},{10,... | collective-permute-start | bytes 786440 | tf_op jit(solution)/shard_map/ppermute | solution.py:330
  65.7 14.1 %collective-permute-start.16 = (bf16[512,256]{1,0:T(8,128)(2,1)S(1)}, bf16[512,256]{1,0:T(8,128)(2,1)S(1)}, u32[]{:S(2)}, u32[]{:S(2)}) collective-permute-start(bf16[512,256]{1,0:T(8,128)(2,1)S(1)} %add_second.6.refs_0_), channel_id=1, source_target_pairs={{0,4},{1,5},{2,6},{3,7},{4,0},{5,1},{6,2},{7,3},{8,12},{9,13},{10,... | collective-permute-start | bytes 786440 | tf_op jit(solution)/shard_map/ppermute | solution.py:330
  74.5 6.4 %collective-permute-start.17 = (bf16[512,256]{1,0:T(8,128)(2,1)S(1)}, bf16[512,256]{1,0:T(8,128)(2,1)S(1)}, u32[]{:S(2)}, u32[]{:S(2)}) collective-permute-start(bf16[512,256]{1,0:T(8,128)(2,1)S(1)} %get-tuple-element.60), channel_id=1, source_target_pairs={{0,1},{1,0},{2,3},{3,2},{4,5},{5,4},{6,7},{7,6},{8,24},{9,25},{10,... | collective-permute-start | bytes 786440 | tf_op jit(solution)/shard_map/ppermute | solution.py:330
  75.0 10.2 %collective-permute-start.18 = (bf16[512,256]{1,0:T(8,128)(2,1)S(1)}, bf16[512,256]{1,0:T(8,128)(2,1)S(1)}, u32[]{:S(2)}, u32[]{:S(2)}) collective-permute-start(bf16[512,256]{1,0:T(8,128)(2,1)S(1)} %add_second.7.refs_0_), channel_id=1, source_target_pairs={{0,2},{1,3},{2,0},{3,1},{4,6},{5,7},{6,4},{7,5},{8,10},{9,11},{10,... | collective-permute-start | bytes 786440 | tf_op jit(solution)/shard_map/ppermute | solution.py:330

commit v4 on v3

--- a/solution.py
+++ b/solution.py
@@ -359,34 +359,29 @@
     left_other = make_left(mass_other, other_t)
     lefts, psis = [left, left_other], [own, other]
 
-    keep, first, second, third = {}, {}, {}, []
+    keep, first, second, third = {}, {}, {}, {}
     tails = {c: [] for c in chunks}
     last = len(chunks) - 1
-    for i in range(last + 2):
-        if i == 0:
-            go, = product(
-                chunks[0], spot, [left_other], [other], band, tile, go=jnp.bfloat16, acc=head
-            )
-            keep[0], = product(
-                chunks[0], spot, lefts, psis, band, tile, keep=True, behind=[go]
-            )
-            first[0] = swap_first(go)
-        elif i <= last:
-            behind = [keep[0]] if i == 1 else [second[i - 2][0]]
-            go, keep[i] = product(
-                chunks[i], spot, lefts, psis, band, tile, go=jnp.bfloat16, keep=True,
-                behind=behind,
-            )
-            first[i] = swap_first(go)
-        if i > 1:
-            chunk = chunks[i - 2]
-            third.append(add_second(*second[i - 2], jnp.bfloat16, tails[chunk]))
-            tails[goes_to[chunk]].append(swap_third(third[-1], chunk))
+    common = spot, lefts, psis, band, tile
+    go, = product(
+        chunks[0], spot, [left_other], [other], band, tile, go=jnp.bfloat16, acc=head
+    )
+    for i in range(last + 1):
+        first[i] = swap_first(go)
+        if i < last:
+            behind = [second[i - 1][0]] if i else [go]
+            go, = product(chunks[i + 1], *common, go=jnp.bfloat16, behind=behind)
+        behind = [go] + ([third[i - 2]] if i - 2 in third else [])
+        keep[i], = product(chunks[i], *common, keep=True, behind=behind)
+        behind = [third[i - 2]] if 0 and i > 1 else []
+        low, move = add_first(keep[i], first[i], behind)
+        second[i] = low, swap_second(move)
         if i:
-            low, go = add_first(keep[i - 1], first[i - 1], third[i - 2:])
-            second[i - 1] = low, swap_second(go)
+            chunk = chunks[i - 1]
+            third[i - 1] = add_second(*second[i - 1], jnp.bfloat16, tails[chunk])
+            tails[goes_to[chunk]].append(swap_third(third[i - 1], chunk))
     low, got = second[last]
-    early, late = tails[chunks[-1]][:-1], tails[chunks[-1]][-1:]
+    early, late = tails[chunks[-1]], []
     if early:
         low = add_second(low, early[0], jnp.float32, early[1:])
     return add_second(low, got, jnp.float32, late)

time: 86.3 us -> 80.7 us (0.935)
  waiting for transfers between devices: 17.3 us -> 10.7 us
  Pallas kernels: 45.7 us -> 47.9 us
  starting transfers between devices: 22.8 us -> 21.3 us
    ppermute x11, waiting for transfers between devices: 15.3 us -> 8.74 us  [swap(): return lax.ppermute(v, ('sub', 'tile'), pairs)]
    pallas_call x6 -> x9, Pallas kernels: 22.2 us -> 24.3 us  [product(): pl.pallas_call(functools.partial(product_kernel, chunk, len(lefts), bool(...]
    ppermute x11, starting transfers between devices: 17 us -> 15.5 us  [swap(): return lax.ppermute(v, ('sub', 'tile'), pairs)]
  transfers between devices with their start and end apart: 19 -> 19, of which waited for: 7 -> 6; matrix products, arithmetic and copies ran while one was open for 0% -> 0% of each run, Pallas kernels for 48% -> 54%
where the time goes in v4:
time: 80.7 us; the launch traced here: 80.2 us
  Pallas kernels  47.9 us (59%)
  starting transfers between devices  21.3 us (26%)
  waiting for transfers between devices  10.7 us (13%)
    pallas_call x9, Pallas kernels, product(): pl.pallas_call(functools.partial(product_kernel, chunk, len(lefts), bool(...  24.3 us
    ppermute x11, starting transfers between devices, swap(): return lax.ppermute(v, ('sub', 'tile'), pairs)  15.5 us
    pallas_call x1, Pallas kernels, make_contrib(): pl.pallas_call(contrib_kernel, grid=(subs,), in_specs=[SMEM, SMEM, pl.Blo...  9.2 us
    ppermute x11, waiting for transfers between devices, swap(): return lax.ppermute(v, ('sub', 'tile'), pairs)  8.74 us
    pallas_call x2, Pallas kernels, turn(): pl.pallas_call(turn_kernel, in_specs=[SMEM, ANY], out_specs=[VMEM, VMEM],...  7.29 us
    ppermute x8, starting transfers between devices, swap_sub(): return lax.ppermute(v, 'sub', [(i, i ^ d) for i in range(n_sub)])  5.73 us
    pallas_call x2, Pallas kernels, make_left(): pl.pallas_call(left_kernel, in_specs=[VMEM, VMEM], out_specs=VMEM, out_sh...  2.52 us
    ppermute x8, waiting for transfers between devices, swap_sub(): return lax.ppermute(v, 'sub', [(i, i ^ d) for i in range(n_sub)])  1.98 us
  transfers between devices with their start and end apart: 19, of which 6 were waited for; matrix products, arithmetic and copies ran while one was open for 0% of the time, Pallas kernels for 54%

profile of v4, /device:TPU:0, one launch (start us, length us, event | category | flops | bytes accessed | tf_op | source)
XLA Modules:
  0.0 80.2 jit_solution(9571304912258321344)
XLA Ops:
  0.0 0.5 collective-permute-start.6
  0.5 1.6 %prep.1 = (s32[2]{0:T(128)}, s32[4,8]{1,0:T(4,128)}, s32[8]{0:T(128)}, s32[8]{0:T(128)}, s32[8]{0:T(128)}, /*index=5*/s32[8]{0:T(128)}) custom-call(s32[4,8]{1,0:T(4,128)} %adj_ref.1), custom_call_target="tpu_custom_call" | custom-call | flops 1 | bytes 1 | tf_op jit(solution)/shard_map/prep/pallas_call | solution.py:53
  2.1 0.0 copy-start
  2.1 9.2 %contrib.1 = (bf16[8,128,128]{2,1,0:T(8,128)(2,1)}, bf16[8,128,128]{2,1,0:T(8,128)(2,1)}, bf16[8,128,128]{2,1,0:T(8,128)(2,1)}, bf16[8,128,128]{2,1,0:T(8,128)(2,1)}) custom-call(s32[4]{0:T(128)} %rows_ref.1, s32[4,8]{1,0:T(4,128)} %get-tuple-element.30.dest_ref, bf16[4,768,512]{2,1,0:T(8,128)(2,1)} %modes_ref.1, bf16[4,8,768,128]{3,2,1,0:T(8,128)(2,1)} %coup_ref.1, ...), custom_call_target="tpu_custom_call" | custom-call | flops 1 | bytes 1 | tf_op jit(solution)/shard_map/contrib/pallas_call | solution.py:97
  11.3 0.1 collective-permute-start.1
  11.3 2.9 %collective-permute-start.4 = (bf16[8,128,128]{2,1,0:T(8,128)(2,1)}, bf16[8,128,128]{2,1,0:T(8,128)(2,1)S(1)}, u32[]{:S(2)}, u32[]{:S(2)}) collective-permute-start(bf16[8,128,128]{2,1,0:T(8,128)(2,1)} %get-tuple-element.35), channel_id=1, source_target_pairs={{0,16},{8,24},{16,0},{24,8},{1,17},{9,25},{17,1},{25,9},{2,18},{10... | collective-permute-start | bytes 786440 | tf_op jit(solution)/shard_map/ppermute | solution.py:322
  14.3 0.1 collective-permute-start
  14.5 3.2 %turn.2 = (bf16[2,512,2048]{2,1,0:T(8,128)(2,1)S(1)}, bf16[2048,2048]{1,0:T(8,128)(2,1)S(1)}) custom-call(s32[2]{0:T(128)S(1)} %copy-done.3, bf16[2048,2048]{1,0:T(8,128)(2,1)S(1)} %copy-done), custom_call_target="tpu_custom_call" | custom-call | flops 1 | bytes 1 | tf_op jit(solution)/shard_map/turn/pallas_call | solution.py:181
  17.7 2.1 %collective-permute-start.2 = (s32[8]{0:T(128)S(1)}, s32[8]{0:T(128)S(1)}, u32[]{:S(2)}, u32[]{:S(2)}) collective-permute-start(s32[8]{0:T(128)S(1)} %copy-done.6), channel_id=1, source_target_pairs={{0,16},{8,24},{16,0},{24,8},{1,17},{9,25},{17,1},{25,9},{2,18},{10... | collective-permute-start | bytes 104 | tf_op jit(solution)/shard_map/ppermute | solution.py:322
  19.8 0.7 near.1.near_ref
  20.6 4.1 %turn.3 = (bf16[2,512,2048]{2,1,0:T(8,128)(2,1)S(1)}, bf16[2048,2048]{1,0:T(8,128)(2,1)S(1)}) custom-call(s32[2]{0:T(128)S(1)} %copy-done.3, bf16[2048,2048]{1,0:T(8,128)(2,1)} %collective-permute-done.6.psi_ref), custom_call_target="tpu_custom_call" | custom-call | flops 1 | bytes 1 | tf_op jit(solution)/shard_map/turn/pallas_call | solution.py:181
  24.7 2.0 %collective-permute-done.2.rest_0_ = s32[8]{0:T(128)S(1)} collective-permute-done((s32[8]{0:T(128)S(1)}, s32[8]{0:T(128)S(1)}, u32[]{:S(2)}, u32[]{:S(2)}) %collective-permute-start.2) | collective-permute-done | bytes 64 | tf_op jit(solution)/shard_map/ppermute | solution.py:322
  26.6 0.8 far.1.mass_ref
  27.4 0.1 collective-permute-start.7
  27.5 1.3 %left.2.refs_0_ = bf16[1024,2048]{1,0:T(8,128)(2,1)S(1)} custom-call(bf16[16,128,128]{2,1,0:T(8,128)(2,1)S(1)} %far.1.mass_ref, bf16[2,512,2048]{2,1,0:T(8,128)(2,1)S(1)} %get-tuple-element.37.rest_4_.turned_ref), custom_call_target="tpu_custom_call" | custom-call | flops 1 | bytes 1 | tf_op jit(solution)/shard_map/left/pallas_call | solution.py:216
  28.8 1.8 %product.9.refs_2_ = f32[2,512,256]{2,1,0:T(8,128)S(1)} custom-call(s32[2]{0:T(128)S(1)} %copy-done.3, bf16[1024,2048]{1,0:T(8,128)(2,1)S(1)} %left.2.refs_0_, bf16[2048,2048]{1,0:T(8,128)(2,1)S(1)} %get-tuple-element.39.refs_1_.refs_2_), custom_call_target="tpu_custom_call" | custom-call | flops 1073741824 | bytes 2097152 | tf_op jit(solution)/shard_map/product/pallas_call | solution.py:261
  30.6 1.3 %left.3.refs_0_.refs_1_ = bf16[1024,2048]{1,0:T(8,128)(2,1)S(1)} custom-call(bf16[16,128,128]{2,1,0:T(8,128)(2,1)S(1)} %collective-permute-done.7.mass_ref, bf16[2,512,2048]{2,1,0:T(8,128)(2,1)S(1)} %get-tuple-element.38.rest_5_.turned_ref), custom_call_target="tpu_custom_call" | custom-call | flops 1 | bytes 1 | tf_op jit(solution)/shard_map/left/pallas_call | solution.py:216
  31.9 1.8 %product.10.refs_4_ = bf16[2,512,256]{2,1,0:T(8,128)(2,1)S(1)} custom-call(s32[2]{0:T(128)S(1)} %copy-done.3, bf16[1024,2048]{1,0:T(8,128)(2,1)S(1)} %left.3.refs_0_.refs_1_, bf16[2048,2048]{1,0:T(8,128)(2,1)S(1)} %get-tuple-element.40.refs_1_.refs_3_, f32[2,512,256]{2,1,0:T(8,128)S(1)} %product.9.refs_2_), custom_call_target="tpu_custom_call" | custom-call | flops 1073741824 | bytes 2097152 | tf_op jit(solution)/shard_map/product/pallas_call | solution.py:261
  33.7 1.8 %collective-permute-start.8 = (bf16[2,512,256]{2,1,0:T(8,128)(2,1)S(1)}, bf16[2,512,256]{2,1,0:T(8,128)(2,1)S(1)}, u32[]{:S(2)}, u32[]{:S(2)}) collective-permute-start(bf16[2,512,256]{2,1,0:T(8,128)(2,1)S(1)} %product.10.refs_4_), channel_id=1, source_target_pairs={{0,16},{1,17},{2,18},{3,19},{4,20},{5,21},{6,22},{7,23},{8,9},{9,8... | collective-permute-start | bytes 1572872 | tf_op jit(solution)/shard_map/ppermute | solution.py:330
  35.6 2.9 %product.11.refs_4_ = bf16[2,512,256]{2,1,0:T(8,128)(2,1)S(1)} custom-call(s32[2]{0:T(128)S(1)} %copy-done.3, bf16[1024,2048]{1,0:T(8,128)(2,1)S(1)} %left.2.refs_0_, bf16[1024,2048]{1,0:T(8,128)(2,1)S(1)} %left.3.refs_0_.refs_1_, bf16[2048,2048]{1,0:T(8,128)(2,1)S(1)} %get-tuple-element.39.refs_1_.refs_2_, ...), custom_call_target="tpu_custom_call" | custom-call | flops 2147483648 | bytes 4194304 | tf_op jit(solution)/shard_map/product/pallas_call | solution.py:261
  38.5 0.3 collective-permute-start.9
  38.8 2.9 %product.12.keep_ref = f32[2,512,256]{2,1,0:T(8,128)S(1)} custom-call(s32[2]{0:T(128)S(1)} %copy-done.3, bf16[1024,2048]{1,0:T(8,128)(2,1)S(1)} %left.2.refs_0_, bf16[1024,2048]{1,0:T(8,128)(2,1)S(1)} %left.3.refs_0_.refs_1_, bf16[2048,2048]{1,0:T(8,128)(2,1)S(1)} %get-tuple-element.39.refs_1_.refs_2_, ...), custom_call_target="tpu_custom_call" | custom-call | flops 2147483648 | bytes 4194304 | tf_op jit(solution)/shard_map/product/pallas_call | solution.py:261
  41.7 1.2 %collective-permute-done.8.got_ref = bf16[2,512,256]{2,1,0:T(8,128)(2,1)S(1)} collective-permute-done((bf16[2,512,256]{2,1,0:T(8,128)(2,1)S(1)}, bf16[2,512,256]{2,1,0:T(8,128)(2,1)S(1)}, u32[]{:S(2)}, u32[]{:S(2)}) %collective-permute-start.8) | collective-permute-done | bytes 524320 | tf_op jit(solution)/shard_map/ppermute | solution.py:330
  43.0 0.1 add_first.4
  43.1 1.8 %collective-permute-start.11 = (bf16[512,256]{1,0:T(8,128)(2,1)S(1)}, bf16[512,256]{1,0:T(8,128)(2,1)S(1)}, u32[]{:S(2)}, u32[]{:S(2)}) collective-permute-start(bf16[512,256]{1,0:T(8,128)(2,1)S(1)} %get-tuple-element.44), channel_id=1, source_target_pairs={{0,1},{1,0},{2,3},{3,2},{4,5},{5,4},{6,7},{7,6},{8,24},{9,25},{10,... | collective-permute-start | bytes 786440 | tf_op jit(solution)/shard_map/ppermute | solution.py:330
  44.9 3.2 %product.13.refs_4_ = bf16[2,512,256]{2,1,0:T(8,128)(2,1)S(1)} custom-call(s32[2]{0:T(128)S(1)} %copy-done.3, bf16[1024,2048]{1,0:T(8,128)(2,1)S(1)} %left.2.refs_0_, bf16[1024,2048]{1,0:T(8,128)(2,1)S(1)} %left.3.refs_0_.refs_1_, bf16[2048,2048]{1,0:T(8,128)(2,1)S(1)} %get-tuple-element.39.refs_1_.refs_2_, ...), custom_call_target="tpu_custom_call" | custom-call | flops 2147483648 | bytes 4194304 | tf_op jit(solution)/shard_map/product/pallas_call | solution.py:261
  48.1 1.6 %collective-permute-start.15 = (bf16[2,512,256]{2,1,0:T(8,128)(2,1)S(1)}, bf16[2,512,256]{2,1,0:T(8,128)(2,1)S(1)}, u32[]{:S(2)}, u32[]{:S(2)}) collective-permute-start(bf16[2,512,256]{2,1,0:T(8,128)(2,1)S(1)} %product.13.refs_4_), channel_id=1, source_target_pairs={{0,16},{1,17},{2,18},{3,19},{4,20},{5,21},{6,22},{7,23},{8,9},{9,8... | collective-permute-start | bytes 1572872 | tf_op jit(solution)/shard_map/ppermute | solution.py:330
  49.6 2.9 %product.14.keep_ref = f32[2,512,256]{2,1,0:T(8,128)S(1)} custom-call(s32[2]{0:T(128)S(1)} %copy-done.3, bf16[1024,2048]{1,0:T(8,128)(2,1)S(1)} %left.2.refs_0_, bf16[1024,2048]{1,0:T(8,128)(2,1)S(1)} %left.3.refs_0_.refs_1_, bf16[2048,2048]{1,0:T(8,128)(2,1)S(1)} %get-tuple-element.39.refs_1_.refs_2_, ...), custom_call_target="tpu_custom_call" | custom-call | flops 2147483648 | bytes 4194304 | tf_op jit(solution)/shard_map/product/pallas_call | solution.py:261
  52.6 0.1 add_first.5
  52.7 2.9 %product.15.refs_4_ = bf16[2,512,256]{2,1,0:T(8,128)(2,1)S(1)} custom-call(s32[2]{0:T(128)S(1)} %copy-done.3, bf16[1024,2048]{1,0:T(8,128)(2,1)S(1)} %left.2.refs_0_, bf16[1024,2048]{1,0:T(8,128)(2,1)S(1)} %left.3.refs_0_.refs_1_, bf16[2048,2048]{1,0:T(8,128)(2,1)S(1)} %get-tuple-element.39.refs_1_.refs_2_, ...), custom_call_target="tpu_custom_call" | custom-call | flops 2147483648 | bytes 4194304 | tf_op jit(solution)/shard_map/product/pallas_call | solution.py:261
  55.6 0.7 collective-permute-start.13
  56.2 1.5 %collective-permute-start.10 = (bf16[512,256]{1,0:T(8,128)(2,1)S(1)}, bf16[512,256]{1,0:T(8,128)(2,1)S(1)}, u32[]{:S(2)}, u32[]{:S(2)}) collective-permute-start(bf16[512,256]{1,0:T(8,128)(2,1)S(1)} %get-tuple-element.43), channel_id=1, source_target_pairs={{0,1},{1,0},{2,3},{3,2},{4,5},{5,4},{6,7},{7,6},{8,24},{9,25},{10,... | collective-permute-start | bytes 786440 | tf_op jit(solution)/shard_map/ppermute | solution.py:330
  57.8 1.7 %collective-permute-start.12 = (bf16[512,256]{1,0:T(8,128)(2,1)S(1)}, bf16[512,256]{1,0:T(8,128)(2,1)S(1)}, u32[]{:S(2)}, u32[]{:S(2)}) collective-permute-start(bf16[512,256]{1,0:T(8,128)(2,1)S(1)} %add_second.5.refs_5_), channel_id=1, source_target_pairs={{0,2},{1,3},{2,0},{3,1},{4,6},{5,7},{6,4},{7,5},{8,10},{9,11},{10,... | collective-permute-start | bytes 786440 | tf_op jit(solution)/shard_map/ppermute | solution.py:330
  59.5 2.9 %product.17.keep_ref = f32[2,512,256]{2,1,0:T(8,128)S(1)} custom-call(s32[2]{0:T(128)S(1)} %copy-done.3, bf16[1024,2048]{1,0:T(8,128)(2,1)S(1)} %left.2.refs_0_, bf16[1024,2048]{1,0:T(8,128)(2,1)S(1)} %left.3.refs_0_.refs_1_, bf16[2048,2048]{1,0:T(8,128)(2,1)S(1)} %get-tuple-element.39.refs_1_.refs_2_, ...), custom_call_target="tpu_custom_call" | custom-call | flops 2147483648 | bytes 4194304 | tf_op jit(solution)/shard_map/product/pallas_call | solution.py:261
  62.4 0.1 add_first.7
  62.5 0.6 collective-permute-start.16
  63.1 2.4 %collective-permute-done.10.got_ref = bf16[512,256]{1,0:T(8,128)(2,1)S(1)} collective-permute-done((bf16[512,256]{1,0:T(8,128)(2,1)S(1)}, bf16[512,256]{1,0:T(8,128)(2,1)S(1)}, u32[]{:S(2)}, u32[]{:S(2)}) %collective-permute-start.10) | collective-permute-done | bytes 262176 | tf_op jit(solution)/shard_map/ppermute | solution.py:330
  65.5 0.1 add_second.6.refs_5_
  65.6 2.6 %collective-permute-start.14 = (bf16[512,256]{1,0:T(8,128)(2,1)S(1)}, bf16[512,256]{1,0:T(8,128)(2,1)S(1)}, u32[]{:S(2)}, u32[]{:S(2)}) collective-permute-start(bf16[512,256]{1,0:T(8,128)(2,1)S(1)} %add_second.6.refs_5_), channel_id=1, source_target_pairs={{0,4},{1,5},{2,6},{3,7},{4,0},{5,1},{6,2},{7,3},{8,12},{9,13},{10,... | collective-permute-start | bytes 786440 | tf_op jit(solution)/shard_map/ppermute | solution.py:330
  68.2 2.9 %product.16.keep_ref = f32[2,512,256]{2,1,0:T(8,128)S(1)} custom-call(s32[2]{0:T(128)S(1)} %copy-done.3, bf16[1024,2048]{1,0:T(8,128)(2,1)S(1)} %left.2.refs_0_, bf16[1024,2048]{1,0:T(8,128)(2,1)S(1)} %left.3.refs_0_.refs_1_, bf16[2048,2048]{1,0:T(8,128)(2,1)S(1)} %get-tuple-element.39.refs_1_.refs_2_, ...), custom_call_target="tpu_custom_call" | custom-call | flops 2147483648 | bytes 4194304 | tf_op jit(solution)/shard_map/product/pallas_call | solution.py:261
  71.2 1.7 %collective-permute-start.17 = (bf16[512,256]{1,0:T(8,128)(2,1)S(1)}, bf16[512,256]{1,0:T(8,128)(2,1)S(1)}, u32[]{:S(2)}, u32[]{:S(2)}) collective-permute-start(bf16[512,256]{1,0:T(8,128)(2,1)S(1)} %add_second.7), channel_id=1, source_target_pairs={{0,2},{1,3},{2,0},{3,1},{4,6},{5,7},{6,4},{7,5},{8,10},{9,11},{10,... | collective-permute-start | bytes 786440 | tf_op jit(solution)/shard_map/ppermute | solution.py:330
  72.9 0.1 add_first.6
  73.0 1.3 %collective-permute-start.18 = (bf16[512,256]{1,0:T(8,128)(2,1)S(1)}, bf16[512,256]{1,0:T(8,128)(2,1)S(1)}, u32[]{:S(2)}, u32[]{:S(2)}) collective-permute-start(bf16[512,256]{1,0:T(8,128)(2,1)S(1)} %get-tuple-element.48), channel_id=1, source_target_pairs={{0,1},{1,0},{2,3},{3,2},{4,5},{5,4},{6,7},{7,6},{8,24},{9,25},{10,... | collective-permute-start | bytes 786440 | tf_op jit(solution)/shard_map/ppermute | solution.py:330
  74.3 2.3 %collective-permute-done.14.got_ref = bf16[512,256]{1,0:T(8,128)(2,1)S(1)} collective-permute-done((bf16[512,256]{1,0:T(8,128)(2,1)S(1)}, bf16[512,256]{1,0:T(8,128)(2,1)S(1)}, u32[]{:S(2)}, u32[]{:S(2)}) %collective-permute-start.14) | collective-permute-done | bytes 262176 | tf_op jit(solution)/shard_map/ppermute | solution.py:330
  76.5 2.7 %collective-permute-done.17.refs_0_ = bf16[512,256]{1,0:T(8,128)(2,1)S(1)} collective-permute-done((bf16[512,256]{1,0:T(8,128)(2,1)S(1)}, bf16[512,256]{1,0:T(8,128)(2,1)S(1)}, u32[]{:S(2)}, u32[]{:S(2)}) %collective-permute-start.17) | collective-permute-done | bytes 262176 | tf_op jit(solution)/shard_map/ppermute | solution.py:330
  79.2 0.1 add_second.8.low_ref
  79.3 0.1 collective-permute-done.18.got_ref
  79.4 0.8 %add_second.9 = f32[512,256]{1,0:T(8,128)} custom-call(f32[512,256]{1,0:T(8,128)S(1)} %add_second.8.low_ref, bf16[512,256]{1,0:T(8,128)(2,1)S(1)} %collective-permute-done.18.got_ref), custom_call_target="tpu_custom_call" | custom-call | flops 1 | bytes 1 | tf_op jit(solution)/shard_map/add_second/pallas_call | solution.py:303
  (32 shorter events, 0.2 us)
Async XLA Ops:
  0.0 20.5 %collective-permute-start.6 = (bf16[2048,2048]{1,0:T(8,128)(2,1)}, bf16[2048,2048]{1,0:T(8,128)(2,1)}, u32[]{:S(2)}, u32[]{:S(2)}) collective-permute-start(bf16[2048,2048]{1,0:T(8,128)(2,1)} %psi_ref.1), channel_id=1, source_target_pairs={{0,8},{8,0},{16,24},{24,16},{1,9},{9,1},{17,25},{25,17},{2,10},{10... | collective-permute-start | bytes 25165832 | tf_op jit(solution)/shard_map/ppermute | solution.py:322
  2.0 12.2 %copy-start.7 = (s32[8]{0:T(128)S(1)}, s32[8]{0:T(128)}, u32[]{:S(2)}) copy-start(s32[8]{0:T(128)} %get-tuple-element.29) | copy-start | bytes 100
  2.1 12.4 %copy-start = (bf16[2048,2048]{1,0:T(8,128)(2,1)S(1)}, bf16[2048,2048]{1,0:T(8,128)(2,1)}, u32[]{:S(2)}) copy-start(bf16[2048,2048]{1,0:T(8,128)(2,1)} %psi_ref.1) | copy-start | bytes 25165828
  2.1 12.4 %copy-start.3 = (s32[2]{0:T(128)S(1)}, s32[2]{0:T(128)}, u32[]{:S(2)}) copy-start(s32[2]{0:T(128)} %get-tuple-element.27.spot_ref) | copy-start | bytes 28
  11.3 8.5 %collective-permute-start.1 = (bf16[8,128,128]{2,1,0:T(8,128)(2,1)}, bf16[8,128,128]{2,1,0:T(8,128)(2,1)S(1)}, u32[]{:S(2)}, u32[]{:S(2)}) collective-permute-start(bf16[8,128,128]{2,1,0:T(8,128)(2,1)} %get-tuple-element.32), channel_id=1, source_target_pairs={{0,8},{8,0},{16,24},{24,16},{1,9},{9,1},{17,25},{25,17},{2,10},{10... | collective-permute-start | bytes 786440 | tf_op jit(solution)/shard_map/ppermute | solution.py:322
  11.3 15.3 %collective-permute-start.4 = (bf16[8,128,128]{2,1,0:T(8,128)(2,1)}, bf16[8,128,128]{2,1,0:T(8,128)(2,1)S(1)}, u32[]{:S(2)}, u32[]{:S(2)}) collective-permute-start(bf16[8,128,128]{2,1,0:T(8,128)(2,1)} %get-tuple-element.35), channel_id=1, source_target_pairs={{0,16},{8,24},{16,0},{24,8},{1,17},{9,25},{17,1},{25,9},{2,18},{10... | collective-permute-start | bytes 786440 | tf_op jit(solution)/shard_map/ppermute | solution.py:322
  14.3 12.4 %collective-permute-start.5 = (bf16[8,128,128]{2,1,0:T(8,128)(2,1)}, bf16[8,128,128]{2,1,0:T(8,128)(2,1)S(1)}, u32[]{:S(2)}, u32[]{:S(2)}) collective-permute-start(bf16[8,128,128]{2,1,0:T(8,128)(2,1)} %get-tuple-element.36), channel_id=1, source_target_pairs={{0,24},{8,16},{16,8},{24,0},{1,25},{9,17},{17,9},{25,1},{2,26},{10... | collective-permute-start | bytes 786440 | tf_op jit(solution)/shard_map/ppermute | solution.py:322
  14.3 3.4 %collective-permute-start = (s32[8]{0:T(128)S(1)}, s32[8]{0:T(128)S(1)}, u32[]{:S(2)}, u32[]{:S(2)}) collective-permute-start(s32[8]{0:T(128)S(1)} %copy-done.7), channel_id=1, source_target_pairs={{0,8},{8,0},{16,24},{24,16},{1,9},{9,1},{17,25},{25,17},{2,10},{10... | collective-permute-start | bytes 104 | tf_op jit(solution)/shard_map/ppermute | solution.py:322
  14.4 3.3 %copy-start.6 = (s32[8]{0:T(128)S(1)}, s32[8]{0:T(128)}, u32[]{:S(2)}) copy-start(s32[8]{0:T(128)} %get-tuple-element.33) | copy-start | bytes 100
  14.4 5.3 %copy-start.5 = (s32[8]{0:T(128)S(1)}, s32[8]{0:T(128)}, u32[]{:S(2)}) copy-start(s32[8]{0:T(128)} %get-tuple-element.34) | copy-start | bytes 100
  14.4 5.3 %copy-start.1 = (f32[16,128,128]{2,1,0:T(8,128)S(1)}, f32[16,128,128]{2,1,0:T(8,128)}, u32[]{:S(2)}) copy-start(f32[16,128,128]{2,1,0:T(8,128)} %base_ref.1) | copy-start | bytes 3145732
  14.5 5.3 %copy-start.2 = (bf16[8,128,128]{2,1,0:T(8,128)(2,1)S(1)}, bf16[8,128,128]{2,1,0:T(8,128)(2,1)}, u32[]{:S(2)}) copy-start(bf16[8,128,128]{2,1,0:T(8,128)(2,1)} %get-tuple-element.31.own_ref) | copy-start | bytes 786436
  14.5 5.3 %copy-start.4 = (s32[8]{0:T(128)S(1)}, s32[8]{0:T(128)}, u32[]{:S(2)}) copy-start(s32[8]{0:T(128)} %get-tuple-element.28.own_at) | copy-start | bytes 100
  17.7 8.9 %collective-permute-start.2 = (s32[8]{0:T(128)S(1)}, s32[8]{0:T(128)S(1)}, u32[]{:S(2)}, u32[]{:S(2)}) collective-permute-start(s32[8]{0:T(128)S(1)} %copy-done.6), channel_id=1, source_target_pairs={{0,16},{8,24},{16,0},{24,8},{1,17},{9,25},{17,1},{25,9},{2,18},{10... | collective-permute-start | bytes 104 | tf_op jit(solution)/shard_map/ppermute | solution.py:322
  19.8 6.9 %collective-permute-start.3 = (s32[8]{0:T(128)S(1)}, s32[8]{0:T(128)S(1)}, u32[]{:S(2)}, u32[]{:S(2)}) collective-permute-start(s32[8]{0:T(128)S(1)} %copy-done.5), channel_id=1, source_target_pairs={{0,24},{8,16},{16,8},{24,0},{1,25},{9,17},{17,9},{25,1},{2,26},{10... | collective-permute-start | bytes 104 | tf_op jit(solution)/shard_map/ppermute | solution.py:322
  27.4 3.2 %collective-permute-start.7 = (bf16[16,128,128]{2,1,0:T(8,128)(2,1)S(1)}, bf16[16,128,128]{2,1,0:T(8,128)(2,1)S(1)}, u32[]{:S(2)}, u32[]{:S(2)}) collective-permute-start(bf16[16,128,128]{2,1,0:T(8,128)(2,1)S(1)} %far.1.mass_ref), channel_id=1, source_target_pairs={{0,8},{8,0},{16,24},{24,16},{1,9},{9,1},{17,25},{25,17},{2,10},{10... | collective-permute-start | bytes 1572872 | tf_op jit(solution)/shard_map/ppermute | solution.py:322
  33.7 9.2 %collective-permute-start.8 = (bf16[2,512,256]{2,1,0:T(8,128)(2,1)S(1)}, bf16[2,512,256]{2,1,0:T(8,128)(2,1)S(1)}, u32[]{:S(2)}, u32[]{:S(2)}) collective-permute-start(bf16[2,512,256]{2,1,0:T(8,128)(2,1)S(1)} %product.10.refs_4_), channel_id=1, source_target_pairs={{0,16},{1,17},{2,18},{3,19},{4,20},{5,21},{6,22},{7,23},{8,9},{9,8... | collective-permute-start | bytes 1572872 | tf_op jit(solution)/shard_map/ppermute | solution.py:330
  38.5 14.1 %collective-permute-start.9 = (bf16[2,512,256]{2,1,0:T(8,128)(2,1)S(1)}, bf16[2,512,256]{2,1,0:T(8,128)(2,1)S(1)}, u32[]{:S(2)}, u32[]{:S(2)}) collective-permute-start(bf16[2,512,256]{2,1,0:T(8,128)(2,1)S(1)} %product.11.refs_4_), channel_id=1, source_target_pairs={{0,16},{1,17},{2,18},{3,19},{4,20},{5,21},{6,22},{7,23},{8,9},{9,8... | collective-permute-start | bytes 1572872 | tf_op jit(solution)/shard_map/ppermute | solution.py:330
  43.1 14.7 %collective-permute-start.11 = (bf16[512,256]{1,0:T(8,128)(2,1)S(1)}, bf16[512,256]{1,0:T(8,128)(2,1)S(1)}, u32[]{:S(2)}, u32[]{:S(2)}) collective-permute-start(bf16[512,256]{1,0:T(8,128)(2,1)S(1)} %get-tuple-element.44), channel_id=1, source_target_pairs={{0,1},{1,0},{2,3},{3,2},{4,5},{5,4},{6,7},{7,6},{8,24},{9,25},{10,... | collective-permute-start | bytes 786440 | tf_op jit(solution)/shard_map/ppermute | solution.py:330
  48.1 14.3 %collective-permute-start.15 = (bf16[2,512,256]{2,1,0:T(8,128)(2,1)S(1)}, bf16[2,512,256]{2,1,0:T(8,128)(2,1)S(1)}, u32[]{:S(2)}, u32[]{:S(2)}) collective-permute-start(bf16[2,512,256]{2,1,0:T(8,128)(2,1)S(1)} %product.13.refs_4_), channel_id=1, source_target_pairs={{0,16},{1,17},{2,18},{3,19},{4,20},{5,21},{6,22},{7,23},{8,9},{9,8... | collective-permute-start | bytes 1572872 | tf_op jit(solution)/shard_map/ppermute | solution.py:330
  55.6 17.3 %collective-permute-start.13 = (bf16[2,512,256]{2,1,0:T(8,128)(2,1)S(1)}, bf16[2,512,256]{2,1,0:T(8,128)(2,1)S(1)}, u32[]{:S(2)}, u32[]{:S(2)}) collective-permute-start(bf16[2,512,256]{2,1,0:T(8,128)(2,1)S(1)} %product.15.refs_4_), channel_id=1, source_target_pairs={{0,16},{1,17},{2,18},{3,19},{4,20},{5,21},{6,22},{7,23},{8,9},{9,8... | collective-permute-start | bytes 1572872 | tf_op jit(solution)/shard_map/ppermute | solution.py:330
  56.2 9.2 %collective-permute-start.10 = (bf16[512,256]{1,0:T(8,128)(2,1)S(1)}, bf16[512,256]{1,0:T(8,128)(2,1)S(1)}, u32[]{:S(2)}, u32[]{:S(2)}) collective-permute-start(bf16[512,256]{1,0:T(8,128)(2,1)S(1)} %get-tuple-element.43), channel_id=1, source_target_pairs={{0,1},{1,0},{2,3},{3,2},{4,5},{5,4},{6,7},{7,6},{8,24},{9,25},{10,... | collective-permute-start | bytes 786440 | tf_op jit(solution)/shard_map/ppermute | solution.py:330
  57.8 7.7 %collective-permute-start.12 = (bf16[512,256]{1,0:T(8,128)(2,1)S(1)}, bf16[512,256]{1,0:T(8,128)(2,1)S(1)}, u32[]{:S(2)}, u32[]{:S(2)}) collective-permute-start(bf16[512,256]{1,0:T(8,128)(2,1)S(1)} %add_second.5.refs_5_), channel_id=1, source_target_pairs={{0,2},{1,3},{2,0},{3,1},{4,6},{5,7},{6,4},{7,5},{8,10},{9,11},{10,... | collective-permute-start | bytes 786440 | tf_op jit(solution)/shard_map/ppermute | solution.py:330
  62.5 8.6 %collective-permute-start.16 = (bf16[512,256]{1,0:T(8,128)(2,1)S(1)}, bf16[512,256]{1,0:T(8,128)(2,1)S(1)}, u32[]{:S(2)}, u32[]{:S(2)}) collective-permute-start(bf16[512,256]{1,0:T(8,128)(2,1)S(1)} %get-tuple-element.47), channel_id=1, source_target_pairs={{0,1},{1,0},{2,3},{3,2},{4,5},{5,4},{6,7},{7,6},{8,24},{9,25},{10,... | collective-permute-start | bytes 786440 | tf_op jit(solution)/shard_map/ppermute | solution.py:330
  65.6 11.0 %collective-permute-start.14 = (bf16[512,256]{1,0:T(8,128)(2,1)S(1)}, bf16[512,256]{1,0:T(8,128)(2,1)S(1)}, u32[]{:S(2)}, u32[]{:S(2)}) collective-permute-start(bf16[512,256]{1,0:T(8,128)(2,1)S(1)} %add_second.6.refs_5_), channel_id=1, source_target_pairs={{0,4},{1,5},{2,6},{3,7},{4,0},{5,1},{6,2},{7,3},{8,12},{9,13},{10,... | collective-permute-start | bytes 786440 | tf_op jit(solution)/shard_map/ppermute | solution.py:330
  71.2 8.0 %collective-permute-start.17 = (bf16[512,256]{1,0:T(8,128)(2,1)S(1)}, bf16[512,256]{1,0:T(8,128)(2,1)S(1)}, u32[]{:S(2)}, u32[]{:S(2)}) collective-permute-start(bf16[512,256]{1,0:T(8,128)(2,1)S(1)} %add_second.7), channel_id=1, source_target_pairs={{0,2},{1,3},{2,0},{3,1},{4,6},{5,7},{6,4},{7,5},{8,10},{9,11},{10,... | collective-permute-start | bytes 786440 | tf_op jit(solution)/shard_map/ppermute | solution.py:330
  73.0 6.4 %collective-permute-start.18 = (bf16[512,256]{1,0:T(8,128)(2,1)S(1)}, bf16[512,256]{1,0:T(8,128)(2,1)S(1)}, u32[]{:S(2)}, u32[]{:S(2)}) collective-permute-start(bf16[512,256]{1,0:T(8,128)(2,1)S(1)} %get-tuple-element.48), channel_id=1, source_target_pairs={{0,1},{1,0},{2,3},{3,2},{4,5},{5,4},{6,7},{7,6},{8,24},{9,25},{10,... | collective-permute-start | bytes 786440 | tf_op jit(solution)/shard_map/ppermute | solution.py:330

commit v5 on v4

--- a/solution.py
+++ b/solution.py
@@ -8,6 +8,7 @@
 from jax.sharding import PartitionSpec as P
 
 CAP = 8
+TAIL = 16
 CORES = 2
 MIB = 1024 * 1024
 SMEM = pl.BlockSpec(memory_space=pltpu.SMEM)
@@ -25,47 +26,47 @@
 ANY = pl.BlockSpec(memory_space=pl.ANY)
 
 
-def prep_kernel(owner_links, blk_dev, n_sub, adj_ref, spot_ref, dest_ref, *refs):
-    lists, (flat_ref, count_ref) = refs[:n_sub], refs[n_sub:]
+def corner(block):
+    row = lax.broadcasted_iota(jnp.int32, (block // 2, block), 0)
+    return row, lax.broadcasted_iota(jnp.int32, (block // 2, block), 1)
+
+
+def pack(square):
+    block = square.shape[0]
+    half = block // 2
+    row, lane = corner(block)
+    last = pltpu.roll(square[half:], half, 1)
+    upper = jnp.where(lane < row, last, square[:half])
+    diagonal = jnp.sum(jnp.where(lane == row, last, 0.0), axis=0, keepdims=True)
+    return upper.astype(jnp.bfloat16), diagonal
+
+
+def unpack(upper, diagonal):
+    block = upper.shape[1]
+    half = block // 2
+    row, lane = corner(block)
+    top = jnp.where(lane > row, upper, jnp.where(lane == row, 0.5 * upper, 0.0))
+    low = jnp.where(lane < row, upper, jnp.where(lane == row, 0.5 * diagonal, 0.0))
+    square = jnp.concatenate([top, pltpu.roll(low, half, 1)], axis=0)
+    return square + square.T
+
+
+def contrib_kernel(
+    owner_links, blk_dev, n_sub, rows_ref, adj_ref, modes_ref, coup_ref, inv_ref, *refs
+):
+    outs = refs[:n_sub]
+    part_ref, edge_ref, all_ref, side_ref, count_ref, local_ref = refs[n_sub:]
+    s = pl.program_id(0)
     sub = lax.axis_index("sub")
-    spot_ref[0] = sub
-    spot_ref[1] = lax.axis_index("tile")
-    subs, links = adj_ref.shape
-    for d in range(n_sub):
-        count_ref[d] = 0
-        for i in range(CAP):
-            flat_ref[d * CAP + i] = blk_dev
-    for s in range(subs):
-        for a in range(links):
-            ident = adj_ref[s, a]
-            rel = (ident // owner_links) ^ sub
-            slot = count_ref[rel]
-            count_ref[rel] = slot + 1
-            flat_ref[rel * CAP + slot] = ident % blk_dev
-            dest_ref[s, a] = rel * CAP + slot
-    for d in range(n_sub):
-        for i in range(CAP):
-            lists[d][i] = flat_ref[d * CAP + i]
-
-
-def make_prep(adjacency, n_sub, owner_links, blk_dev):
-    int_of = lambda *shape: jax.ShapeDtypeStruct(shape, jnp.int32)
-    return pl.pallas_call(
-        functools.partial(prep_kernel, owner_links, blk_dev, n_sub),
-        in_specs=[SMEM],
-        out_specs=[SMEM] * (2 + n_sub),
-        out_shape=[int_of(2), int_of(*adjacency.shape)] + [int_of(CAP)] * n_sub,
-        scratch_shapes=[pltpu.SMEM((n_sub * CAP,), jnp.int32), pltpu.SMEM((n_sub,), jnp.int32)],
-        compiler_params=params(60),
-        cost_estimate=cheap(),
-        name="prep",
-    )(adjacency)
-
-
-def contrib_kernel(rows_ref, dest_ref, modes_ref, coup_ref, inv_ref, *refs):
-    outs, (part_ref, all_ref) = refs[:-2], refs[-2:]
-    s = pl.program_id(0)
     links, rows, block = coup_ref.shape[1:]
+
+    @pl.when(s == 0)
+    def _():
+        for d in range(n_sub):
+            count_ref[d] = 0
+            for i in range(CAP):
+                local_ref[d * CAP + i] = blk_dev
+
     live = lax.broadcasted_iota(jnp.int32, (rows, 1), 0) < rows_ref[s]
     modes = jnp.where(live, modes_ref[0], jnp.zeros((), modes_ref.dtype))
     inv = inv_ref[pl.ds(s, 1), :]
@@ -75,27 +76,50 @@
     )
     weighted = (red * inv).astype(jnp.bfloat16)
     red_b = red.astype(jnp.bfloat16)
-    for a in range(links):
-        part = slice(a * block, (a + 1) * block)
-        part_ref[a] = lax.dot_general(
+    group = 2 if links % 2 == 0 else 1
+    for a in range(0, links, group):
+        part = slice(a * block, (a + group) * block)
+        square = lax.dot_general(
             weighted[part], red_b[part], (((1,), (1,)), ((), ())),
             preferred_element_type=jnp.float32,
-        ).astype(jnp.bfloat16)
+        )
+        for i in range(group):
+            here = slice(i * block, (i + 1) * block)
+            upper, diagonal = pack(square[here, here])
+            part_ref[a + i] = upper
+            edge_ref[a + i] = diagonal
     for a in range(links):
-        all_ref[dest_ref[s, a]] = part_ref[a]
+        ident = adj_ref[s, a]
+        rel = (ident // owner_links) ^ sub
+        slot = count_ref[rel]
+        count_ref[rel] = slot + 1
+        at = rel * CAP + slot
+        local_ref[at] = ident % blk_dev
+        all_ref[at] = part_ref[a]
+        side_ref[at] = edge_ref[a]
 
     @pl.when(s == pl.num_programs(0) - 1)
     def _():
+        half = block // 2
+        row = lax.broadcasted_iota(jnp.int32, (TAIL, block), 0)
+        lane = lax.broadcasted_iota(jnp.int32, (TAIL, block), 1)
         for d, out in enumerate(outs):
-            out[...] = all_ref[d * CAP:(d + 1) * CAP]
-
-
-def make_contrib(dest, modes, coupling, inv_eig, sub_rows, n_sub):
+            tail = jnp.zeros((TAIL, block), jnp.float32)
+            for i in range(CAP):
+                out[i * half:(i + 1) * half] = all_ref[d * CAP + i]
+                place = local_ref[d * CAP + i].astype(jnp.float32)
+                tail = jnp.where(
+                    row == i, jnp.where(lane < half, side_ref[d * CAP + i], place), tail
+                )
+            out[CAP * half:] = tail.astype(jnp.bfloat16)
+
+
+def make_contrib(modes, coupling, inv_eig, sub_rows, adjacency, n_sub, owner_links, blk_dev):
     subs, rows, width = modes.shape
     links, block = coupling.shape[1], coupling.shape[3]
-    out = jax.ShapeDtypeStruct((CAP, block, block), jnp.bfloat16)
-    return pl.pallas_call(
-        contrib_kernel,
+    out = jax.ShapeDtypeStruct((CAP * block // 2 + TAIL, block), jnp.bfloat16)
+    return pl.pallas_call(
+        functools.partial(contrib_kernel, owner_links, blk_dev, n_sub),
         grid=(subs,),
         in_specs=[
             SMEM, SMEM,
@@ -103,66 +127,79 @@
             pl.BlockSpec((1, links, rows, block), lambda s: (s, 0, 0, 0)),
             pl.BlockSpec(inv_eig.shape, lambda s: (0, 0)),
         ],
-        out_specs=[pl.BlockSpec(out.shape, lambda s: (0, 0, 0))] * n_sub,
+        out_specs=[pl.BlockSpec(out.shape, lambda s: (0, 0))] * n_sub,
         out_shape=[out] * n_sub,
         scratch_shapes=[
-            pltpu.VMEM((links, block, block), jnp.bfloat16),
-            pltpu.VMEM((n_sub * CAP, block, block), jnp.bfloat16),
+            pltpu.VMEM((links, block // 2, block), jnp.bfloat16),
+            pltpu.VMEM((links, 1, block), jnp.float32),
+            pltpu.VMEM((n_sub * CAP, block // 2, block), jnp.bfloat16),
+            pltpu.VMEM((n_sub * CAP, 1, block), jnp.float32),
+            pltpu.SMEM((n_sub,), jnp.int32),
+            pltpu.SMEM((n_sub * CAP,), jnp.int32),
         ],
         compiler_params=params(55),
         cost_estimate=cheap(),
         name="contrib",
-    )(sub_rows, dest, modes, coupling, inv_eig)
-
-
-def near_kernel(base_ref, own_at, pair_at, own_ref, pair_ref, total_ref):
-    total_ref[:base_ref.shape[0]] = base_ref[...]
-    for place, group in ((own_at, own_ref), (pair_at, pair_ref)):
+    )(sub_rows, adjacency, modes, coupling, inv_eig)
+
+
+def add_groups(upper_ref, side_ref, groups):
+    half, block = upper_ref.shape[1:]
+    for group in groups:
+        tail = group[CAP * half:].astype(jnp.float32)
         for i in range(CAP):
-            total_ref[place[i]] += group[i].astype(jnp.float32)
-
-
-def make_near(base, places, groups):
-    blk_dev, block = base.shape[:2]
+            place = jnp.max(tail[i:i + 1, half:]).astype(jnp.int32)
+            upper_ref[place] += group[i * half:(i + 1) * half].astype(jnp.float32)
+            side_ref[place] += tail[i:i + 1]
+
+
+def near_kernel(own_ref, pair_ref, upper_ref, side_ref):
+    upper_ref[...] = jnp.zeros_like(upper_ref)
+    side_ref[...] = jnp.zeros_like(side_ref)
+    add_groups(upper_ref, side_ref, (own_ref, pair_ref))
+
+
+def make_near(blk_dev, groups):
+    block = groups[0].shape[1]
+    shapes = [(blk_dev + 1, block // 2, block), (blk_dev + 1, 1, block)]
     return pl.pallas_call(
         near_kernel,
-        in_specs=[VMEM] + [SMEM] * 2 + [VMEM] * 2,
+        in_specs=[VMEM] * 2,
+        out_specs=[VMEM] * 2,
+        out_shape=[jax.ShapeDtypeStruct(v, jnp.float32) for v in shapes],
+        compiler_params=params(12),
+        cost_estimate=cheap(),
+        name="near",
+    )(*groups)
+
+
+def far_kernel(count, base_ref, near_ref, near_side_ref, *rest):
+    mass_ref, upper_ref, side_ref = rest[-3:]
+    upper_ref[...] = near_ref[...]
+    side_ref[...] = near_side_ref[...]
+    add_groups(upper_ref, side_ref, rest[:count])
+    for b in range(mass_ref.shape[0]):
+        mass_ref[b] = (base_ref[b] + unpack(upper_ref[b], side_ref[b])).astype(jnp.bfloat16)
+
+
+def make_far(base, near, groups, behind):
+    return pl.pallas_call(
+        functools.partial(far_kernel, len(groups)),
+        in_specs=[VMEM] * (3 + len(groups)) + [ANY] * len(behind),
         out_specs=VMEM,
-        out_shape=jax.ShapeDtypeStruct((blk_dev + 1, block, block), jnp.float32),
+        out_shape=jax.ShapeDtypeStruct(base.shape, jnp.bfloat16),
+        scratch_shapes=[pltpu.VMEM(v.shape, jnp.float32) for v in near],
         compiler_params=params(12),
         cost_estimate=cheap(),
-        name="near",
-    )(base, *places, *groups)
-
-
-def far_kernel(count, near_ref, *rest):
-    mass_ref, total_ref = rest[-2:]
-    total_ref[...] = near_ref[...]
-    for place, group in zip(rest[:count], rest[count:2 * count]):
-        for i in range(CAP):
-            total_ref[place[i]] += group[i].astype(jnp.float32)
-    mass_ref[...] = total_ref[:mass_ref.shape[0]].astype(jnp.bfloat16)
-
-
-def make_far(near, places, groups, behind):
-    count, block = near.shape[:2]
-    return pl.pallas_call(
-        functools.partial(far_kernel, len(groups)),
-        in_specs=[VMEM] + [SMEM] * len(places) + [VMEM] * len(groups) + [ANY] * len(behind),
-        out_specs=VMEM,
-        out_shape=jax.ShapeDtypeStruct((count - 1, block, block), jnp.bfloat16),
-        scratch_shapes=[pltpu.VMEM(near.shape, jnp.float32)],
-        compiler_params=params(12),
-        cost_estimate=cheap(),
         name="far",
-    )(near, *places, *groups, *behind)
-
-
-def turn_kernel(spot_ref, psi_ref, out_ref, copy_ref, sems):
+    )(base, *near, *groups, *behind)
+
+
+def turn_kernel(psi_ref, out_ref, copy_ref, sems):
     band, n_sub = out_ref.shape[1], sems.shape[0]
 
     def bring(j):
-        at = pl.ds(pl.multiple_of((spot_ref[0] ^ j) * band, band), band)
+        at = pl.ds(pl.multiple_of((lax.axis_index("sub") ^ j) * band, band), band)
         return pltpu.make_async_copy(psi_ref.at[:, at], copy_ref.at[:, at], sems.at[j])
 
     order = list(range(0, n_sub, CORES)) + [j for j in range(n_sub) if j % CORES]
@@ -171,16 +208,16 @@
     for j in order:
         bring(j).wait()
         if j % CORES == 0:
-            at = pl.multiple_of((spot_ref[0] ^ j) * band, band)
+            at = pl.multiple_of((lax.axis_index("sub") ^ j) * band, band)
             out_ref[j // CORES] = copy_ref[:, pl.ds(at, band)].T
 
 
-def turn(spot, psi, n_sub):
+def turn(psi, n_sub):
     depth, width = psi.shape
     shape = (n_sub // CORES, width // n_sub, depth)
     return pl.pallas_call(
         turn_kernel,
-        in_specs=[SMEM, ANY],
+        in_specs=[ANY],
         out_specs=[VMEM, VMEM],
         out_shape=[
             jax.ShapeDtypeStruct(shape, psi.dtype), jax.ShapeDtypeStruct(psi.shape, psi.dtype)
@@ -189,7 +226,27 @@
         compiler_params=params(16),
         cost_estimate=cheap(),
         name="turn",
-    )(spot, psi)
+    )(psi)
+
+
+def turn_own_kernel(psi_ref, out_ref):
+    n_x, band = out_ref.shape[:2]
+    for x in range(n_x):
+        at = pl.multiple_of((lax.axis_index("sub") ^ (x * CORES)) * band, band)
+        out_ref[x] = psi_ref[:, pl.ds(at, band)].T
+
+
+def turn_own(psi, n_sub):
+    depth, width = psi.shape
+    return pl.pallas_call(
+        turn_own_kernel,
+        in_specs=[VMEM],
+        out_specs=VMEM,
+        out_shape=jax.ShapeDtypeStruct((n_sub // CORES, width // n_sub, depth), psi.dtype),
+        compiler_params=params(16),
+        cost_estimate=cheap(),
+        name="turn_own",
+    )(psi)
 
 
 def left_kernel(mass_ref, turned_ref, out_ref):
@@ -224,17 +281,17 @@
     )(mass, turned)
 
 
-def product_kernel(chunk, pairs, acc_in, go, keep, behind, spot_ref, *refs):
+def product_kernel(chunk, pairs, acc_in, go, keep, behind, *refs):
     lefts, psis, refs = refs[:pairs], refs[pairs:2 * pairs], refs[2 * pairs:]
     acc = refs[0] if acc_in else None
     outs = list(refs[int(acc_in) + behind:])
     high, z = chunk
-    core = spot_ref[0] % CORES
+    core = lax.axis_index("sub") % CORES
 
     def block(x, y):
         band, width = outs[0].shape[1:]
         rows = pl.ds(pl.multiple_of((2 * high + x) * band, band), band)
-        tile = spot_ref[1] ^ (2 * z + y)
+        tile = lax.axis_index("tile") ^ (2 * z + y)
         cols = pl.ds(pl.multiple_of(tile * width, width), width)
         res = None
         for left, psi in zip(lefts, psis):
@@ -254,7 +311,7 @@
         out[i] = res.astype(out.dtype)
 
 
-def product(chunk, spot, lefts, psis, band, width, go=None, keep=False, acc=(), behind=()):
+def product(chunk, lefts, psis, band, width, go=None, keep=False, acc=(), behind=()):
     depth = lefts[0].shape[1]
     types = ([go] if go is not None else []) + ([jnp.float32] if keep else [])
     flops = len(types) * 4 * band * width * depth * len(lefts)
@@ -262,7 +319,7 @@
         functools.partial(
             product_kernel, chunk, len(lefts), bool(acc), go is not None, keep, len(behind)
         ),
-        in_specs=[SMEM] + [VMEM] * (2 * len(lefts) + len(acc)) + [ANY] * len(behind),
+        in_specs=[VMEM] * (2 * len(lefts) + len(acc)) + [ANY] * len(behind),
         out_specs=[VMEM] * len(types),
         out_shape=[jax.ShapeDtypeStruct((2, band, width), t) for t in types],
         compiler_params=params(16),
@@ -270,7 +327,7 @@
             flops=flops, bytes_accessed=flops // 512, transcendentals=0
         ),
         name="product",
-    )(spot, *lefts, *psis, *acc, *behind)
+    )(*lefts, *psis, *acc, *behind)
 
 
 def first_kernel(keep_ref, got_ref, *refs):
@@ -341,30 +398,30 @@
         step = 0 if z else (high & -high) * 2 * CORES
         return swap(v, lambda i, j: (i ^ step, j ^ (2 * bit)))
 
-    spot, dest, *lists = make_prep(adjacency, n_sub, owner_links, blk_dev)
-    lists = [swap_sub(v, d) if d else v for d, v in enumerate(lists)]
     other = swap_sub(iface_modes, 1)
-    sent = make_contrib(dest, modes, coupling, inv_eig, sub_rows, n_sub)
+    sent = make_contrib(
+        modes, coupling, inv_eig, sub_rows, adjacency, n_sub, owner_links, blk_dev
+    )
     far = [swap_sub(sent[d], d) for d in range(CORES, n_sub)]
-    near = make_near(base_mass, lists[:CORES], [sent[0], swap_sub(sent[1], 1)])
-    own_t, own = turn(spot, iface_modes, n_sub)
-    other_t, other = turn(spot, other, n_sub)
-    mass = make_far(near, lists[CORES:], far, [own_t, other_t])
+    near = make_near(blk_dev, [sent[0], swap_sub(sent[1], 1)])
+    own_t, own = turn_own(iface_modes, n_sub), iface_modes
+    other_t, other = turn(other, n_sub)
+    mass = make_far(base_mass, near, far, [own_t, other_t])
     mass_other = swap_sub(mass, 1)
     left = make_left(mass, own_t)
 
     chunks = [(h, z) for h in range(n_sub // (2 * CORES)) for z in range(n_tile // 2)][::-1]
     goes_to = {(h, z): (h, z & (z - 1)) if z else (h & (h - 1), 0) for h, z in chunks[:-1]}
-    head = product(chunks[0], spot, [left], [own], band, tile, go=jnp.float32)
+    head = product(chunks[0], [left], [own], band, tile, go=jnp.float32)
     left_other = make_left(mass_other, other_t)
     lefts, psis = [left, left_other], [own, other]
 
     keep, first, second, third = {}, {}, {}, {}
     tails = {c: [] for c in chunks}
     last = len(chunks) - 1
-    common = spot, lefts, psis, band, tile
+    common = lefts, psis, band, tile
     go, = product(
-        chunks[0], spot, [left_other], [other], band, tile, go=jnp.bfloat16, acc=head
+        chunks[0], [left_other], [other], band, tile, go=jnp.bfloat16, acc=head
     )
     for i in range(last + 1):
         first[i] = swap_first(go)

time: 80.7 us -> 71.4 us (0.88)
  Pallas kernels: 47.9 us -> 37.8 us
  waiting for transfers between devices: 10.7 us -> 12.5 us
    pallas_call x5 -> x4, Pallas kernels: 18.8 us -> 13.7 us  [the longest x1 8.65 us: make_contrib(): pl.pallas_call(functools.partial(contrib_kernel, owner_links, blk_dev, n_...]
    pallas_call x9, Pallas kernels: 24.3 us -> 19.4 us  [product(): pl.pallas_call(functools.partial(product_kernel, chunk, len(lefts), bool(...]
    ppermute x11, waiting for transfers between devices: 8.74 us -> 10.9 us  [swap(): return lax.ppermute(v, ('sub', 'tile'), pairs)]
    ppermute x8 -> x5, starting transfers between devices: 5.73 us -> 3.73 us  [swap_sub(): return lax.ppermute(v, 'sub', [(i, i ^ d) for i in range(n_sub)])]
    ppermute x11, starting transfers between devices: 15.5 us -> 16.9 us  [swap(): return lax.ppermute(v, ('sub', 'tile'), pairs)]
    ppermute x8 -> x5, waiting for transfers between devices: 1.98 us -> 1.69 us  [swap_sub(): return lax.ppermute(v, 'sub', [(i, i ^ d) for i in range(n_sub)])]
  transfers between devices with their start and end apart: 19 -> 16, of which waited for: 6 -> 6; matrix products, arithmetic and copies ran while one was open for 0% -> 0% of each run, Pallas kernels for 54% -> 47%
where the time goes in v5:
time: 71.4 us; the launch traced here: 71.2 us
  Pallas kernels  37.8 us (53%)
  starting transfers between devices  20.6 us (29%)
  waiting for transfers between devices  12.5 us (18%)
    pallas_call x9, Pallas kernels, product(): pl.pallas_call(functools.partial(product_kernel, chunk, len(lefts), bool(...  19.4 us
    ppermute x11, starting transfers between devices, swap(): return lax.ppermute(v, ('sub', 'tile'), pairs)  16.9 us
    ppermute x11, waiting for transfers between devices, swap(): return lax.ppermute(v, ('sub', 'tile'), pairs)  10.9 us
    pallas_call x1, Pallas kernels, make_contrib(): pl.pallas_call(functools.partial(contrib_kernel, owner_links, blk_dev, n_...  8.65 us
    ppermute x5, starting transfers between devices, swap_sub(): return lax.ppermute(v, 'sub', [(i, i ^ d) for i in range(n_sub)])  3.73 us
    pallas_call x1, Pallas kernels, turn(): pl.pallas_call(turn_kernel, in_specs=[ANY], out_specs=[VMEM, VMEM], out_s...  3.64 us
    pallas_call x2, Pallas kernels, make_left(): pl.pallas_call(left_kernel, in_specs=[VMEM, VMEM], out_specs=VMEM, out_sh...  2.51 us
    ppermute x5, waiting for transfers between devices, swap_sub(): return lax.ppermute(v, 'sub', [(i, i ^ d) for i in range(n_sub)])  1.69 us
  transfers between devices with their start and end apart: 16, of which 6 were waited for; matrix products, arithmetic and copies ran while one was open for 0% of the time, Pallas kernels for 47%

profile of v5, /device:TPU:0, one launch (start us, length us, event | category | flops | bytes accessed | tf_op | source)
XLA Modules:
  0.0 71.2 jit_solution(16991508706895530763)
XLA Ops:
  0.0 0.5 collective-permute-start.3
  0.5 8.6 %contrib.1 = (bf16[528,128]{1,0:T(8,128)(2,1)}, bf16[528,128]{1,0:T(8,128)(2,1)}, bf16[528,128]{1,0:T(8,128)(2,1)}, bf16[528,128]{1,0:T(8,128)(2,1)}) custom-call(s32[4]{0:T(128)} %rows_ref.1, s32[4,8]{1,0:T(4,128)} %adj_ref.1, bf16[4,768,512]{2,1,0:T(8,128)(2,1)} %modes_ref.1, bf16[4,8,768,128]{3,2,1,0:T(8,128)(2,1)} %coup_ref.1, f32[4,512]{1,0:T(4,128)} %inv_ref.1), custom_call_target="tpu_custom_call" | custom-call | flops 1 | bytes 1 | tf_op jit(solution)/shard_map/contrib/pallas_call | solution.py:121
  9.1 0.4 collective-permute-start
  9.5 2.6 %collective-permute-start.1 = (bf16[528,128]{1,0:T(8,128)(2,1)}, bf16[528,128]{1,0:T(8,128)(2,1)S(1)}, u32[]{:S(2)}, u32[]{:S(2)}) collective-permute-start(bf16[528,128]{1,0:T(8,128)(2,1)} %get-tuple-element.25), channel_id=1, source_target_pairs={{0,16},{8,24},{16,0},{24,8},{1,17},{9,25},{17,1},{25,9},{2,18},{10... | collective-permute-start | bytes 405512 | tf_op jit(solution)/shard_map/ppermute | solution.py:379
  12.2 0.0 collective-permute-start.2
  12.2 1.3 %turn_own.1.rest_2_.turned_ref = bf16[2,512,2048]{2,1,0:T(8,128)(2,1)S(1)} custom-call(bf16[2048,2048]{1,0:T(8,128)(2,1)S(1)} %copy-done), custom_call_target="tpu_custom_call" | custom-call | flops 1 | bytes 1 | tf_op jit(solution)/shard_map/turn_own/pallas_call | solution.py:241
  13.4 0.2 collective-permute-done.pair_ref
  13.6 0.2 near.1
  13.9 0.0 copy-start.1
  13.9 0.0 collective-permute-done.3.psi_ref
  13.9 3.6 %turn.1 = (bf16[2,512,2048]{2,1,0:T(8,128)(2,1)S(1)}, bf16[2048,2048]{1,0:T(8,128)(2,1)S(1)}) custom-call(bf16[2048,2048]{1,0:T(8,128)(2,1)} %collective-permute-done.3.psi_ref), custom_call_target="tpu_custom_call" | custom-call | flops 1 | bytes 1 | tf_op jit(solution)/shard_map/turn/pallas_call | solution.py:218
  17.5 1.5 %collective-permute-done.2.rest_1_ = bf16[528,128]{1,0:T(8,128)(2,1)S(1)} collective-permute-done((bf16[528,128]{1,0:T(8,128)(2,1)}, bf16[528,128]{1,0:T(8,128)(2,1)S(1)}, u32[]{:S(2)}, u32[]{:S(2)}) %collective-permute-start.2) | collective-permute-done | bytes 135200 | tf_op jit(solution)/shard_map/ppermute | solution.py:379
  19.0 0.7 %far.1.mass_ref = bf16[16,128,128]{2,1,0:T(8,128)(2,1)S(1)} custom-call(f32[16,128,128]{2,1,0:T(8,128)S(1)} %copy-done.1, f32[17,64,128]{2,1,0:T(8,128)S(1)} %get-tuple-element.23.near_ref, f32[17,1,128]{2,1,0:T(1,128)S(1)} %get-tuple-element.24.near_side_ref, bf16[528,128]{1,0:T(8,128)(2,1)S(1)} %collective-permute-done.1.rest_0_, ...), custom_call_target="tpu_custom_call" | custom-call | flops 1 | bytes 1 | tf_op jit(solution)/shard_map/far/pallas_call | solution.py:186
  19.7 0.2 collective-permute-start.4
  20.0 1.3 %left.2.refs_0_ = bf16[1024,2048]{1,0:T(8,128)(2,1)S(1)} custom-call(bf16[16,128,128]{2,1,0:T(8,128)(2,1)S(1)} %far.1.mass_ref, bf16[2,512,2048]{2,1,0:T(8,128)(2,1)S(1)} %turn_own.1.rest_2_.turned_ref), custom_call_target="tpu_custom_call" | custom-call | flops 1 | bytes 1 | tf_op jit(solution)/shard_map/left/pallas_call | solution.py:273
  21.2 1.3 %product.9.refs_2_ = f32[2,512,256]{2,1,0:T(8,128)S(1)} custom-call(bf16[1024,2048]{1,0:T(8,128)(2,1)S(1)} %left.2.refs_0_, bf16[2048,2048]{1,0:T(8,128)(2,1)S(1)} %copy-done), custom_call_target="tpu_custom_call" | custom-call | flops 1073741824 | bytes 2097152 | tf_op jit(solution)/shard_map/product/pallas_call | solution.py:318
  22.5 0.0 collective-permute-done.4.mass_ref
  22.5 1.3 %left.3.refs_0_.refs_1_ = bf16[1024,2048]{1,0:T(8,128)(2,1)S(1)} custom-call(bf16[16,128,128]{2,1,0:T(8,128)(2,1)S(1)} %collective-permute-done.4.mass_ref, bf16[2,512,2048]{2,1,0:T(8,128)(2,1)S(1)} %get-tuple-element.27.rest_3_.turned_ref), custom_call_target="tpu_custom_call" | custom-call | flops 1 | bytes 1 | tf_op jit(solution)/shard_map/left/pallas_call | solution.py:273
  23.8 1.3 %product.10.refs_4_ = bf16[2,512,256]{2,1,0:T(8,128)(2,1)S(1)} custom-call(bf16[1024,2048]{1,0:T(8,128)(2,1)S(1)} %left.3.refs_0_.refs_1_, bf16[2048,2048]{1,0:T(8,128)(2,1)S(1)} %get-tuple-element.28.refs_1_.refs_3_, f32[2,512,256]{2,1,0:T(8,128)S(1)} %product.9.refs_2_), custom_call_target="tpu_custom_call" | custom-call | flops 1073741824 | bytes 2097152 | tf_op jit(solution)/shard_map/product/pallas_call | solution.py:318
  25.1 1.8 %collective-permute-start.5 = (bf16[2,512,256]{2,1,0:T(8,128)(2,1)S(1)}, bf16[2,512,256]{2,1,0:T(8,128)(2,1)S(1)}, u32[]{:S(2)}, u32[]{:S(2)}) collective-permute-start(bf16[2,512,256]{2,1,0:T(8,128)(2,1)S(1)} %product.10.refs_4_), channel_id=1, source_target_pairs={{0,16},{1,17},{2,18},{3,19},{4,20},{5,21},{6,22},{7,23},{8,9},{9,8... | collective-permute-start | bytes 1572872 | tf_op jit(solution)/shard_map/ppermute | solution.py:387
  26.9 2.4 %product.11.refs_4_ = bf16[2,512,256]{2,1,0:T(8,128)(2,1)S(1)} custom-call(bf16[1024,2048]{1,0:T(8,128)(2,1)S(1)} %left.2.refs_0_, bf16[1024,2048]{1,0:T(8,128)(2,1)S(1)} %left.3.refs_0_.refs_1_, bf16[2048,2048]{1,0:T(8,128)(2,1)S(1)} %copy-done, bf16[2048,2048]{1,0:T(8,128)(2,1)S(1)} %get-tuple-element.28.refs_1_.refs_3_, ...), custom_call_target="tpu_custom_call" | custom-call | flops 2147483648 | bytes 4194304 | tf_op jit(solution)/shard_map/product/pallas_call | solution.py:318
  29.3 0.3 collective-permute-start.6
  29.6 2.4 %product.12.keep_ref = f32[2,512,256]{2,1,0:T(8,128)S(1)} custom-call(bf16[1024,2048]{1,0:T(8,128)(2,1)S(1)} %left.2.refs_0_, bf16[1024,2048]{1,0:T(8,128)(2,1)S(1)} %left.3.refs_0_.refs_1_, bf16[2048,2048]{1,0:T(8,128)(2,1)S(1)} %copy-done, bf16[2048,2048]{1,0:T(8,128)(2,1)S(1)} %get-tuple-element.28.refs_1_.refs_3_, bf16[2,512,256]{2,1,0:T(8,128)(2,1)S(1)} %product.11.refs_4_), custom_call_target="tpu_custom_call" | custom-call | flops 2147483648 | bytes 4194304 | tf_op jit(solution)/shard_map/product/pallas_call | solution.py:318
  32.0 2.3 %collective-permute-done.5.got_ref = bf16[2,512,256]{2,1,0:T(8,128)(2,1)S(1)} collective-permute-done((bf16[2,512,256]{2,1,0:T(8,128)(2,1)S(1)}, bf16[2,512,256]{2,1,0:T(8,128)(2,1)S(1)}, u32[]{:S(2)}, u32[]{:S(2)}) %collective-permute-start.5) | collective-permute-done | bytes 524320 | tf_op jit(solution)/shard_map/ppermute | solution.py:387
  34.3 0.1 add_first.4
  34.4 1.8 %collective-permute-start.8 = (bf16[512,256]{1,0:T(8,128)(2,1)S(1)}, bf16[512,256]{1,0:T(8,128)(2,1)S(1)}, u32[]{:S(2)}, u32[]{:S(2)}) collective-permute-start(bf16[512,256]{1,0:T(8,128)(2,1)S(1)} %get-tuple-element.32), channel_id=1, source_target_pairs={{0,1},{1,0},{2,3},{3,2},{4,5},{5,4},{6,7},{7,6},{8,24},{9,25},{10,... | collective-permute-start | bytes 786440 | tf_op jit(solution)/shard_map/ppermute | solution.py:387
  36.2 2.6 %product.13.refs_4_ = bf16[2,512,256]{2,1,0:T(8,128)(2,1)S(1)} custom-call(bf16[1024,2048]{1,0:T(8,128)(2,1)S(1)} %left.2.refs_0_, bf16[1024,2048]{1,0:T(8,128)(2,1)S(1)} %left.3.refs_0_.refs_1_, bf16[2048,2048]{1,0:T(8,128)(2,1)S(1)} %copy-done, bf16[2048,2048]{1,0:T(8,128)(2,1)S(1)} %get-tuple-element.28.refs_1_.refs_3_, ...), custom_call_target="tpu_custom_call" | custom-call | flops 2147483648 | bytes 4194304 | tf_op jit(solution)/shard_map/product/pallas_call | solution.py:318
  38.8 1.6 %collective-permute-start.12 = (bf16[2,512,256]{2,1,0:T(8,128)(2,1)S(1)}, bf16[2,512,256]{2,1,0:T(8,128)(2,1)S(1)}, u32[]{:S(2)}, u32[]{:S(2)}) collective-permute-start(bf16[2,512,256]{2,1,0:T(8,128)(2,1)S(1)} %product.13.refs_4_), channel_id=1, source_target_pairs={{0,16},{1,17},{2,18},{3,19},{4,20},{5,21},{6,22},{7,23},{8,9},{9,8... | collective-permute-start | bytes 1572872 | tf_op jit(solution)/shard_map/ppermute | solution.py:387
  40.4 2.4 %product.14.keep_ref = f32[2,512,256]{2,1,0:T(8,128)S(1)} custom-call(bf16[1024,2048]{1,0:T(8,128)(2,1)S(1)} %left.2.refs_0_, bf16[1024,2048]{1,0:T(8,128)(2,1)S(1)} %left.3.refs_0_.refs_1_, bf16[2048,2048]{1,0:T(8,128)(2,1)S(1)} %copy-done, bf16[2048,2048]{1,0:T(8,128)(2,1)S(1)} %get-tuple-element.28.refs_1_.refs_3_, bf16[2,512,256]{2,1,0:T(8,128)(2,1)S(1)} %product.13.refs_4_), custom_call_target="tpu_custom_call" | custom-call | flops 2147483648 | bytes 4194304 | tf_op jit(solution)/shard_map/product/pallas_call | solution.py:318
  42.8 0.1 add_first.5
  42.9 2.4 %product.15.refs_4_ = bf16[2,512,256]{2,1,0:T(8,128)(2,1)S(1)} custom-call(bf16[1024,2048]{1,0:T(8,128)(2,1)S(1)} %left.2.refs_0_, bf16[1024,2048]{1,0:T(8,128)(2,1)S(1)} %left.3.refs_0_.refs_1_, bf16[2048,2048]{1,0:T(8,128)(2,1)S(1)} %copy-done, bf16[2048,2048]{1,0:T(8,128)(2,1)S(1)} %get-tuple-element.28.refs_1_.refs_3_, ...), custom_call_target="tpu_custom_call" | custom-call | flops 2147483648 | bytes 4194304 | tf_op jit(solution)/shard_map/product/pallas_call | solution.py:318
  45.2 1.8 %collective-permute-start.10 = (bf16[2,512,256]{2,1,0:T(8,128)(2,1)S(1)}, bf16[2,512,256]{2,1,0:T(8,128)(2,1)S(1)}, u32[]{:S(2)}, u32[]{:S(2)}) collective-permute-start(bf16[2,512,256]{2,1,0:T(8,128)(2,1)S(1)} %product.15.refs_4_), channel_id=1, source_target_pairs={{0,16},{1,17},{2,18},{3,19},{4,20},{5,21},{6,22},{7,23},{8,9},{9,8... | collective-permute-start | bytes 1572872 | tf_op jit(solution)/shard_map/ppermute | solution.py:387
  47.0 1.5 %collective-permute-start.7 = (bf16[512,256]{1,0:T(8,128)(2,1)S(1)}, bf16[512,256]{1,0:T(8,128)(2,1)S(1)}, u32[]{:S(2)}, u32[]{:S(2)}) collective-permute-start(bf16[512,256]{1,0:T(8,128)(2,1)S(1)} %get-tuple-element.31), channel_id=1, source_target_pairs={{0,1},{1,0},{2,3},{3,2},{4,5},{5,4},{6,7},{7,6},{8,24},{9,25},{10,... | collective-permute-start | bytes 786440 | tf_op jit(solution)/shard_map/ppermute | solution.py:387
  48.6 1.7 %collective-permute-start.9 = (bf16[512,256]{1,0:T(8,128)(2,1)S(1)}, bf16[512,256]{1,0:T(8,128)(2,1)S(1)}, u32[]{:S(2)}, u32[]{:S(2)}) collective-permute-start(bf16[512,256]{1,0:T(8,128)(2,1)S(1)} %add_second.5.refs_5_), channel_id=1, source_target_pairs={{0,2},{1,3},{2,0},{3,1},{4,6},{5,7},{6,4},{7,5},{8,10},{9,11},{10,... | collective-permute-start | bytes 786440 | tf_op jit(solution)/shard_map/ppermute | solution.py:387
  50.3 2.4 %product.17.keep_ref = f32[2,512,256]{2,1,0:T(8,128)S(1)} custom-call(bf16[1024,2048]{1,0:T(8,128)(2,1)S(1)} %left.2.refs_0_, bf16[1024,2048]{1,0:T(8,128)(2,1)S(1)} %left.3.refs_0_.refs_1_, bf16[2048,2048]{1,0:T(8,128)(2,1)S(1)} %copy-done, bf16[2048,2048]{1,0:T(8,128)(2,1)S(1)} %get-tuple-element.28.refs_1_.refs_3_, ...), custom_call_target="tpu_custom_call" | custom-call | flops 2147483648 | bytes 4194304 | tf_op jit(solution)/shard_map/product/pallas_call | solution.py:318
  52.7 0.1 add_first.7
  52.8 0.6 collective-permute-start.13
  53.3 2.9 %collective-permute-done.7.got_ref = bf16[512,256]{1,0:T(8,128)(2,1)S(1)} collective-permute-done((bf16[512,256]{1,0:T(8,128)(2,1)S(1)}, bf16[512,256]{1,0:T(8,128)(2,1)S(1)}, u32[]{:S(2)}, u32[]{:S(2)}) %collective-permute-start.7) | collective-permute-done | bytes 262176 | tf_op jit(solution)/shard_map/ppermute | solution.py:387
  56.2 0.1 add_second.6.refs_5_
  56.3 2.6 %collective-permute-start.11 = (bf16[512,256]{1,0:T(8,128)(2,1)S(1)}, bf16[512,256]{1,0:T(8,128)(2,1)S(1)}, u32[]{:S(2)}, u32[]{:S(2)}) collective-permute-start(bf16[512,256]{1,0:T(8,128)(2,1)S(1)} %add_second.6.refs_5_), channel_id=1, source_target_pairs={{0,4},{1,5},{2,6},{3,7},{4,0},{5,1},{6,2},{7,3},{8,12},{9,13},{10,... | collective-permute-start | bytes 786440 | tf_op jit(solution)/shard_map/ppermute | solution.py:387
  58.9 2.4 %product.16.keep_ref = f32[2,512,256]{2,1,0:T(8,128)S(1)} custom-call(bf16[1024,2048]{1,0:T(8,128)(2,1)S(1)} %left.2.refs_0_, bf16[1024,2048]{1,0:T(8,128)(2,1)S(1)} %left.3.refs_0_.refs_1_, bf16[2048,2048]{1,0:T(8,128)(2,1)S(1)} %copy-done, bf16[2048,2048]{1,0:T(8,128)(2,1)S(1)} %get-tuple-element.28.refs_1_.refs_3_, ...), custom_call_target="tpu_custom_call" | custom-call | flops 2147483648 | bytes 4194304 | tf_op jit(solution)/shard_map/product/pallas_call | solution.py:318
  61.3 1.7 %collective-permute-start.14 = (bf16[512,256]{1,0:T(8,128)(2,1)S(1)}, bf16[512,256]{1,0:T(8,128)(2,1)S(1)}, u32[]{:S(2)}, u32[]{:S(2)}) collective-permute-start(bf16[512,256]{1,0:T(8,128)(2,1)S(1)} %add_second.7), channel_id=1, source_target_pairs={{0,2},{1,3},{2,0},{3,1},{4,6},{5,7},{6,4},{7,5},{8,10},{9,11},{10,... | collective-permute-start | bytes 786440 | tf_op jit(solution)/shard_map/ppermute | solution.py:387
  63.0 0.1 add_first.6
  63.1 1.5 %collective-permute-start.15 = (bf16[512,256]{1,0:T(8,128)(2,1)S(1)}, bf16[512,256]{1,0:T(8,128)(2,1)S(1)}, u32[]{:S(2)}, u32[]{:S(2)}) collective-permute-start(bf16[512,256]{1,0:T(8,128)(2,1)S(1)} %get-tuple-element.36), channel_id=1, source_target_pairs={{0,1},{1,0},{2,3},{3,2},{4,5},{5,4},{6,7},{7,6},{8,24},{9,25},{10,... | collective-permute-start | bytes 786440 | tf_op jit(solution)/shard_map/ppermute | solution.py:387
  64.6 2.9 %collective-permute-done.11.got_ref = bf16[512,256]{1,0:T(8,128)(2,1)S(1)} collective-permute-done((bf16[512,256]{1,0:T(8,128)(2,1)S(1)}, bf16[512,256]{1,0:T(8,128)(2,1)S(1)}, u32[]{:S(2)}, u32[]{:S(2)}) %collective-permute-start.11) | collective-permute-done | bytes 262176 | tf_op jit(solution)/shard_map/ppermute | solution.py:387
  67.6 2.7 %collective-permute-done.14.refs_0_ = bf16[512,256]{1,0:T(8,128)(2,1)S(1)} collective-permute-done((bf16[512,256]{1,0:T(8,128)(2,1)S(1)}, bf16[512,256]{1,0:T(8,128)(2,1)S(1)}, u32[]{:S(2)}, u32[]{:S(2)}) %collective-permute-start.14) | collective-permute-done | bytes 262176 | tf_op jit(solution)/shard_map/ppermute | solution.py:387
  70.3 0.1 add_second.8.low_ref
  70.4 0.8 %add_second.9 = f32[512,256]{1,0:T(8,128)} custom-call(f32[512,256]{1,0:T(8,128)S(1)} %add_second.8.low_ref, bf16[512,256]{1,0:T(8,128)(2,1)S(1)} %collective-permute-done.15.got_ref), custom_call_target="tpu_custom_call" | custom-call | flops 1 | bytes 1 | tf_op jit(solution)/shard_map/add_second/pallas_call | solution.py:360
  (15 shorter events, 0.1 us)
Async XLA Ops:
  0.0 12.2 %copy-start = (bf16[2048,2048]{1,0:T(8,128)(2,1)S(1)}, bf16[2048,2048]{1,0:T(8,128)(2,1)}, u32[]{:S(2)}) copy-start(bf16[2048,2048]{1,0:T(8,128)(2,1)} %refs_2_.13) | copy-start | bytes 25165828
  0.0 13.9 %collective-permute-start.3 = (bf16[2048,2048]{1,0:T(8,128)(2,1)}, bf16[2048,2048]{1,0:T(8,128)(2,1)}, u32[]{:S(2)}, u32[]{:S(2)}) collective-permute-start(bf16[2048,2048]{1,0:T(8,128)(2,1)} %refs_2_.13), channel_id=1, source_target_pairs={{0,8},{8,0},{16,24},{24,16},{1,9},{9,1},{17,25},{25,17},{2,10},{10... | collective-permute-start | bytes 25165832 | tf_op jit(solution)/shard_map/ppermute | solution.py:379
  9.1 4.5 %collective-permute-start = (bf16[528,128]{1,0:T(8,128)(2,1)}, bf16[528,128]{1,0:T(8,128)(2,1)S(1)}, u32[]{:S(2)}, u32[]{:S(2)}) collective-permute-start(bf16[528,128]{1,0:T(8,128)(2,1)} %get-tuple-element.22), channel_id=1, source_target_pairs={{0,8},{8,0},{16,24},{24,16},{1,9},{9,1},{17,25},{25,17},{2,10},{10... | collective-permute-start | bytes 405512 | tf_op jit(solution)/shard_map/ppermute | solution.py:379
  9.5 8.0 %collective-permute-start.1 = (bf16[528,128]{1,0:T(8,128)(2,1)}, bf16[528,128]{1,0:T(8,128)(2,1)S(1)}, u32[]{:S(2)}, u32[]{:S(2)}) collective-permute-start(bf16[528,128]{1,0:T(8,128)(2,1)} %get-tuple-element.25), channel_id=1, source_target_pairs={{0,16},{8,24},{16,0},{24,8},{1,17},{9,25},{17,1},{25,9},{2,18},{10... | collective-permute-start | bytes 405512 | tf_op jit(solution)/shard_map/ppermute | solution.py:379
  12.1 1.5 %copy-start.2 = (bf16[528,128]{1,0:T(8,128)(2,1)S(1)}, bf16[528,128]{1,0:T(8,128)(2,1)}, u32[]{:S(2)}) copy-start(bf16[528,128]{1,0:T(8,128)(2,1)} %get-tuple-element.21.own_ref) | copy-start | bytes 405508
  12.2 6.8 %collective-permute-start.2 = (bf16[528,128]{1,0:T(8,128)(2,1)}, bf16[528,128]{1,0:T(8,128)(2,1)S(1)}, u32[]{:S(2)}, u32[]{:S(2)}) collective-permute-start(bf16[528,128]{1,0:T(8,128)(2,1)} %get-tuple-element.26), channel_id=1, source_target_pairs={{0,24},{8,16},{16,8},{24,0},{1,25},{9,17},{17,9},{25,1},{2,26},{10... | collective-permute-start | bytes 405512 | tf_op jit(solution)/shard_map/ppermute | solution.py:379
  13.9 5.1 %copy-start.1 = (f32[16,128,128]{2,1,0:T(8,128)S(1)}, f32[16,128,128]{2,1,0:T(8,128)}, u32[]{:S(2)}) copy-start(f32[16,128,128]{2,1,0:T(8,128)} %base_ref.1) | copy-start | bytes 3145732
  19.7 2.8 %collective-permute-start.4 = (bf16[16,128,128]{2,1,0:T(8,128)(2,1)S(1)}, bf16[16,128,128]{2,1,0:T(8,128)(2,1)S(1)}, u32[]{:S(2)}, u32[]{:S(2)}) collective-permute-start(bf16[16,128,128]{2,1,0:T(8,128)(2,1)S(1)} %far.1.mass_ref), channel_id=1, source_target_pairs={{0,8},{8,0},{16,24},{24,16},{1,9},{9,1},{17,25},{25,17},{2,10},{10... | collective-permute-start | bytes 1572872 | tf_op jit(solution)/shard_map/ppermute | solution.py:379
  25.1 9.2 %collective-permute-start.5 = (bf16[2,512,256]{2,1,0:T(8,128)(2,1)S(1)}, bf16[2,512,256]{2,1,0:T(8,128)(2,1)S(1)}, u32[]{:S(2)}, u32[]{:S(2)}) collective-permute-start(bf16[2,512,256]{2,1,0:T(8,128)(2,1)S(1)} %product.10.refs_4_), channel_id=1, source_target_pairs={{0,16},{1,17},{2,18},{3,19},{4,20},{5,21},{6,22},{7,23},{8,9},{9,8... | collective-permute-start | bytes 1572872 | tf_op jit(solution)/shard_map/ppermute | solution.py:387
  29.3 13.5 %collective-permute-start.6 = (bf16[2,512,256]{2,1,0:T(8,128)(2,1)S(1)}, bf16[2,512,256]{2,1,0:T(8,128)(2,1)S(1)}, u32[]{:S(2)}, u32[]{:S(2)}) collective-permute-start(bf16[2,512,256]{2,1,0:T(8,128)(2,1)S(1)} %product.11.refs_4_), channel_id=1, source_target_pairs={{0,16},{1,17},{2,18},{3,19},{4,20},{5,21},{6,22},{7,23},{8,9},{9,8... | collective-permute-start | bytes 1572872 | tf_op jit(solution)/shard_map/ppermute | solution.py:387
  34.4 14.1 %collective-permute-start.8 = (bf16[512,256]{1,0:T(8,128)(2,1)S(1)}, bf16[512,256]{1,0:T(8,128)(2,1)S(1)}, u32[]{:S(2)}, u32[]{:S(2)}) collective-permute-start(bf16[512,256]{1,0:T(8,128)(2,1)S(1)} %get-tuple-element.32), channel_id=1, source_target_pairs={{0,1},{1,0},{2,3},{3,2},{4,5},{5,4},{6,7},{7,6},{8,24},{9,25},{10,... | collective-permute-start | bytes 786440 | tf_op jit(solution)/shard_map/ppermute | solution.py:387
  38.8 13.8 %collective-permute-start.12 = (bf16[2,512,256]{2,1,0:T(8,128)(2,1)S(1)}, bf16[2,512,256]{2,1,0:T(8,128)(2,1)S(1)}, u32[]{:S(2)}, u32[]{:S(2)}) collective-permute-start(bf16[2,512,256]{2,1,0:T(8,128)(2,1)S(1)} %product.13.refs_4_), channel_id=1, source_target_pairs={{0,16},{1,17},{2,18},{3,19},{4,20},{5,21},{6,22},{7,23},{8,9},{9,8... | collective-permute-start | bytes 1572872 | tf_op jit(solution)/shard_map/ppermute | solution.py:387
  45.2 17.8 %collective-permute-start.10 = (bf16[2,512,256]{2,1,0:T(8,128)(2,1)S(1)}, bf16[2,512,256]{2,1,0:T(8,128)(2,1)S(1)}, u32[]{:S(2)}, u32[]{:S(2)}) collective-permute-start(bf16[2,512,256]{2,1,0:T(8,128)(2,1)S(1)} %product.15.refs_4_), channel_id=1, source_target_pairs={{0,16},{1,17},{2,18},{3,19},{4,20},{5,21},{6,22},{7,23},{8,9},{9,8... | collective-permute-start | bytes 1572872 | tf_op jit(solution)/shard_map/ppermute | solution.py:387
  47.0 9.1 %collective-permute-start.7 = (bf16[512,256]{1,0:T(8,128)(2,1)S(1)}, bf16[512,256]{1,0:T(8,128)(2,1)S(1)}, u32[]{:S(2)}, u32[]{:S(2)}) collective-permute-start(bf16[512,256]{1,0:T(8,128)(2,1)S(1)} %get-tuple-element.31), channel_id=1, source_target_pairs={{0,1},{1,0},{2,3},{3,2},{4,5},{5,4},{6,7},{7,6},{8,24},{9,25},{10,... | collective-permute-start | bytes 786440 | tf_op jit(solution)/shard_map/ppermute | solution.py:387
  48.6 7.6 %collective-permute-start.9 = (bf16[512,256]{1,0:T(8,128)(2,1)S(1)}, bf16[512,256]{1,0:T(8,128)(2,1)S(1)}, u32[]{:S(2)}, u32[]{:S(2)}) collective-permute-start(bf16[512,256]{1,0:T(8,128)(2,1)S(1)} %add_second.5.refs_5_), channel_id=1, source_target_pairs={{0,2},{1,3},{2,0},{3,1},{4,6},{5,7},{6,4},{7,5},{8,10},{9,11},{10,... | collective-permute-start | bytes 786440 | tf_op jit(solution)/shard_map/ppermute | solution.py:387
  52.8 8.5 %collective-permute-start.13 = (bf16[512,256]{1,0:T(8,128)(2,1)S(1)}, bf16[512,256]{1,0:T(8,128)(2,1)S(1)}, u32[]{:S(2)}, u32[]{:S(2)}) collective-permute-start(bf16[512,256]{1,0:T(8,128)(2,1)S(1)} %get-tuple-element.35), channel_id=1, source_target_pairs={{0,1},{1,0},{2,3},{3,2},{4,5},{5,4},{6,7},{7,6},{8,24},{9,25},{10,... | collective-permute-start | bytes 786440 | tf_op jit(solution)/shard_map/ppermute | solution.py:387
  56.3 11.3 %collective-permute-start.11 = (bf16[512,256]{1,0:T(8,128)(2,1)S(1)}, bf16[512,256]{1,0:T(8,128)(2,1)S(1)}, u32[]{:S(2)}, u32[]{:S(2)}) collective-permute-start(bf16[512,256]{1,0:T(8,128)(2,1)S(1)} %add_second.6.refs_5_), channel_id=1, source_target_pairs={{0,4},{1,5},{2,6},{3,7},{4,0},{5,1},{6,2},{7,3},{8,12},{9,13},{10,... | collective-permute-start | bytes 786440 | tf_op jit(solution)/shard_map/ppermute | solution.py:387
  61.3 9.0 %collective-permute-start.14 = (bf16[512,256]{1,0:T(8,128)(2,1)S(1)}, bf16[512,256]{1,0:T(8,128)(2,1)S(1)}, u32[]{:S(2)}, u32[]{:S(2)}) collective-permute-start(bf16[512,256]{1,0:T(8,128)(2,1)S(1)} %add_second.7), channel_id=1, source_target_pairs={{0,2},{1,3},{2,0},{3,1},{4,6},{5,7},{6,4},{7,5},{8,10},{9,11},{10,... | collective-permute-start | bytes 786440 | tf_op jit(solution)/shard_map/ppermute | solution.py:387
  63.1 7.2 %collective-permute-start.15 = (bf16[512,256]{1,0:T(8,128)(2,1)S(1)}, bf16[512,256]{1,0:T(8,128)(2,1)S(1)}, u32[]{:S(2)}, u32[]{:S(2)}) collective-permute-start(bf16[512,256]{1,0:T(8,128)(2,1)S(1)} %get-tuple-element.36), channel_id=1, source_target_pairs={{0,1},{1,0},{2,3},{3,2},{4,5},{5,4},{6,7},{7,6},{8,24},{9,25},{10,... | collective-permute-start | bytes 786440 | tf_op jit(solution)/shard_map/ppermute | solution.py:387

commit v6 on v5

--- a/solution.py
+++ b/solution.py
@@ -268,6 +268,31 @@
         ).astype(jnp.bfloat16)
 
 
+def head_kernel(chunk, acc_in, mass_ref, turned_ref, psi_ref, *refs):
+    left_ref = refs[-1]
+    left_kernel(mass_ref, turned_ref, left_ref)
+    product_kernel(chunk, 1, acc_in, True, False, 0, left_ref, psi_ref, *refs[:-1])
+
+
+def make_head(chunk, mass, turned, psi, band, width, go, acc=()):
+    n_x, _, depth = turned.shape
+    flops = 4 * band * width * depth
+    return pl.pallas_call(
+        functools.partial(head_kernel, chunk, bool(acc)),
+        in_specs=[VMEM] * (3 + len(acc)),
+        out_specs=[VMEM] * 2,
+        out_shape=[
+            jax.ShapeDtypeStruct((2, band, width), go),
+            jax.ShapeDtypeStruct((n_x * band, depth), jnp.bfloat16),
+        ],
+        compiler_params=params(16),
+        cost_estimate=pl.CostEstimate(
+            flops=flops, bytes_accessed=flops // 512, transcendentals=0
+        ),
+        name="head",
+    )(mass, turned, psi, *acc)
+
+
 def make_left(mass, turned):
     groups, half, depth = turned.shape
     return pl.pallas_call(
@@ -408,21 +433,19 @@
     other_t, other = turn(other, n_sub)
     mass = make_far(base_mass, near, far, [own_t, other_t])
     mass_other = swap_sub(mass, 1)
-    left = make_left(mass, own_t)
 
     chunks = [(h, z) for h in range(n_sub // (2 * CORES)) for z in range(n_tile // 2)][::-1]
     goes_to = {(h, z): (h, z & (z - 1)) if z else (h & (h - 1), 0) for h, z in chunks[:-1]}
-    head = product(chunks[0], [left], [own], band, tile, go=jnp.float32)
-    left_other = make_left(mass_other, other_t)
+    head, left = make_head(chunks[0], mass, own_t, own, band, tile, jnp.float32)
+    go, left_other = make_head(
+        chunks[0], mass_other, other_t, other, band, tile, jnp.bfloat16, [head]
+    )
     lefts, psis = [left, left_other], [own, other]
 
     keep, first, second, third = {}, {}, {}, {}
     tails = {c: [] for c in chunks}
     last = len(chunks) - 1
     common = lefts, psis, band, tile
-    go, = product(
-        chunks[0], [left_other], [other], band, tile, go=jnp.bfloat16, acc=head
-    )
     for i in range(last + 1):
         first[i] = swap_first(go)
         if i < last:
@@ -438,10 +461,10 @@
             third[i - 1] = add_second(*second[i - 1], jnp.bfloat16, tails[chunk])
             tails[goes_to[chunk]].append(swap_third(third[i - 1], chunk))
     low, got = second[last]
-    early, late = tails[chunks[-1]], []
+    early, late = [got] + tails[chunks[-1]][:-1], tails[chunks[-1]][-1:]
     if early:
         low = add_second(low, early[0], jnp.float32, early[1:])
-    return add_second(low, got, jnp.float32, late)
+    return add_second(low, late[0], jnp.float32, late[1:])
 
 
 def solution(mesh):

time: 71.4 us -> 71.1 us (level)
    pallas_call x9 -> x7, Pallas kernels: 19.4 us -> 16.8 us  [product(): pl.pallas_call(functools.partial(product_kernel, chunk, len(lefts), bool(...]
    pallas_call x2, Pallas kernels: 2.51 us -> 4.87 us  [make_head(): pl.pallas_call(functools.partial(head_kernel, chunk, bool(acc)), in_specs...]
where the time goes in v6:
time: 71.1 us; the launch traced here: 70.9 us
  Pallas kernels  37.6 us (53%)
  starting transfers between devices  20.6 us (29%)
  waiting for transfers between devices  12.5 us (18%)
    ppermute x11, starting transfers between devices, swap(): return lax.ppermute(v, ('sub', 'tile'), pairs)  16.9 us
    pallas_call x7, Pallas kernels, product(): pl.pallas_call(functools.partial(product_kernel, chunk, len(lefts), bool(...  16.8 us
    ppermute x11, waiting for transfers between devices, swap(): return lax.ppermute(v, ('sub', 'tile'), pairs)  10.8 us
    pallas_call x1, Pallas kernels, make_contrib(): pl.pallas_call(functools.partial(contrib_kernel, owner_links, blk_dev, n_...  8.65 us
    pallas_call x2, Pallas kernels, make_head(): pl.pallas_call(functools.partial(head_kernel, chunk, bool(acc)), in_specs...  4.87 us
    ppermute x5, starting transfers between devices, swap_sub(): return lax.ppermute(v, 'sub', [(i, i ^ d) for i in range(n_sub)])  3.73 us
    pallas_call x1, Pallas kernels, turn(): pl.pallas_call(turn_kernel, in_specs=[ANY], out_specs=[VMEM, VMEM], out_s...  3.64 us
    ppermute x5, waiting for transfers between devices, swap_sub(): return lax.ppermute(v, 'sub', [(i, i ^ d) for i in range(n_sub)])  1.69 us
  transfers between devices with their start and end apart: 16, of which 6 were waited for; matrix products, arithmetic and copies ran while one was open for 0% of the time, Pallas kernels for 47%

profile of v6, /device:TPU:0, one launch (start us, length us, event | category | flops | bytes accessed | tf_op | source)
XLA Modules:
  0.0 70.9 jit_solution(16091357283832524140)
XLA Ops:
  0.0 0.5 collective-permute-start.3
  0.5 8.7 %contrib.1 = (bf16[528,128]{1,0:T(8,128)(2,1)}, bf16[528,128]{1,0:T(8,128)(2,1)}, bf16[528,128]{1,0:T(8,128)(2,1)}, bf16[528,128]{1,0:T(8,128)(2,1)}) custom-call(s32[4]{0:T(128)} %rows_ref.1, s32[4,8]{1,0:T(4,128)} %adj_ref.1, bf16[4,768,512]{2,1,0:T(8,128)(2,1)} %modes_ref.1, bf16[4,8,768,128]{3,2,1,0:T(8,128)(2,1)} %coup_ref.1, f32[4,512]{1,0:T(4,128)} %inv_ref.1), custom_call_target="tpu_custom_call" | custom-call | flops 1 | bytes 1 | tf_op jit(solution)/shard_map/contrib/pallas_call | solution.py:121
  9.1 0.4 collective-permute-start
  9.5 2.6 %collective-permute-start.1 = (bf16[528,128]{1,0:T(8,128)(2,1)}, bf16[528,128]{1,0:T(8,128)(2,1)S(1)}, u32[]{:S(2)}, u32[]{:S(2)}) collective-permute-start(bf16[528,128]{1,0:T(8,128)(2,1)} %get-tuple-element.29), channel_id=1, source_target_pairs={{0,16},{8,24},{16,0},{24,8},{1,17},{9,25},{17,1},{25,9},{2,18},{10... | collective-permute-start | bytes 405512 | tf_op jit(solution)/shard_map/ppermute | solution.py:404
  12.2 0.0 collective-permute-start.2
  12.2 1.3 %turn_own.1.rest_2_.turned_ref = bf16[2,512,2048]{2,1,0:T(8,128)(2,1)S(1)} custom-call(bf16[2048,2048]{1,0:T(8,128)(2,1)S(1)} %copy-done), custom_call_target="tpu_custom_call" | custom-call | flops 1 | bytes 1 | tf_op jit(solution)/shard_map/turn_own/pallas_call | solution.py:241
  13.4 0.2 collective-permute-done.pair_ref
  13.6 0.2 near.1
  13.9 0.0 copy-start.1
  13.9 0.0 collective-permute-done.3.psi_ref
  13.9 3.6 %turn.1 = (bf16[2,512,2048]{2,1,0:T(8,128)(2,1)S(1)}, bf16[2048,2048]{1,0:T(8,128)(2,1)S(1)}) custom-call(bf16[2048,2048]{1,0:T(8,128)(2,1)} %collective-permute-done.3.psi_ref), custom_call_target="tpu_custom_call" | custom-call | flops 1 | bytes 1 | tf_op jit(solution)/shard_map/turn/pallas_call | solution.py:218
  17.5 0.0 collective-permute-done.1.rest_0_
  17.5 1.5 %collective-permute-done.2.rest_1_ = bf16[528,128]{1,0:T(8,128)(2,1)S(1)} collective-permute-done((bf16[528,128]{1,0:T(8,128)(2,1)}, bf16[528,128]{1,0:T(8,128)(2,1)S(1)}, u32[]{:S(2)}, u32[]{:S(2)}) %collective-permute-start.2) | collective-permute-done | bytes 135200 | tf_op jit(solution)/shard_map/ppermute | solution.py:404
  19.0 0.7 %far.1.mass_ref = bf16[16,128,128]{2,1,0:T(8,128)(2,1)S(1)} custom-call(f32[16,128,128]{2,1,0:T(8,128)S(1)} %copy-done.1, f32[17,64,128]{2,1,0:T(8,128)S(1)} %get-tuple-element.27.near_ref, f32[17,1,128]{2,1,0:T(1,128)S(1)} %get-tuple-element.28.near_side_ref, bf16[528,128]{1,0:T(8,128)(2,1)S(1)} %collective-permute-done.1.rest_0_, ...), custom_call_target="tpu_custom_call" | custom-call | flops 1 | bytes 1 | tf_op jit(solution)/shard_map/far/pallas_call | solution.py:186
  19.7 0.2 collective-permute-start.4
  20.0 2.4 %head.2 = (f32[2,512,256]{2,1,0:T(8,128)S(1)}, bf16[1024,2048]{1,0:T(8,128)(2,1)S(1)}) custom-call(bf16[16,128,128]{2,1,0:T(8,128)(2,1)S(1)} %far.1.mass_ref, bf16[2,512,2048]{2,1,0:T(8,128)(2,1)S(1)} %turn_own.1.rest_2_.turned_ref, bf16[2048,2048]{1,0:T(8,128)(2,1)S(1)} %copy-done), custom_call_target="tpu_custom_call" | custom-call | flops 1073741824 | bytes 2097152 | tf_op jit(solution)/shard_map/head/pallas_call | solution.py:280
  22.4 2.4 %head.3 = (bf16[2,512,256]{2,1,0:T(8,128)(2,1)S(1)}, bf16[1024,2048]{1,0:T(8,128)(2,1)S(1)}) custom-call(bf16[16,128,128]{2,1,0:T(8,128)(2,1)S(1)} %collective-permute-done.4.mass_ref, bf16[2,512,2048]{2,1,0:T(8,128)(2,1)S(1)} %get-tuple-element.31.rest_3_.turned_ref, bf16[2048,2048]{1,0:T(8,128)(2,1)S(1)} %get-tuple-element.33.psi_ref.refs_3_, ...), custom_call_target="tpu_custom_call" | custom-call | flops 1073741824 | bytes 2097152 | tf_op jit(solution)/shard_map/head/pallas_call | solution.py:280
  24.9 1.8 %collective-permute-start.5 = (bf16[2,512,256]{2,1,0:T(8,128)(2,1)S(1)}, bf16[2,512,256]{2,1,0:T(8,128)(2,1)S(1)}, u32[]{:S(2)}, u32[]{:S(2)}) collective-permute-start(bf16[2,512,256]{2,1,0:T(8,128)(2,1)S(1)} %get-tuple-element.36.refs_4_), channel_id=1, source_target_pairs={{0,16},{1,17},{2,18},{3,19},{4,20},{5,21},{6,22},{7,23},{8,9},{9,8... | collective-permute-start | bytes 1572872 | tf_op jit(solution)/shard_map/ppermute | solution.py:412
  26.7 2.4 %product.7.refs_4_ = bf16[2,512,256]{2,1,0:T(8,128)(2,1)S(1)} custom-call(bf16[1024,2048]{1,0:T(8,128)(2,1)S(1)} %get-tuple-element.32.refs_0_, bf16[1024,2048]{1,0:T(8,128)(2,1)S(1)} %get-tuple-element.35.refs_1_, bf16[2048,2048]{1,0:T(8,128)(2,1)S(1)} %copy-done, bf16[2048,2048]{1,0:T(8,128)(2,1)S(1)} %get-tuple-element.33.psi_ref.refs_3_, ...), custom_call_target="tpu_custom_call" | custom-call | flops 2147483648 | bytes 4194304 | tf_op jit(solution)/shard_map/product/pallas_call | solution.py:343
  29.0 0.3 collective-permute-start.6
  29.4 2.4 %product.8.keep_ref = f32[2,512,256]{2,1,0:T(8,128)S(1)} custom-call(bf16[1024,2048]{1,0:T(8,128)(2,1)S(1)} %get-tuple-element.32.refs_0_, bf16[1024,2048]{1,0:T(8,128)(2,1)S(1)} %get-tuple-element.35.refs_1_, bf16[2048,2048]{1,0:T(8,128)(2,1)S(1)} %copy-done, bf16[2048,2048]{1,0:T(8,128)(2,1)S(1)} %get-tuple-element.33.psi_ref.refs_3_, ...), custom_call_target="tpu_custom_call" | custom-call | flops 2147483648 | bytes 4194304 | tf_op jit(solution)/shard_map/product/pallas_call | solution.py:343
  31.8 2.3 %collective-permute-done.5.got_ref = bf16[2,512,256]{2,1,0:T(8,128)(2,1)S(1)} collective-permute-done((bf16[2,512,256]{2,1,0:T(8,128)(2,1)S(1)}, bf16[2,512,256]{2,1,0:T(8,128)(2,1)S(1)}, u32[]{:S(2)}, u32[]{:S(2)}) %collective-permute-start.5) | collective-permute-done | bytes 524320 | tf_op jit(solution)/shard_map/ppermute | solution.py:412
  34.1 0.1 add_first.4
  34.2 1.8 %collective-permute-start.8 = (bf16[512,256]{1,0:T(8,128)(2,1)S(1)}, bf16[512,256]{1,0:T(8,128)(2,1)S(1)}, u32[]{:S(2)}, u32[]{:S(2)}) collective-permute-start(bf16[512,256]{1,0:T(8,128)(2,1)S(1)} %get-tuple-element.40), channel_id=1, source_target_pairs={{0,1},{1,0},{2,3},{3,2},{4,5},{5,4},{6,7},{7,6},{8,24},{9,25},{10,... | collective-permute-start | bytes 786440 | tf_op jit(solution)/shard_map/ppermute | solution.py:412
  36.0 2.6 %product.9.refs_4_ = bf16[2,512,256]{2,1,0:T(8,128)(2,1)S(1)} custom-call(bf16[1024,2048]{1,0:T(8,128)(2,1)S(1)} %get-tuple-element.32.refs_0_, bf16[1024,2048]{1,0:T(8,128)(2,1)S(1)} %get-tuple-element.35.refs_1_, bf16[2048,2048]{1,0:T(8,128)(2,1)S(1)} %copy-done, bf16[2048,2048]{1,0:T(8,128)(2,1)S(1)} %get-tuple-element.33.psi_ref.refs_3_, ...), custom_call_target="tpu_custom_call" | custom-call | flops 2147483648 | bytes 4194304 | tf_op jit(solution)/shard_map/product/pallas_call | solution.py:343
  38.6 1.6 %collective-permute-start.13 = (bf16[2,512,256]{2,1,0:T(8,128)(2,1)S(1)}, bf16[2,512,256]{2,1,0:T(8,128)(2,1)S(1)}, u32[]{:S(2)}, u32[]{:S(2)}) collective-permute-start(bf16[2,512,256]{2,1,0:T(8,128)(2,1)S(1)} %product.9.refs_4_), channel_id=1, source_target_pairs={{0,16},{1,17},{2,18},{3,19},{4,20},{5,21},{6,22},{7,23},{8,9},{9,8... | collective-permute-start | bytes 1572872 | tf_op jit(solution)/shard_map/ppermute | solution.py:412
  40.2 2.4 %product.10.keep_ref = f32[2,512,256]{2,1,0:T(8,128)S(1)} custom-call(bf16[1024,2048]{1,0:T(8,128)(2,1)S(1)} %get-tuple-element.32.refs_0_, bf16[1024,2048]{1,0:T(8,128)(2,1)S(1)} %get-tuple-element.35.refs_1_, bf16[2048,2048]{1,0:T(8,128)(2,1)S(1)} %copy-done, bf16[2048,2048]{1,0:T(8,128)(2,1)S(1)} %get-tuple-element.33.psi_ref.refs_3_, ...), custom_call_target="tpu_custom_call" | custom-call | flops 2147483648 | bytes 4194304 | tf_op jit(solution)/shard_map/product/pallas_call | solution.py:343
  42.6 0.1 add_first.5
  42.7 2.4 %product.11.refs_4_ = bf16[2,512,256]{2,1,0:T(8,128)(2,1)S(1)} custom-call(bf16[1024,2048]{1,0:T(8,128)(2,1)S(1)} %get-tuple-element.32.refs_0_, bf16[1024,2048]{1,0:T(8,128)(2,1)S(1)} %get-tuple-element.35.refs_1_, bf16[2048,2048]{1,0:T(8,128)(2,1)S(1)} %copy-done, bf16[2048,2048]{1,0:T(8,128)(2,1)S(1)} %get-tuple-element.33.psi_ref.refs_3_, ...), custom_call_target="tpu_custom_call" | custom-call | flops 2147483648 | bytes 4194304 | tf_op jit(solution)/shard_map/product/pallas_call | solution.py:343
  45.1 1.8 %collective-permute-start.10 = (bf16[2,512,256]{2,1,0:T(8,128)(2,1)S(1)}, bf16[2,512,256]{2,1,0:T(8,128)(2,1)S(1)}, u32[]{:S(2)}, u32[]{:S(2)}) collective-permute-start(bf16[2,512,256]{2,1,0:T(8,128)(2,1)S(1)} %product.11.refs_4_), channel_id=1, source_target_pairs={{0,16},{1,17},{2,18},{3,19},{4,20},{5,21},{6,22},{7,23},{8,9},{9,8... | collective-permute-start | bytes 1572872 | tf_op jit(solution)/shard_map/ppermute | solution.py:412
  46.8 1.5 %collective-permute-start.7 = (bf16[512,256]{1,0:T(8,128)(2,1)S(1)}, bf16[512,256]{1,0:T(8,128)(2,1)S(1)}, u32[]{:S(2)}, u32[]{:S(2)}) collective-permute-start(bf16[512,256]{1,0:T(8,128)(2,1)S(1)} %get-tuple-element.39), channel_id=1, source_target_pairs={{0,1},{1,0},{2,3},{3,2},{4,5},{5,4},{6,7},{7,6},{8,24},{9,25},{10,... | collective-permute-start | bytes 786440 | tf_op jit(solution)/shard_map/ppermute | solution.py:412
  48.4 0.0 collective-permute-done.8.got_ref
  48.4 1.6 %collective-permute-start.9 = (bf16[512,256]{1,0:T(8,128)(2,1)S(1)}, bf16[512,256]{1,0:T(8,128)(2,1)S(1)}, u32[]{:S(2)}, u32[]{:S(2)}) collective-permute-start(bf16[512,256]{1,0:T(8,128)(2,1)S(1)} %add_second.5.refs_5_), channel_id=1, source_target_pairs={{0,2},{1,3},{2,0},{3,1},{4,6},{5,7},{6,4},{7,5},{8,10},{9,11},{10,... | collective-permute-start | bytes 786440 | tf_op jit(solution)/shard_map/ppermute | solution.py:412
  50.0 2.4 %product.13.keep_ref = f32[2,512,256]{2,1,0:T(8,128)S(1)} custom-call(bf16[1024,2048]{1,0:T(8,128)(2,1)S(1)} %get-tuple-element.32.refs_0_, bf16[1024,2048]{1,0:T(8,128)(2,1)S(1)} %get-tuple-element.35.refs_1_, bf16[2048,2048]{1,0:T(8,128)(2,1)S(1)} %copy-done, bf16[2048,2048]{1,0:T(8,128)(2,1)S(1)} %get-tuple-element.33.psi_ref.refs_3_, ...), custom_call_target="tpu_custom_call" | custom-call | flops 2147483648 | bytes 4194304 | tf_op jit(solution)/shard_map/product/pallas_call | solution.py:343
  52.4 0.1 add_first.7
  52.5 0.6 collective-permute-start.14
  53.1 2.9 %collective-permute-done.7.got_ref = bf16[512,256]{1,0:T(8,128)(2,1)S(1)} collective-permute-done((bf16[512,256]{1,0:T(8,128)(2,1)S(1)}, bf16[512,256]{1,0:T(8,128)(2,1)S(1)}, u32[]{:S(2)}, u32[]{:S(2)}) %collective-permute-start.7) | collective-permute-done | bytes 262176 | tf_op jit(solution)/shard_map/ppermute | solution.py:412
  56.0 0.1 add_second.6.refs_5_
  56.0 2.6 %collective-permute-start.12 = (bf16[512,256]{1,0:T(8,128)(2,1)S(1)}, bf16[512,256]{1,0:T(8,128)(2,1)S(1)}, u32[]{:S(2)}, u32[]{:S(2)}) collective-permute-start(bf16[512,256]{1,0:T(8,128)(2,1)S(1)} %add_second.6.refs_5_), channel_id=1, source_target_pairs={{0,4},{1,5},{2,6},{3,7},{4,0},{5,1},{6,2},{7,3},{8,12},{9,13},{10,... | collective-permute-start | bytes 786440 | tf_op jit(solution)/shard_map/ppermute | solution.py:412
  58.7 2.4 %product.12.keep_ref = f32[2,512,256]{2,1,0:T(8,128)S(1)} custom-call(bf16[1024,2048]{1,0:T(8,128)(2,1)S(1)} %get-tuple-element.32.refs_0_, bf16[1024,2048]{1,0:T(8,128)(2,1)S(1)} %get-tuple-element.35.refs_1_, bf16[2048,2048]{1,0:T(8,128)(2,1)S(1)} %copy-done, bf16[2048,2048]{1,0:T(8,128)(2,1)S(1)} %get-tuple-element.33.psi_ref.refs_3_, ...), custom_call_target="tpu_custom_call" | custom-call | flops 2147483648 | bytes 4194304 | tf_op jit(solution)/shard_map/product/pallas_call | solution.py:343
  61.1 0.0 collective-permute-done.10.got_ref
  61.1 0.1 add_first.6
  61.2 1.6 %collective-permute-start.11 = (bf16[512,256]{1,0:T(8,128)(2,1)S(1)}, bf16[512,256]{1,0:T(8,128)(2,1)S(1)}, u32[]{:S(2)}, u32[]{:S(2)}) collective-permute-start(bf16[512,256]{1,0:T(8,128)(2,1)S(1)} %get-tuple-element.42), channel_id=1, source_target_pairs={{0,1},{1,0},{2,3},{3,2},{4,5},{5,4},{6,7},{7,6},{8,24},{9,25},{10,... | collective-permute-start | bytes 786440 | tf_op jit(solution)/shard_map/ppermute | solution.py:412
  62.8 1.6 %collective-permute-start.15 = (bf16[512,256]{1,0:T(8,128)(2,1)S(1)}, bf16[512,256]{1,0:T(8,128)(2,1)S(1)}, u32[]{:S(2)}, u32[]{:S(2)}) collective-permute-start(bf16[512,256]{1,0:T(8,128)(2,1)S(1)} %add_second.8), channel_id=1, source_target_pairs={{0,2},{1,3},{2,0},{3,1},{4,6},{5,7},{6,4},{7,5},{8,10},{9,11},{10,... | collective-permute-start | bytes 786440 | tf_op jit(solution)/shard_map/ppermute | solution.py:412
  64.4 3.2 %collective-permute-done.11.got_ref = bf16[512,256]{1,0:T(8,128)(2,1)S(1)} collective-permute-done((bf16[512,256]{1,0:T(8,128)(2,1)S(1)}, bf16[512,256]{1,0:T(8,128)(2,1)S(1)}, u32[]{:S(2)}, u32[]{:S(2)}) %collective-permute-start.11) | collective-permute-done | bytes 262176 | tf_op jit(solution)/shard_map/ppermute | solution.py:412
  67.6 0.1 add_second.7.low_ref
  67.7 2.4 %collective-permute-done.15.got_ref = bf16[512,256]{1,0:T(8,128)(2,1)S(1)} collective-permute-done((bf16[512,256]{1,0:T(8,128)(2,1)S(1)}, bf16[512,256]{1,0:T(8,128)(2,1)S(1)}, u32[]{:S(2)}, u32[]{:S(2)}) %collective-permute-start.15) | collective-permute-done | bytes 262176 | tf_op jit(solution)/shard_map/ppermute | solution.py:412
  70.1 0.8 %add_second.9 = f32[512,256]{1,0:T(8,128)} custom-call(f32[512,256]{1,0:T(8,128)S(1)} %add_second.7.low_ref, bf16[512,256]{1,0:T(8,128)(2,1)S(1)} %collective-permute-done.15.got_ref), custom_call_target="tpu_custom_call" | custom-call | flops 1 | bytes 1 | tf_op jit(solution)/shard_map/add_second/pallas_call | solution.py:385
  (13 shorter events, 0.1 us)
Async XLA Ops:
  0.0 12.2 %copy-start = (bf16[2048,2048]{1,0:T(8,128)(2,1)S(1)}, bf16[2048,2048]{1,0:T(8,128)(2,1)}, u32[]{:S(2)}) copy-start(bf16[2048,2048]{1,0:T(8,128)(2,1)} %refs_2_.13) | copy-start | bytes 25165828
  0.0 13.9 %collective-permute-start.3 = (bf16[2048,2048]{1,0:T(8,128)(2,1)}, bf16[2048,2048]{1,0:T(8,128)(2,1)}, u32[]{:S(2)}, u32[]{:S(2)}) collective-permute-start(bf16[2048,2048]{1,0:T(8,128)(2,1)} %refs_2_.13), channel_id=1, source_target_pairs={{0,8},{8,0},{16,24},{24,16},{1,9},{9,1},{17,25},{25,17},{2,10},{10... | collective-permute-start | bytes 25165832 | tf_op jit(solution)/shard_map/ppermute | solution.py:404
  9.1 4.5 %collective-permute-start = (bf16[528,128]{1,0:T(8,128)(2,1)}, bf16[528,128]{1,0:T(8,128)(2,1)S(1)}, u32[]{:S(2)}, u32[]{:S(2)}) collective-permute-start(bf16[528,128]{1,0:T(8,128)(2,1)} %get-tuple-element.26), channel_id=1, source_target_pairs={{0,8},{8,0},{16,24},{24,16},{1,9},{9,1},{17,25},{25,17},{2,10},{10... | collective-permute-start | bytes 405512 | tf_op jit(solution)/shard_map/ppermute | solution.py:404
  9.5 8.0 %collective-permute-start.1 = (bf16[528,128]{1,0:T(8,128)(2,1)}, bf16[528,128]{1,0:T(8,128)(2,1)S(1)}, u32[]{:S(2)}, u32[]{:S(2)}) collective-permute-start(bf16[528,128]{1,0:T(8,128)(2,1)} %get-tuple-element.29), channel_id=1, source_target_pairs={{0,16},{8,24},{16,0},{24,8},{1,17},{9,25},{17,1},{25,9},{2,18},{10... | collective-permute-start | bytes 405512 | tf_op jit(solution)/shard_map/ppermute | solution.py:404
  12.2 1.5 %copy-start.2 = (bf16[528,128]{1,0:T(8,128)(2,1)S(1)}, bf16[528,128]{1,0:T(8,128)(2,1)}, u32[]{:S(2)}) copy-start(bf16[528,128]{1,0:T(8,128)(2,1)} %get-tuple-element.25.own_ref) | copy-start | bytes 405508
  12.2 6.8 %collective-permute-start.2 = (bf16[528,128]{1,0:T(8,128)(2,1)}, bf16[528,128]{1,0:T(8,128)(2,1)S(1)}, u32[]{:S(2)}, u32[]{:S(2)}) collective-permute-start(bf16[528,128]{1,0:T(8,128)(2,1)} %get-tuple-element.30), channel_id=1, source_target_pairs={{0,24},{8,16},{16,8},{24,0},{1,25},{9,17},{17,9},{25,1},{2,26},{10... | collective-permute-start | bytes 405512 | tf_op jit(solution)/shard_map/ppermute | solution.py:404
  13.9 5.1 %copy-start.1 = (f32[16,128,128]{2,1,0:T(8,128)S(1)}, f32[16,128,128]{2,1,0:T(8,128)}, u32[]{:S(2)}) copy-start(f32[16,128,128]{2,1,0:T(8,128)} %base_ref.1) | copy-start | bytes 3145732
  19.7 2.7 %collective-permute-start.4 = (bf16[16,128,128]{2,1,0:T(8,128)(2,1)S(1)}, bf16[16,128,128]{2,1,0:T(8,128)(2,1)S(1)}, u32[]{:S(2)}, u32[]{:S(2)}) collective-permute-start(bf16[16,128,128]{2,1,0:T(8,128)(2,1)S(1)} %far.1.mass_ref), channel_id=1, source_target_pairs={{0,8},{8,0},{16,24},{24,16},{1,9},{9,1},{17,25},{25,17},{2,10},{10... | collective-permute-start | bytes 1572872 | tf_op jit(solution)/shard_map/ppermute | solution.py:404
  24.9 9.2 %collective-permute-start.5 = (bf16[2,512,256]{2,1,0:T(8,128)(2,1)S(1)}, bf16[2,512,256]{2,1,0:T(8,128)(2,1)S(1)}, u32[]{:S(2)}, u32[]{:S(2)}) collective-permute-start(bf16[2,512,256]{2,1,0:T(8,128)(2,1)S(1)} %get-tuple-element.36.refs_4_), channel_id=1, source_target_pairs={{0,16},{1,17},{2,18},{3,19},{4,20},{5,21},{6,22},{7,23},{8,9},{9,8... | collective-permute-start | bytes 1572872 | tf_op jit(solution)/shard_map/ppermute | solution.py:412
  29.0 13.5 %collective-permute-start.6 = (bf16[2,512,256]{2,1,0:T(8,128)(2,1)S(1)}, bf16[2,512,256]{2,1,0:T(8,128)(2,1)S(1)}, u32[]{:S(2)}, u32[]{:S(2)}) collective-permute-start(bf16[2,512,256]{2,1,0:T(8,128)(2,1)S(1)} %product.7.refs_4_), channel_id=1, source_target_pairs={{0,16},{1,17},{2,18},{3,19},{4,20},{5,21},{6,22},{7,23},{8,9},{9,8... | collective-permute-start | bytes 1572872 | tf_op jit(solution)/shard_map/ppermute | solution.py:412
  34.2 14.2 %collective-permute-start.8 = (bf16[512,256]{1,0:T(8,128)(2,1)S(1)}, bf16[512,256]{1,0:T(8,128)(2,1)S(1)}, u32[]{:S(2)}, u32[]{:S(2)}) collective-permute-start(bf16[512,256]{1,0:T(8,128)(2,1)S(1)} %get-tuple-element.40), channel_id=1, source_target_pairs={{0,1},{1,0},{2,3},{3,2},{4,5},{5,4},{6,7},{7,6},{8,24},{9,25},{10,... | collective-permute-start | bytes 786440 | tf_op jit(solution)/shard_map/ppermute | solution.py:412
  38.6 13.8 %collective-permute-start.13 = (bf16[2,512,256]{2,1,0:T(8,128)(2,1)S(1)}, bf16[2,512,256]{2,1,0:T(8,128)(2,1)S(1)}, u32[]{:S(2)}, u32[]{:S(2)}) collective-permute-start(bf16[2,512,256]{2,1,0:T(8,128)(2,1)S(1)} %product.9.refs_4_), channel_id=1, source_target_pairs={{0,16},{1,17},{2,18},{3,19},{4,20},{5,21},{6,22},{7,23},{8,9},{9,8... | collective-permute-start | bytes 1572872 | tf_op jit(solution)/shard_map/ppermute | solution.py:412
  45.1 16.0 %collective-permute-start.10 = (bf16[2,512,256]{2,1,0:T(8,128)(2,1)S(1)}, bf16[2,512,256]{2,1,0:T(8,128)(2,1)S(1)}, u32[]{:S(2)}, u32[]{:S(2)}) collective-permute-start(bf16[2,512,256]{2,1,0:T(8,128)(2,1)S(1)} %product.11.refs_4_), channel_id=1, source_target_pairs={{0,16},{1,17},{2,18},{3,19},{4,20},{5,21},{6,22},{7,23},{8,9},{9,8... | collective-permute-start | bytes 1572872 | tf_op jit(solution)/shard_map/ppermute | solution.py:412
  46.8 9.1 %collective-permute-start.7 = (bf16[512,256]{1,0:T(8,128)(2,1)S(1)}, bf16[512,256]{1,0:T(8,128)(2,1)S(1)}, u32[]{:S(2)}, u32[]{:S(2)}) collective-permute-start(bf16[512,256]{1,0:T(8,128)(2,1)S(1)} %get-tuple-element.39), channel_id=1, source_target_pairs={{0,1},{1,0},{2,3},{3,2},{4,5},{5,4},{6,7},{7,6},{8,24},{9,25},{10,... | collective-permute-start | bytes 786440 | tf_op jit(solution)/shard_map/ppermute | solution.py:412
  48.4 7.5 %collective-permute-start.9 = (bf16[512,256]{1,0:T(8,128)(2,1)S(1)}, bf16[512,256]{1,0:T(8,128)(2,1)S(1)}, u32[]{:S(2)}, u32[]{:S(2)}) collective-permute-start(bf16[512,256]{1,0:T(8,128)(2,1)S(1)} %add_second.5.refs_5_), channel_id=1, source_target_pairs={{0,2},{1,3},{2,0},{3,1},{4,6},{5,7},{6,4},{7,5},{8,10},{9,11},{10,... | collective-permute-start | bytes 786440 | tf_op jit(solution)/shard_map/ppermute | solution.py:412
  52.5 10.2 %collective-permute-start.14 = (bf16[512,256]{1,0:T(8,128)(2,1)S(1)}, bf16[512,256]{1,0:T(8,128)(2,1)S(1)}, u32[]{:S(2)}, u32[]{:S(2)}) collective-permute-start(bf16[512,256]{1,0:T(8,128)(2,1)S(1)} %get-tuple-element.44), channel_id=1, source_target_pairs={{0,1},{1,0},{2,3},{3,2},{4,5},{5,4},{6,7},{7,6},{8,24},{9,25},{10,... | collective-permute-start | bytes 786440 | tf_op jit(solution)/shard_map/ppermute | solution.py:412
  56.0 11.6 %collective-permute-start.12 = (bf16[512,256]{1,0:T(8,128)(2,1)S(1)}, bf16[512,256]{1,0:T(8,128)(2,1)S(1)}, u32[]{:S(2)}, u32[]{:S(2)}) collective-permute-start(bf16[512,256]{1,0:T(8,128)(2,1)S(1)} %add_second.6.refs_5_), channel_id=1, source_target_pairs={{0,4},{1,5},{2,6},{3,7},{4,0},{5,1},{6,2},{7,3},{8,12},{9,13},{10,... | collective-permute-start | bytes 786440 | tf_op jit(solution)/shard_map/ppermute | solution.py:412
  61.2 6.4 %collective-permute-start.11 = (bf16[512,256]{1,0:T(8,128)(2,1)S(1)}, bf16[512,256]{1,0:T(8,128)(2,1)S(1)}, u32[]{:S(2)}, u32[]{:S(2)}) collective-permute-start(bf16[512,256]{1,0:T(8,128)(2,1)S(1)} %get-tuple-element.42), channel_id=1, source_target_pairs={{0,1},{1,0},{2,3},{3,2},{4,5},{5,4},{6,7},{7,6},{8,24},{9,25},{10,... | collective-permute-start | bytes 786440 | tf_op jit(solution)/shard_map/ppermute | solution.py:412
  62.8 7.3 %collective-permute-start.15 = (bf16[512,256]{1,0:T(8,128)(2,1)S(1)}, bf16[512,256]{1,0:T(8,128)(2,1)S(1)}, u32[]{:S(2)}, u32[]{:S(2)}) collective-permute-start(bf16[512,256]{1,0:T(8,128)(2,1)S(1)} %add_second.8), channel_id=1, source_target_pairs={{0,2},{1,3},{2,0},{3,1},{4,6},{5,7},{6,4},{7,5},{8,10},{9,11},{10,... | collective-permute-start | bytes 786440 | tf_op jit(solution)/shard_map/ppermute | solution.py:412

commit v7 on v6

--- a/solution.py
+++ b/solution.py
@@ -393,6 +393,36 @@
     )(low, got, *tails)
 
 
+def last_kernel(low_ref, *refs):
+    tails, (out_ref, held_ref, sems) = refs[:-3], refs[-3:]
+    pieces = sems.shape[0]
+    rows = low_ref.shape[0] // pieces
+    copies = []
+    for i in range(pieces):
+        here = pl.ds(i * rows, rows)
+        total = low_ref[here]
+        for v in tails:
+            total += v[here].astype(jnp.float32)
+        held_ref[here] = total
+        copies.append(pltpu.make_async_copy(held_ref.at[here], out_ref.at[here], sems.at[i]))
+        copies[-1].start()
+    for copy in copies:
+        copy.wait()
+
+
+def add_last(low, tails):
+    return pl.pallas_call(
+        last_kernel,
+        in_specs=[VMEM] * (1 + len(tails)),
+        out_specs=ANY,
+        out_shape=jax.ShapeDtypeStruct(low.shape, jnp.float32),
+        scratch_shapes=[pltpu.VMEM(low.shape, jnp.float32), pltpu.SemaphoreType.DMA((4,))],
+        compiler_params=params(12),
+        cost_estimate=cheap(),
+        name="add_last",
+    )(low, *tails)
+
+
 def on_device(modes, coupling, inv_eig, sub_rows, adjacency, base_mass, iface_modes):
     n_sub = lax.axis_size("sub")
     n_tile = lax.axis_size("tile")
@@ -464,7 +494,7 @@
     early, late = [got] + tails[chunks[-1]][:-1], tails[chunks[-1]][-1:]
     if early:
         low = add_second(low, early[0], jnp.float32, early[1:])
-    return add_second(low, late[0], jnp.float32, late[1:])
+    return add_last(low, late)
 
 
 def solution(mesh):

time: 71.1 us -> 71.2 us (level)
    pallas_call x5 -> x4, Pallas kernels: 1.08 us -> 0.24 us  [add_second(): pl.pallas_call(second_kernel, in_specs=[VMEM] * (2 + len(tails)), out_spe...]
    pallas_call x0 -> x1, Pallas kernels: none -> 0.83 us  [add_last(): pl.pallas_call(last_kernel, in_specs=[VMEM] * (1 + len(tails)), out_specs...]
where the time goes in v7:
time: 71.2 us; the launch traced here: 71.1 us
  Pallas kernels  37.6 us (53%)
  starting transfers between devices  20.6 us (29%)
  waiting for transfers between devices  12.5 us (18%)
    ppermute x11, starting transfers between devices, swap(): return lax.ppermute(v, ('sub', 'tile'), pairs)  16.9 us
    pallas_call x7, Pallas kernels, product(): pl.pallas_call(functools.partial(product_kernel, chunk, len(lefts), bool(...  16.8 us
    ppermute x11, waiting for transfers between devices, swap(): return lax.ppermute(v, ('sub', 'tile'), pairs)  10.8 us
    pallas_call x1, Pallas kernels, make_contrib(): pl.pallas_call(functools.partial(contrib_kernel, owner_links, blk_dev, n_...  8.65 us
    pallas_call x2, Pallas kernels, make_head(): pl.pallas_call(functools.partial(head_kernel, chunk, bool(acc)), in_specs...  4.87 us
    ppermute x5, starting transfers between devices, swap_sub(): return lax.ppermute(v, 'sub', [(i, i ^ d) for i in range(n_sub)])  3.73 us
    pallas_call x1, Pallas kernels, turn(): pl.pallas_call(turn_kernel, in_specs=[ANY], out_specs=[VMEM, VMEM], out_s...  3.64 us
    ppermute x5, waiting for transfers between devices, swap_sub(): return lax.ppermute(v, 'sub', [(i, i ^ d) for i in range(n_sub)])  1.69 us
  transfers between devices with their start and end apart: 16, of which 6 were waited for; matrix products, arithmetic and copies ran while one was open for 0% of the time, Pallas kernels for 47%

profile of v7, /device:TPU:0, one launch (start us, length us, event | category | flops | bytes accessed | tf_op | source)
XLA Modules:
  0.0 71.1 jit_solution(3045134973674753942)
XLA Ops:
  0.0 0.5 collective-permute-start.3
  0.5 8.7 %contrib.1 = (bf16[528,128]{1,0:T(8,128)(2,1)}, bf16[528,128]{1,0:T(8,128)(2,1)}, bf16[528,128]{1,0:T(8,128)(2,1)}, bf16[528,128]{1,0:T(8,128)(2,1)}) custom-call(s32[4]{0:T(128)} %rows_ref.1, s32[4,8]{1,0:T(4,128)} %adj_ref.1, bf16[4,768,512]{2,1,0:T(8,128)(2,1)} %modes_ref.1, bf16[4,8,768,128]{3,2,1,0:T(8,128)(2,1)} %coup_ref.1, f32[4,512]{1,0:T(4,128)} %inv_ref.1), custom_call_target="tpu_custom_call" | custom-call | flops 1 | bytes 1 | tf_op jit(solution)/shard_map/contrib/pallas_call | solution.py:121
  9.1 0.4 collective-permute-start
  9.5 2.6 %collective-permute-start.1 = (bf16[528,128]{1,0:T(8,128)(2,1)}, bf16[528,128]{1,0:T(8,128)(2,1)S(1)}, u32[]{:S(2)}, u32[]{:S(2)}) collective-permute-start(bf16[528,128]{1,0:T(8,128)(2,1)} %get-tuple-element.29), channel_id=1, source_target_pairs={{0,16},{8,24},{16,0},{24,8},{1,17},{9,25},{17,1},{25,9},{2,18},{10... | collective-permute-start | bytes 405512 | tf_op jit(solution)/shard_map/ppermute | solution.py:434
  12.2 0.0 collective-permute-start.2
  12.2 1.3 %turn_own.1.rest_2_.turned_ref = bf16[2,512,2048]{2,1,0:T(8,128)(2,1)S(1)} custom-call(bf16[2048,2048]{1,0:T(8,128)(2,1)S(1)} %copy-done), custom_call_target="tpu_custom_call" | custom-call | flops 1 | bytes 1 | tf_op jit(solution)/shard_map/turn_own/pallas_call | solution.py:241
  13.4 0.2 collective-permute-done.pair_ref
  13.6 0.2 near.1
  13.9 0.0 copy-start.1
  13.9 0.0 collective-permute-done.3.psi_ref
  13.9 3.6 %turn.1 = (bf16[2,512,2048]{2,1,0:T(8,128)(2,1)S(1)}, bf16[2048,2048]{1,0:T(8,128)(2,1)S(1)}) custom-call(bf16[2048,2048]{1,0:T(8,128)(2,1)} %collective-permute-done.3.psi_ref), custom_call_target="tpu_custom_call" | custom-call | flops 1 | bytes 1 | tf_op jit(solution)/shard_map/turn/pallas_call | solution.py:218
  17.5 0.0 collective-permute-done.1.rest_0_
  17.5 1.5 %collective-permute-done.2.rest_1_ = bf16[528,128]{1,0:T(8,128)(2,1)S(1)} collective-permute-done((bf16[528,128]{1,0:T(8,128)(2,1)}, bf16[528,128]{1,0:T(8,128)(2,1)S(1)}, u32[]{:S(2)}, u32[]{:S(2)}) %collective-permute-start.2) | collective-permute-done | bytes 135200 | tf_op jit(solution)/shard_map/ppermute | solution.py:434
  19.0 0.7 %far.1.mass_ref = bf16[16,128,128]{2,1,0:T(8,128)(2,1)S(1)} custom-call(f32[16,128,128]{2,1,0:T(8,128)S(1)} %copy-done.1, f32[17,64,128]{2,1,0:T(8,128)S(1)} %get-tuple-element.27.near_ref, f32[17,1,128]{2,1,0:T(1,128)S(1)} %get-tuple-element.28.near_side_ref, bf16[528,128]{1,0:T(8,128)(2,1)S(1)} %collective-permute-done.1.rest_0_, ...), custom_call_target="tpu_custom_call" | custom-call | flops 1 | bytes 1 | tf_op jit(solution)/shard_map/far/pallas_call | solution.py:186
  19.7 0.2 collective-permute-start.4
  20.0 2.4 %head.2 = (f32[2,512,256]{2,1,0:T(8,128)S(1)}, bf16[1024,2048]{1,0:T(8,128)(2,1)S(1)}) custom-call(bf16[16,128,128]{2,1,0:T(8,128)(2,1)S(1)} %far.1.mass_ref, bf16[2,512,2048]{2,1,0:T(8,128)(2,1)S(1)} %turn_own.1.rest_2_.turned_ref, bf16[2048,2048]{1,0:T(8,128)(2,1)S(1)} %copy-done), custom_call_target="tpu_custom_call" | custom-call | flops 1073741824 | bytes 2097152 | tf_op jit(solution)/shard_map/head/pallas_call | solution.py:280
  22.4 0.0 collective-permute-done.4.mass_ref
  22.4 2.4 %head.3 = (bf16[2,512,256]{2,1,0:T(8,128)(2,1)S(1)}, bf16[1024,2048]{1,0:T(8,128)(2,1)S(1)}) custom-call(bf16[16,128,128]{2,1,0:T(8,128)(2,1)S(1)} %collective-permute-done.4.mass_ref, bf16[2,512,2048]{2,1,0:T(8,128)(2,1)S(1)} %get-tuple-element.31.rest_3_.turned_ref, bf16[2048,2048]{1,0:T(8,128)(2,1)S(1)} %get-tuple-element.33.psi_ref.refs_3_, ...), custom_call_target="tpu_custom_call" | custom-call | flops 1073741824 | bytes 2097152 | tf_op jit(solution)/shard_map/head/pallas_call | solution.py:280
  24.9 1.8 %collective-permute-start.5 = (bf16[2,512,256]{2,1,0:T(8,128)(2,1)S(1)}, bf16[2,512,256]{2,1,0:T(8,128)(2,1)S(1)}, u32[]{:S(2)}, u32[]{:S(2)}) collective-permute-start(bf16[2,512,256]{2,1,0:T(8,128)(2,1)S(1)} %get-tuple-element.36.refs_4_), channel_id=1, source_target_pairs={{0,16},{1,17},{2,18},{3,19},{4,20},{5,21},{6,22},{7,23},{8,9},{9,8... | collective-permute-start | bytes 1572872 | tf_op jit(solution)/shard_map/ppermute | solution.py:442
  26.7 2.4 %product.7.refs_4_ = bf16[2,512,256]{2,1,0:T(8,128)(2,1)S(1)} custom-call(bf16[1024,2048]{1,0:T(8,128)(2,1)S(1)} %get-tuple-element.32.refs_0_, bf16[1024,2048]{1,0:T(8,128)(2,1)S(1)} %get-tuple-element.35.refs_1_, bf16[2048,2048]{1,0:T(8,128)(2,1)S(1)} %copy-done, bf16[2048,2048]{1,0:T(8,128)(2,1)S(1)} %get-tuple-element.33.psi_ref.refs_3_, ...), custom_call_target="tpu_custom_call" | custom-call | flops 2147483648 | bytes 4194304 | tf_op jit(solution)/shard_map/product/pallas_call | solution.py:343
  29.0 0.3 collective-permute-start.6
  29.4 2.4 %product.8.keep_ref = f32[2,512,256]{2,1,0:T(8,128)S(1)} custom-call(bf16[1024,2048]{1,0:T(8,128)(2,1)S(1)} %get-tuple-element.32.refs_0_, bf16[1024,2048]{1,0:T(8,128)(2,1)S(1)} %get-tuple-element.35.refs_1_, bf16[2048,2048]{1,0:T(8,128)(2,1)S(1)} %copy-done, bf16[2048,2048]{1,0:T(8,128)(2,1)S(1)} %get-tuple-element.33.psi_ref.refs_3_, ...), custom_call_target="tpu_custom_call" | custom-call | flops 2147483648 | bytes 4194304 | tf_op jit(solution)/shard_map/product/pallas_call | solution.py:343
  31.8 2.3 %collective-permute-done.5.got_ref = bf16[2,512,256]{2,1,0:T(8,128)(2,1)S(1)} collective-permute-done((bf16[2,512,256]{2,1,0:T(8,128)(2,1)S(1)}, bf16[2,512,256]{2,1,0:T(8,128)(2,1)S(1)}, u32[]{:S(2)}, u32[]{:S(2)}) %collective-permute-start.5) | collective-permute-done | bytes 524320 | tf_op jit(solution)/shard_map/ppermute | solution.py:442
  34.1 0.1 add_first.4
  34.2 1.9 %collective-permute-start.8 = (bf16[512,256]{1,0:T(8,128)(2,1)S(1)}, bf16[512,256]{1,0:T(8,128)(2,1)S(1)}, u32[]{:S(2)}, u32[]{:S(2)}) collective-permute-start(bf16[512,256]{1,0:T(8,128)(2,1)S(1)} %get-tuple-element.40), channel_id=1, source_target_pairs={{0,1},{1,0},{2,3},{3,2},{4,5},{5,4},{6,7},{7,6},{8,24},{9,25},{10,... | collective-permute-start | bytes 786440 | tf_op jit(solution)/shard_map/ppermute | solution.py:442
  36.0 2.6 %product.9.refs_4_ = bf16[2,512,256]{2,1,0:T(8,128)(2,1)S(1)} custom-call(bf16[1024,2048]{1,0:T(8,128)(2,1)S(1)} %get-tuple-element.32.refs_0_, bf16[1024,2048]{1,0:T(8,128)(2,1)S(1)} %get-tuple-element.35.refs_1_, bf16[2048,2048]{1,0:T(8,128)(2,1)S(1)} %copy-done, bf16[2048,2048]{1,0:T(8,128)(2,1)S(1)} %get-tuple-element.33.psi_ref.refs_3_, ...), custom_call_target="tpu_custom_call" | custom-call | flops 2147483648 | bytes 4194304 | tf_op jit(solution)/shard_map/product/pallas_call | solution.py:343
  38.6 1.6 %collective-permute-start.13 = (bf16[2,512,256]{2,1,0:T(8,128)(2,1)S(1)}, bf16[2,512,256]{2,1,0:T(8,128)(2,1)S(1)}, u32[]{:S(2)}, u32[]{:S(2)}) collective-permute-start(bf16[2,512,256]{2,1,0:T(8,128)(2,1)S(1)} %product.9.refs_4_), channel_id=1, source_target_pairs={{0,16},{1,17},{2,18},{3,19},{4,20},{5,21},{6,22},{7,23},{8,9},{9,8... | collective-permute-start | bytes 1572872 | tf_op jit(solution)/shard_map/ppermute | solution.py:442
  40.2 2.4 %product.10.keep_ref = f32[2,512,256]{2,1,0:T(8,128)S(1)} custom-call(bf16[1024,2048]{1,0:T(8,128)(2,1)S(1)} %get-tuple-element.32.refs_0_, bf16[1024,2048]{1,0:T(8,128)(2,1)S(1)} %get-tuple-element.35.refs_1_, bf16[2048,2048]{1,0:T(8,128)(2,1)S(1)} %copy-done, bf16[2048,2048]{1,0:T(8,128)(2,1)S(1)} %get-tuple-element.33.psi_ref.refs_3_, ...), custom_call_target="tpu_custom_call" | custom-call | flops 2147483648 | bytes 4194304 | tf_op jit(solution)/shard_map/product/pallas_call | solution.py:343
  42.6 0.1 add_first.5
  42.7 2.4 %product.11.refs_4_ = bf16[2,512,256]{2,1,0:T(8,128)(2,1)S(1)} custom-call(bf16[1024,2048]{1,0:T(8,128)(2,1)S(1)} %get-tuple-element.32.refs_0_, bf16[1024,2048]{1,0:T(8,128)(2,1)S(1)} %get-tuple-element.35.refs_1_, bf16[2048,2048]{1,0:T(8,128)(2,1)S(1)} %copy-done, bf16[2048,2048]{1,0:T(8,128)(2,1)S(1)} %get-tuple-element.33.psi_ref.refs_3_, ...), custom_call_target="tpu_custom_call" | custom-call | flops 2147483648 | bytes 4194304 | tf_op jit(solution)/shard_map/product/pallas_call | solution.py:343
  45.1 1.8 %collective-permute-start.10 = (bf16[2,512,256]{2,1,0:T(8,128)(2,1)S(1)}, bf16[2,512,256]{2,1,0:T(8,128)(2,1)S(1)}, u32[]{:S(2)}, u32[]{:S(2)}) collective-permute-start(bf16[2,512,256]{2,1,0:T(8,128)(2,1)S(1)} %product.11.refs_4_), channel_id=1, source_target_pairs={{0,16},{1,17},{2,18},{3,19},{4,20},{5,21},{6,22},{7,23},{8,9},{9,8... | collective-permute-start | bytes 1572872 | tf_op jit(solution)/shard_map/ppermute | solution.py:442
  46.8 1.5 %collective-permute-start.7 = (bf16[512,256]{1,0:T(8,128)(2,1)S(1)}, bf16[512,256]{1,0:T(8,128)(2,1)S(1)}, u32[]{:S(2)}, u32[]{:S(2)}) collective-permute-start(bf16[512,256]{1,0:T(8,128)(2,1)S(1)} %get-tuple-element.39), channel_id=1, source_target_pairs={{0,1},{1,0},{2,3},{3,2},{4,5},{5,4},{6,7},{7,6},{8,24},{9,25},{10,... | collective-permute-start | bytes 786440 | tf_op jit(solution)/shard_map/ppermute | solution.py:442
  48.4 1.6 %collective-permute-start.9 = (bf16[512,256]{1,0:T(8,128)(2,1)S(1)}, bf16[512,256]{1,0:T(8,128)(2,1)S(1)}, u32[]{:S(2)}, u32[]{:S(2)}) collective-permute-start(bf16[512,256]{1,0:T(8,128)(2,1)S(1)} %add_second.4.refs_5_), channel_id=1, source_target_pairs={{0,2},{1,3},{2,0},{3,1},{4,6},{5,7},{6,4},{7,5},{8,10},{9,11},{10,... | collective-permute-start | bytes 786440 | tf_op jit(solution)/shard_map/ppermute | solution.py:442
  50.0 2.4 %product.13.keep_ref = f32[2,512,256]{2,1,0:T(8,128)S(1)} custom-call(bf16[1024,2048]{1,0:T(8,128)(2,1)S(1)} %get-tuple-element.32.refs_0_, bf16[1024,2048]{1,0:T(8,128)(2,1)S(1)} %get-tuple-element.35.refs_1_, bf16[2048,2048]{1,0:T(8,128)(2,1)S(1)} %copy-done, bf16[2048,2048]{1,0:T(8,128)(2,1)S(1)} %get-tuple-element.33.psi_ref.refs_3_, ...), custom_call_target="tpu_custom_call" | custom-call | flops 2147483648 | bytes 4194304 | tf_op jit(solution)/shard_map/product/pallas_call | solution.py:343
  52.4 0.1 add_first.7
  52.5 0.6 collective-permute-start.14
  53.1 2.9 %collective-permute-done.7.got_ref = bf16[512,256]{1,0:T(8,128)(2,1)S(1)} collective-permute-done((bf16[512,256]{1,0:T(8,128)(2,1)S(1)}, bf16[512,256]{1,0:T(8,128)(2,1)S(1)}, u32[]{:S(2)}, u32[]{:S(2)}) %collective-permute-start.7) | collective-permute-done | bytes 262176 | tf_op jit(solution)/shard_map/ppermute | solution.py:442
  56.0 0.1 add_second.5.refs_5_
  56.0 2.6 %collective-permute-start.12 = (bf16[512,256]{1,0:T(8,128)(2,1)S(1)}, bf16[512,256]{1,0:T(8,128)(2,1)S(1)}, u32[]{:S(2)}, u32[]{:S(2)}) collective-permute-start(bf16[512,256]{1,0:T(8,128)(2,1)S(1)} %add_second.5.refs_5_), channel_id=1, source_target_pairs={{0,4},{1,5},{2,6},{3,7},{4,0},{5,1},{6,2},{7,3},{8,12},{9,13},{10,... | collective-permute-start | bytes 786440 | tf_op jit(solution)/shard_map/ppermute | solution.py:442
  58.7 2.4 %product.12.keep_ref = f32[2,512,256]{2,1,0:T(8,128)S(1)} custom-call(bf16[1024,2048]{1,0:T(8,128)(2,1)S(1)} %get-tuple-element.32.refs_0_, bf16[1024,2048]{1,0:T(8,128)(2,1)S(1)} %get-tuple-element.35.refs_1_, bf16[2048,2048]{1,0:T(8,128)(2,1)S(1)} %copy-done, bf16[2048,2048]{1,0:T(8,128)(2,1)S(1)} %get-tuple-element.33.psi_ref.refs_3_, ...), custom_call_target="tpu_custom_call" | custom-call | flops 2147483648 | bytes 4194304 | tf_op jit(solution)/shard_map/product/pallas_call | solution.py:343
  61.1 0.1 add_first.6
  61.2 1.6 %collective-permute-start.11 = (bf16[512,256]{1,0:T(8,128)(2,1)S(1)}, bf16[512,256]{1,0:T(8,128)(2,1)S(1)}, u32[]{:S(2)}, u32[]{:S(2)}) collective-permute-start(bf16[512,256]{1,0:T(8,128)(2,1)S(1)} %get-tuple-element.42), channel_id=1, source_target_pairs={{0,1},{1,0},{2,3},{3,2},{4,5},{5,4},{6,7},{7,6},{8,24},{9,25},{10,... | collective-permute-start | bytes 786440 | tf_op jit(solution)/shard_map/ppermute | solution.py:442
  62.8 1.6 %collective-permute-start.15 = (bf16[512,256]{1,0:T(8,128)(2,1)S(1)}, bf16[512,256]{1,0:T(8,128)(2,1)S(1)}, u32[]{:S(2)}, u32[]{:S(2)}) collective-permute-start(bf16[512,256]{1,0:T(8,128)(2,1)S(1)} %add_second.7), channel_id=1, source_target_pairs={{0,2},{1,3},{2,0},{3,1},{4,6},{5,7},{6,4},{7,5},{8,10},{9,11},{10,... | collective-permute-start | bytes 786440 | tf_op jit(solution)/shard_map/ppermute | solution.py:442
  64.4 3.2 %collective-permute-done.11.got_ref = bf16[512,256]{1,0:T(8,128)(2,1)S(1)} collective-permute-done((bf16[512,256]{1,0:T(8,128)(2,1)S(1)}, bf16[512,256]{1,0:T(8,128)(2,1)S(1)}, u32[]{:S(2)}, u32[]{:S(2)}) %collective-permute-start.11) | collective-permute-done | bytes 262176 | tf_op jit(solution)/shard_map/ppermute | solution.py:442
  67.6 0.0 collective-permute-done.12.refs_0_
  67.6 0.1 add_second.6.low_ref
  67.7 2.4 %collective-permute-done.15.refs_0_ = bf16[512,256]{1,0:T(8,128)(2,1)S(1)} collective-permute-done((bf16[512,256]{1,0:T(8,128)(2,1)S(1)}, bf16[512,256]{1,0:T(8,128)(2,1)S(1)}, u32[]{:S(2)}, u32[]{:S(2)}) %collective-permute-start.15) | collective-permute-done | bytes 262176 | tf_op jit(solution)/shard_map/ppermute | solution.py:442
  70.1 0.8 %add_last.1 = f32[512,256]{1,0:T(8,128)} custom-call(f32[512,256]{1,0:T(8,128)S(1)} %add_second.6.low_ref, bf16[512,256]{1,0:T(8,128)(2,1)S(1)} %collective-permute-done.15.refs_0_), custom_call_target="tpu_custom_call" | custom-call | flops 1 | bytes 1 | tf_op jit(solution)/shard_map/add_last/pallas_call | solution.py:414
  (13 shorter events, 0.1 us)
Async XLA Ops:
  0.0 12.2 %copy-start = (bf16[2048,2048]{1,0:T(8,128)(2,1)S(1)}, bf16[2048,2048]{1,0:T(8,128)(2,1)}, u32[]{:S(2)}) copy-start(bf16[2048,2048]{1,0:T(8,128)(2,1)} %refs_2_.13) | copy-start | bytes 25165828
  0.0 13.9 %collective-permute-start.3 = (bf16[2048,2048]{1,0:T(8,128)(2,1)}, bf16[2048,2048]{1,0:T(8,128)(2,1)}, u32[]{:S(2)}, u32[]{:S(2)}) collective-permute-start(bf16[2048,2048]{1,0:T(8,128)(2,1)} %refs_2_.13), channel_id=1, source_target_pairs={{0,8},{8,0},{16,24},{24,16},{1,9},{9,1},{17,25},{25,17},{2,10},{10... | collective-permute-start | bytes 25165832 | tf_op jit(solution)/shard_map/ppermute | solution.py:434
  9.1 4.5 %collective-permute-start = (bf16[528,128]{1,0:T(8,128)(2,1)}, bf16[528,128]{1,0:T(8,128)(2,1)S(1)}, u32[]{:S(2)}, u32[]{:S(2)}) collective-permute-start(bf16[528,128]{1,0:T(8,128)(2,1)} %get-tuple-element.26), channel_id=1, source_target_pairs={{0,8},{8,0},{16,24},{24,16},{1,9},{9,1},{17,25},{25,17},{2,10},{10... | collective-permute-start | bytes 405512 | tf_op jit(solution)/shard_map/ppermute | solution.py:434
  9.5 8.0 %collective-permute-start.1 = (bf16[528,128]{1,0:T(8,128)(2,1)}, bf16[528,128]{1,0:T(8,128)(2,1)S(1)}, u32[]{:S(2)}, u32[]{:S(2)}) collective-permute-start(bf16[528,128]{1,0:T(8,128)(2,1)} %get-tuple-element.29), channel_id=1, source_target_pairs={{0,16},{8,24},{16,0},{24,8},{1,17},{9,25},{17,1},{25,9},{2,18},{10... | collective-permute-start | bytes 405512 | tf_op jit(solution)/shard_map/ppermute | solution.py:434
  12.2 1.5 %copy-start.2 = (bf16[528,128]{1,0:T(8,128)(2,1)S(1)}, bf16[528,128]{1,0:T(8,128)(2,1)}, u32[]{:S(2)}) copy-start(bf16[528,128]{1,0:T(8,128)(2,1)} %get-tuple-element.25.own_ref) | copy-start | bytes 405508
  12.2 6.8 %collective-permute-start.2 = (bf16[528,128]{1,0:T(8,128)(2,1)}, bf16[528,128]{1,0:T(8,128)(2,1)S(1)}, u32[]{:S(2)}, u32[]{:S(2)}) collective-permute-start(bf16[528,128]{1,0:T(8,128)(2,1)} %get-tuple-element.30), channel_id=1, source_target_pairs={{0,24},{8,16},{16,8},{24,0},{1,25},{9,17},{17,9},{25,1},{2,26},{10... | collective-permute-start | bytes 405512 | tf_op jit(solution)/shard_map/ppermute | solution.py:434
  13.9 5.1 %copy-start.1 = (f32[16,128,128]{2,1,0:T(8,128)S(1)}, f32[16,128,128]{2,1,0:T(8,128)}, u32[]{:S(2)}) copy-start(f32[16,128,128]{2,1,0:T(8,128)} %base_ref.1) | copy-start | bytes 3145732
  19.7 2.7 %collective-permute-start.4 = (bf16[16,128,128]{2,1,0:T(8,128)(2,1)S(1)}, bf16[16,128,128]{2,1,0:T(8,128)(2,1)S(1)}, u32[]{:S(2)}, u32[]{:S(2)}) collective-permute-start(bf16[16,128,128]{2,1,0:T(8,128)(2,1)S(1)} %far.1.mass_ref), channel_id=1, source_target_pairs={{0,8},{8,0},{16,24},{24,16},{1,9},{9,1},{17,25},{25,17},{2,10},{10... | collective-permute-start | bytes 1572872 | tf_op jit(solution)/shard_map/ppermute | solution.py:434
  24.9 9.2 %collective-permute-start.5 = (bf16[2,512,256]{2,1,0:T(8,128)(2,1)S(1)}, bf16[2,512,256]{2,1,0:T(8,128)(2,1)S(1)}, u32[]{:S(2)}, u32[]{:S(2)}) collective-permute-start(bf16[2,512,256]{2,1,0:T(8,128)(2,1)S(1)} %get-tuple-element.36.refs_4_), channel_id=1, source_target_pairs={{0,16},{1,17},{2,18},{3,19},{4,20},{5,21},{6,22},{7,23},{8,9},{9,8... | collective-permute-start | bytes 1572872 | tf_op jit(solution)/shard_map/ppermute | solution.py:442
  29.0 13.5 %collective-permute-start.6 = (bf16[2,512,256]{2,1,0:T(8,128)(2,1)S(1)}, bf16[2,512,256]{2,1,0:T(8,128)(2,1)S(1)}, u32[]{:S(2)}, u32[]{:S(2)}) collective-permute-start(bf16[2,512,256]{2,1,0:T(8,128)(2,1)S(1)} %product.7.refs_4_), channel_id=1, source_target_pairs={{0,16},{1,17},{2,18},{3,19},{4,20},{5,21},{6,22},{7,23},{8,9},{9,8... | collective-permute-start | bytes 1572872 | tf_op jit(solution)/shard_map/ppermute | solution.py:442
  34.2 14.2 %collective-permute-start.8 = (bf16[512,256]{1,0:T(8,128)(2,1)S(1)}, bf16[512,256]{1,0:T(8,128)(2,1)S(1)}, u32[]{:S(2)}, u32[]{:S(2)}) collective-permute-start(bf16[512,256]{1,0:T(8,128)(2,1)S(1)} %get-tuple-element.40), channel_id=1, source_target_pairs={{0,1},{1,0},{2,3},{3,2},{4,5},{5,4},{6,7},{7,6},{8,24},{9,25},{10,... | collective-permute-start | bytes 786440 | tf_op jit(solution)/shard_map/ppermute | solution.py:442
  38.6 13.8 %collective-permute-start.13 = (bf16[2,512,256]{2,1,0:T(8,128)(2,1)S(1)}, bf16[2,512,256]{2,1,0:T(8,128)(2,1)S(1)}, u32[]{:S(2)}, u32[]{:S(2)}) collective-permute-start(bf16[2,512,256]{2,1,0:T(8,128)(2,1)S(1)} %product.9.refs_4_), channel_id=1, source_target_pairs={{0,16},{1,17},{2,18},{3,19},{4,20},{5,21},{6,22},{7,23},{8,9},{9,8... | collective-permute-start | bytes 1572872 | tf_op jit(solution)/shard_map/ppermute | solution.py:442
  45.1 16.0 %collective-permute-start.10 = (bf16[2,512,256]{2,1,0:T(8,128)(2,1)S(1)}, bf16[2,512,256]{2,1,0:T(8,128)(2,1)S(1)}, u32[]{:S(2)}, u32[]{:S(2)}) collective-permute-start(bf16[2,512,256]{2,1,0:T(8,128)(2,1)S(1)} %product.11.refs_4_), channel_id=1, source_target_pairs={{0,16},{1,17},{2,18},{3,19},{4,20},{5,21},{6,22},{7,23},{8,9},{9,8... | collective-permute-start | bytes 1572872 | tf_op jit(solution)/shard_map/ppermute | solution.py:442
  46.8 9.1 %collective-permute-start.7 = (bf16[512,256]{1,0:T(8,128)(2,1)S(1)}, bf16[512,256]{1,0:T(8,128)(2,1)S(1)}, u32[]{:S(2)}, u32[]{:S(2)}) collective-permute-start(bf16[512,256]{1,0:T(8,128)(2,1)S(1)} %get-tuple-element.39), channel_id=1, source_target_pairs={{0,1},{1,0},{2,3},{3,2},{4,5},{5,4},{6,7},{7,6},{8,24},{9,25},{10,... | collective-permute-start | bytes 786440 | tf_op jit(solution)/shard_map/ppermute | solution.py:442
  48.4 7.6 %collective-permute-start.9 = (bf16[512,256]{1,0:T(8,128)(2,1)S(1)}, bf16[512,256]{1,0:T(8,128)(2,1)S(1)}, u32[]{:S(2)}, u32[]{:S(2)}) collective-permute-start(bf16[512,256]{1,0:T(8,128)(2,1)S(1)} %add_second.4.refs_5_), channel_id=1, source_target_pairs={{0,2},{1,3},{2,0},{3,1},{4,6},{5,7},{6,4},{7,5},{8,10},{9,11},{10,... | collective-permute-start | bytes 786440 | tf_op jit(solution)/shard_map/ppermute | solution.py:442
  52.5 10.2 %collective-permute-start.14 = (bf16[512,256]{1,0:T(8,128)(2,1)S(1)}, bf16[512,256]{1,0:T(8,128)(2,1)S(1)}, u32[]{:S(2)}, u32[]{:S(2)}) collective-permute-start(bf16[512,256]{1,0:T(8,128)(2,1)S(1)} %get-tuple-element.44), channel_id=1, source_target_pairs={{0,1},{1,0},{2,3},{3,2},{4,5},{5,4},{6,7},{7,6},{8,24},{9,25},{10,... | collective-permute-start | bytes 786440 | tf_op jit(solution)/shard_map/ppermute | solution.py:442
  56.0 11.6 %collective-permute-start.12 = (bf16[512,256]{1,0:T(8,128)(2,1)S(1)}, bf16[512,256]{1,0:T(8,128)(2,1)S(1)}, u32[]{:S(2)}, u32[]{:S(2)}) collective-permute-start(bf16[512,256]{1,0:T(8,128)(2,1)S(1)} %add_second.5.refs_5_), channel_id=1, source_target_pairs={{0,4},{1,5},{2,6},{3,7},{4,0},{5,1},{6,2},{7,3},{8,12},{9,13},{10,... | collective-permute-start | bytes 786440 | tf_op jit(solution)/shard_map/ppermute | solution.py:442
  61.2 6.4 %collective-permute-start.11 = (bf16[512,256]{1,0:T(8,128)(2,1)S(1)}, bf16[512,256]{1,0:T(8,128)(2,1)S(1)}, u32[]{:S(2)}, u32[]{:S(2)}) collective-permute-start(bf16[512,256]{1,0:T(8,128)(2,1)S(1)} %get-tuple-element.42), channel_id=1, source_target_pairs={{0,1},{1,0},{2,3},{3,2},{4,5},{5,4},{6,7},{7,6},{8,24},{9,25},{10,... | collective-permute-start | bytes 786440 | tf_op jit(solution)/shard_map/ppermute | solution.py:442
  62.8 7.3 %collective-permute-start.15 = (bf16[512,256]{1,0:T(8,128)(2,1)S(1)}, bf16[512,256]{1,0:T(8,128)(2,1)S(1)}, u32[]{:S(2)}, u32[]{:S(2)}) collective-permute-start(bf16[512,256]{1,0:T(8,128)(2,1)S(1)} %add_second.7), channel_id=1, source_target_pairs={{0,2},{1,3},{2,0},{3,1},{4,6},{5,7},{6,4},{7,5},{8,10},{9,11},{10,... | collective-permute-start | bytes 786440 | tf_op jit(solution)/shard_map/ppermute | solution.py:442

commit v8 on v6

--- a/solution.py
+++ b/solution.py
@@ -451,7 +451,7 @@
         if i < last:
             behind = [second[i - 1][0]] if i else [go]
             go, = product(chunks[i + 1], *common, go=jnp.bfloat16, behind=behind)
-        behind = [go] + ([third[i - 2]] if i - 2 in third else [])
+        behind = [keep[0]] if i == 1 else [go] + ([third[i - 2]] if i - 2 in third else [])
         keep[i], = product(chunks[i], *common, keep=True, behind=behind)
         behind = [third[i - 2]] if 0 and i > 1 else []
         low, move = add_first(keep[i], first[i], behind)

time: 71.1 us -> 71.7 us (level)
  waiting for transfers between devices: 12.5 us -> 14.1 us
  starting transfers between devices: 20.6 us -> 19.3 us
    ppermute x11, waiting for transfers between devices: 10.8 us -> 12.4 us  [swap(): return lax.ppermute(v, ('sub', 'tile'), pairs)]
    ppermute x11, starting transfers between devices: 16.9 us -> 15.6 us  [swap(): return lax.ppermute(v, ('sub', 'tile'), pairs)]
  transfers between devices with their start and end apart: 16 -> 16, of which waited for: 6 -> 8; matrix products, arithmetic and copies ran while one was open for 0% -> 0% of each run, Pallas kernels for 47% -> 47%
where the time goes in v8:
time: 71.7 us; the launch traced here: 71.2 us
  Pallas kernels  37.6 us (52%)
  starting transfers between devices  19.3 us (27%)
  waiting for transfers between devices  14.1 us (20%)
    pallas_call x7, Pallas kernels, product(): pl.pallas_call(functools.partial(product_kernel, chunk, len(lefts), bool(...  16.8 us
    ppermute x11, starting transfers between devices, swap(): return lax.ppermute(v, ('sub', 'tile'), pairs)  15.6 us
    ppermute x11, waiting for transfers between devices, swap(): return lax.ppermute(v, ('sub', 'tile'), pairs)  12.4 us
    pallas_call x1, Pallas kernels, make_contrib(): pl.pallas_call(functools.partial(contrib_kernel, owner_links, blk_dev, n_...  8.65 us
    pallas_call x2, Pallas kernels, make_head(): pl.pallas_call(functools.partial(head_kernel, chunk, bool(acc)), in_specs...  4.87 us
    ppermute x5, starting transfers between devices, swap_sub(): return lax.ppermute(v, 'sub', [(i, i ^ d) for i in range(n_sub)])  3.73 us
    pallas_call x1, Pallas kernels, turn(): pl.pallas_call(turn_kernel, in_specs=[ANY], out_specs=[VMEM, VMEM], out_s...  3.64 us
    ppermute x5, waiting for transfers between devices, swap_sub(): return lax.ppermute(v, 'sub', [(i, i ^ d) for i in range(n_sub)])  1.69 us
  transfers between devices with their start and end apart: 16, of which 8 were waited for; matrix products, arithmetic and copies ran while one was open for 0% of the time, Pallas kernels for 47%

profile of v8, /device:TPU:0, one launch (start us, length us, event | category | flops | bytes accessed | tf_op | source)
XLA Modules:
  0.0 71.2 jit_solution(8628526664232239561)
XLA Ops:
  0.0 0.5 collective-permute-start.3
  0.5 8.7 %contrib.1 = (bf16[528,128]{1,0:T(8,128)(2,1)}, bf16[528,128]{1,0:T(8,128)(2,1)}, bf16[528,128]{1,0:T(8,128)(2,1)}, bf16[528,128]{1,0:T(8,128)(2,1)}) custom-call(s32[4]{0:T(128)} %rows_ref.1, s32[4,8]{1,0:T(4,128)} %adj_ref.1, bf16[4,768,512]{2,1,0:T(8,128)(2,1)} %modes_ref.1, bf16[4,8,768,128]{3,2,1,0:T(8,128)(2,1)} %coup_ref.1, f32[4,512]{1,0:T(4,128)} %inv_ref.1), custom_call_target="tpu_custom_call" | custom-call | flops 1 | bytes 1 | tf_op jit(solution)/shard_map/contrib/pallas_call | solution.py:121
  9.1 0.4 collective-permute-start
  9.5 2.6 %collective-permute-start.1 = (bf16[528,128]{1,0:T(8,128)(2,1)}, bf16[528,128]{1,0:T(8,128)(2,1)S(1)}, u32[]{:S(2)}, u32[]{:S(2)}) collective-permute-start(bf16[528,128]{1,0:T(8,128)(2,1)} %get-tuple-element.29), channel_id=1, source_target_pairs={{0,16},{8,24},{16,0},{24,8},{1,17},{9,25},{17,1},{25,9},{2,18},{10... | collective-permute-start | bytes 405512 | tf_op jit(solution)/shard_map/ppermute | solution.py:404
  12.2 0.0 collective-permute-start.2
  12.2 1.3 %turn_own.1.rest_2_.turned_ref = bf16[2,512,2048]{2,1,0:T(8,128)(2,1)S(1)} custom-call(bf16[2048,2048]{1,0:T(8,128)(2,1)S(1)} %copy-done), custom_call_target="tpu_custom_call" | custom-call | flops 1 | bytes 1 | tf_op jit(solution)/shard_map/turn_own/pallas_call | solution.py:241
  13.4 0.2 collective-permute-done.pair_ref
  13.6 0.2 near.1
  13.9 0.0 copy-start.1
  13.9 3.6 %turn.1 = (bf16[2,512,2048]{2,1,0:T(8,128)(2,1)S(1)}, bf16[2048,2048]{1,0:T(8,128)(2,1)S(1)}) custom-call(bf16[2048,2048]{1,0:T(8,128)(2,1)} %collective-permute-done.3.psi_ref), custom_call_target="tpu_custom_call" | custom-call | flops 1 | bytes 1 | tf_op jit(solution)/shard_map/turn/pallas_call | solution.py:218
  17.5 0.0 collective-permute-done.1.rest_0_
  17.5 1.5 %collective-permute-done.2.rest_1_ = bf16[528,128]{1,0:T(8,128)(2,1)S(1)} collective-permute-done((bf16[528,128]{1,0:T(8,128)(2,1)}, bf16[528,128]{1,0:T(8,128)(2,1)S(1)}, u32[]{:S(2)}, u32[]{:S(2)}) %collective-permute-start.2) | collective-permute-done | bytes 135200 | tf_op jit(solution)/shard_map/ppermute | solution.py:404
  19.0 0.7 %far.1.mass_ref = bf16[16,128,128]{2,1,0:T(8,128)(2,1)S(1)} custom-call(f32[16,128,128]{2,1,0:T(8,128)S(1)} %copy-done.1, f32[17,64,128]{2,1,0:T(8,128)S(1)} %get-tuple-element.27.near_ref, f32[17,1,128]{2,1,0:T(1,128)S(1)} %get-tuple-element.28.near_side_ref, bf16[528,128]{1,0:T(8,128)(2,1)S(1)} %collective-permute-done.1.rest_0_, ...), custom_call_target="tpu_custom_call" | custom-call | flops 1 | bytes 1 | tf_op jit(solution)/shard_map/far/pallas_call | solution.py:186
  19.7 0.2 collective-permute-start.4
  20.0 2.4 %head.2 = (f32[2,512,256]{2,1,0:T(8,128)S(1)}, bf16[1024,2048]{1,0:T(8,128)(2,1)S(1)}) custom-call(bf16[16,128,128]{2,1,0:T(8,128)(2,1)S(1)} %far.1.mass_ref, bf16[2,512,2048]{2,1,0:T(8,128)(2,1)S(1)} %turn_own.1.rest_2_.turned_ref, bf16[2048,2048]{1,0:T(8,128)(2,1)S(1)} %copy-done), custom_call_target="tpu_custom_call" | custom-call | flops 1073741824 | bytes 2097152 | tf_op jit(solution)/shard_map/head/pallas_call | solution.py:280
  22.4 0.0 collective-permute-done.4.mass_ref
  22.4 2.4 %head.3 = (bf16[2,512,256]{2,1,0:T(8,128)(2,1)S(1)}, bf16[1024,2048]{1,0:T(8,128)(2,1)S(1)}) custom-call(bf16[16,128,128]{2,1,0:T(8,128)(2,1)S(1)} %collective-permute-done.4.mass_ref, bf16[2,512,2048]{2,1,0:T(8,128)(2,1)S(1)} %get-tuple-element.31.rest_3_.turned_ref, bf16[2048,2048]{1,0:T(8,128)(2,1)S(1)} %get-tuple-element.33.psi_ref.refs_3_, ...), custom_call_target="tpu_custom_call" | custom-call | flops 1073741824 | bytes 2097152 | tf_op jit(solution)/shard_map/head/pallas_call | solution.py:280
  24.9 1.8 %collective-permute-start.7 = (bf16[2,512,256]{2,1,0:T(8,128)(2,1)S(1)}, bf16[2,512,256]{2,1,0:T(8,128)(2,1)S(1)}, u32[]{:S(2)}, u32[]{:S(2)}) collective-permute-start(bf16[2,512,256]{2,1,0:T(8,128)(2,1)S(1)} %get-tuple-element.36.refs_4_), channel_id=1, source_target_pairs={{0,16},{1,17},{2,18},{3,19},{4,20},{5,21},{6,22},{7,23},{8,9},{9,8... | collective-permute-start | bytes 1572872 | tf_op jit(solution)/shard_map/ppermute | solution.py:412
  26.7 2.4 %product.7.refs_4_ = bf16[2,512,256]{2,1,0:T(8,128)(2,1)S(1)} custom-call(bf16[1024,2048]{1,0:T(8,128)(2,1)S(1)} %get-tuple-element.32.refs_0_, bf16[1024,2048]{1,0:T(8,128)(2,1)S(1)} %get-tuple-element.35.refs_1_, bf16[2048,2048]{1,0:T(8,128)(2,1)S(1)} %copy-done, bf16[2048,2048]{1,0:T(8,128)(2,1)S(1)} %get-tuple-element.33.psi_ref.refs_3_, ...), custom_call_target="tpu_custom_call" | custom-call | flops 2147483648 | bytes 4194304 | tf_op jit(solution)/shard_map/product/pallas_call | solution.py:343
  29.0 0.3 collective-permute-start.5
  29.4 2.4 %product.8.refs_4_.keep_ref = f32[2,512,256]{2,1,0:T(8,128)S(1)} custom-call(bf16[1024,2048]{1,0:T(8,128)(2,1)S(1)} %get-tuple-element.32.refs_0_, bf16[1024,2048]{1,0:T(8,128)(2,1)S(1)} %get-tuple-element.35.refs_1_, bf16[2048,2048]{1,0:T(8,128)(2,1)S(1)} %copy-done, bf16[2048,2048]{1,0:T(8,128)(2,1)S(1)} %get-tuple-element.33.psi_ref.refs_3_, ...), custom_call_target="tpu_custom_call" | custom-call | flops 2147483648 | bytes 4194304 | tf_op jit(solution)/shard_map/product/pallas_call | solution.py:343
  31.8 2.3 %collective-permute-done.7.got_ref = bf16[2,512,256]{2,1,0:T(8,128)(2,1)S(1)} collective-permute-done((bf16[2,512,256]{2,1,0:T(8,128)(2,1)S(1)}, bf16[2,512,256]{2,1,0:T(8,128)(2,1)S(1)}, u32[]{:S(2)}, u32[]{:S(2)}) %collective-permute-start.7) | collective-permute-done | bytes 524320 | tf_op jit(solution)/shard_map/ppermute | solution.py:412
  34.1 0.1 add_first.5
  34.2 2.6 %product.13 = bf16[2,512,256]{2,1,0:T(8,128)(2,1)S(1)} custom-call(bf16[1024,2048]{1,0:T(8,128)(2,1)S(1)} %get-tuple-element.32.refs_0_, bf16[1024,2048]{1,0:T(8,128)(2,1)S(1)} %get-tuple-element.35.refs_1_, bf16[2048,2048]{1,0:T(8,128)(2,1)S(1)} %copy-done, bf16[2048,2048]{1,0:T(8,128)(2,1)S(1)} %get-tuple-element.33.psi_ref.refs_3_, ...), custom_call_target="tpu_custom_call" | custom-call | flops 2147483648 | bytes 4194304 | tf_op jit(solution)/shard_map/product/pallas_call | solution.py:343
  36.8 1.8 %collective-permute-start.13 = (bf16[2,512,256]{2,1,0:T(8,128)(2,1)S(1)}, bf16[2,512,256]{2,1,0:T(8,128)(2,1)S(1)}, u32[]{:S(2)}, u32[]{:S(2)}) collective-permute-start(bf16[2,512,256]{2,1,0:T(8,128)(2,1)S(1)} %product.13), channel_id=1, source_target_pairs={{0,16},{1,17},{2,18},{3,19},{4,20},{5,21},{6,22},{7,23},{8,9},{9,8... | collective-permute-start | bytes 1572872 | tf_op jit(solution)/shard_map/ppermute | solution.py:412
  38.6 1.6 %collective-permute-start.8 = (bf16[512,256]{1,0:T(8,128)(2,1)S(1)}, bf16[512,256]{1,0:T(8,128)(2,1)S(1)}, u32[]{:S(2)}, u32[]{:S(2)}) collective-permute-start(bf16[512,256]{1,0:T(8,128)(2,1)S(1)} %get-tuple-element.40), channel_id=1, source_target_pairs={{0,1},{1,0},{2,3},{3,2},{4,5},{5,4},{6,7},{7,6},{8,24},{9,25},{10,... | collective-permute-start | bytes 786440 | tf_op jit(solution)/shard_map/ppermute | solution.py:412
  40.1 2.4 %product.9.keep_ref = f32[2,512,256]{2,1,0:T(8,128)S(1)} custom-call(bf16[1024,2048]{1,0:T(8,128)(2,1)S(1)} %get-tuple-element.32.refs_0_, bf16[1024,2048]{1,0:T(8,128)(2,1)S(1)} %get-tuple-element.35.refs_1_, bf16[2048,2048]{1,0:T(8,128)(2,1)S(1)} %copy-done, bf16[2048,2048]{1,0:T(8,128)(2,1)S(1)} %get-tuple-element.33.psi_ref.refs_3_, ...), custom_call_target="tpu_custom_call" | custom-call | flops 2147483648 | bytes 4194304 | tf_op jit(solution)/shard_map/product/pallas_call | solution.py:343
  42.5 0.1 add_first.4
  42.6 2.4 %product.10.refs_4_ = bf16[2,512,256]{2,1,0:T(8,128)(2,1)S(1)} custom-call(bf16[1024,2048]{1,0:T(8,128)(2,1)S(1)} %get-tuple-element.32.refs_0_, bf16[1024,2048]{1,0:T(8,128)(2,1)S(1)} %get-tuple-element.35.refs_1_, bf16[2048,2048]{1,0:T(8,128)(2,1)S(1)} %copy-done, bf16[2048,2048]{1,0:T(8,128)(2,1)S(1)} %get-tuple-element.33.psi_ref.refs_3_, ...), custom_call_target="tpu_custom_call" | custom-call | flops 2147483648 | bytes 4194304 | tf_op jit(solution)/shard_map/product/pallas_call | solution.py:343
  45.0 0.6 collective-permute-start.10
  45.6 0.7 %collective-permute-start.6 = (bf16[512,256]{1,0:T(8,128)(2,1)S(1)}, bf16[512,256]{1,0:T(8,128)(2,1)S(1)}, u32[]{:S(2)}, u32[]{:S(2)}) collective-permute-start(bf16[512,256]{1,0:T(8,128)(2,1)S(1)} %get-tuple-element.38), channel_id=1, source_target_pairs={{0,1},{1,0},{2,3},{3,2},{4,5},{5,4},{6,7},{7,6},{8,24},{9,25},{10,... | collective-permute-start | bytes 786440 | tf_op jit(solution)/shard_map/ppermute | solution.py:412
  46.3 1.5 %collective-permute-done.8.got_ref = bf16[512,256]{1,0:T(8,128)(2,1)S(1)} collective-permute-done((bf16[512,256]{1,0:T(8,128)(2,1)S(1)}, bf16[512,256]{1,0:T(8,128)(2,1)S(1)}, u32[]{:S(2)}, u32[]{:S(2)}) %collective-permute-start.8) | collective-permute-done | bytes 262176 | tf_op jit(solution)/shard_map/ppermute | solution.py:412
  47.9 1.6 %collective-permute-start.9 = (bf16[512,256]{1,0:T(8,128)(2,1)S(1)}, bf16[512,256]{1,0:T(8,128)(2,1)S(1)}, u32[]{:S(2)}, u32[]{:S(2)}) collective-permute-start(bf16[512,256]{1,0:T(8,128)(2,1)S(1)} %add_second.5.refs_5_), channel_id=1, source_target_pairs={{0,2},{1,3},{2,0},{3,1},{4,6},{5,7},{6,4},{7,5},{8,10},{9,11},{10,... | collective-permute-start | bytes 786440 | tf_op jit(solution)/shard_map/ppermute | solution.py:412
  49.5 2.4 %product.12.keep_ref = f32[2,512,256]{2,1,0:T(8,128)S(1)} custom-call(bf16[1024,2048]{1,0:T(8,128)(2,1)S(1)} %get-tuple-element.32.refs_0_, bf16[1024,2048]{1,0:T(8,128)(2,1)S(1)} %get-tuple-element.35.refs_1_, bf16[2048,2048]{1,0:T(8,128)(2,1)S(1)} %copy-done, bf16[2048,2048]{1,0:T(8,128)(2,1)S(1)} %get-tuple-element.33.psi_ref.refs_3_, ...), custom_call_target="tpu_custom_call" | custom-call | flops 2147483648 | bytes 4194304 | tf_op jit(solution)/shard_map/product/pallas_call | solution.py:343
  51.9 0.1 add_first.7
  52.0 1.6 %collective-permute-start.14 = (bf16[512,256]{1,0:T(8,128)(2,1)S(1)}, bf16[512,256]{1,0:T(8,128)(2,1)S(1)}, u32[]{:S(2)}, u32[]{:S(2)}) collective-permute-start(bf16[512,256]{1,0:T(8,128)(2,1)S(1)} %get-tuple-element.44), channel_id=1, source_target_pairs={{0,1},{1,0},{2,3},{3,2},{4,5},{5,4},{6,7},{7,6},{8,24},{9,25},{10,... | collective-permute-start | bytes 786440 | tf_op jit(solution)/shard_map/ppermute | solution.py:412
  53.6 1.2 %collective-permute-done.6.got_ref = bf16[512,256]{1,0:T(8,128)(2,1)S(1)} collective-permute-done((bf16[512,256]{1,0:T(8,128)(2,1)S(1)}, bf16[512,256]{1,0:T(8,128)(2,1)S(1)}, u32[]{:S(2)}, u32[]{:S(2)}) %collective-permute-start.6) | collective-permute-done | bytes 262176 | tf_op jit(solution)/shard_map/ppermute | solution.py:412
  54.8 0.1 add_second.6.refs_5_
  54.9 2.7 %collective-permute-start.12 = (bf16[512,256]{1,0:T(8,128)(2,1)S(1)}, bf16[512,256]{1,0:T(8,128)(2,1)S(1)}, u32[]{:S(2)}, u32[]{:S(2)}) collective-permute-start(bf16[512,256]{1,0:T(8,128)(2,1)S(1)} %add_second.6.refs_5_), channel_id=1, source_target_pairs={{0,4},{1,5},{2,6},{3,7},{4,0},{5,1},{6,2},{7,3},{8,12},{9,13},{10,... | collective-permute-start | bytes 786440 | tf_op jit(solution)/shard_map/ppermute | solution.py:412
  57.6 2.4 %product.11.keep_ref = f32[2,512,256]{2,1,0:T(8,128)S(1)} custom-call(bf16[1024,2048]{1,0:T(8,128)(2,1)S(1)} %get-tuple-element.32.refs_0_, bf16[1024,2048]{1,0:T(8,128)(2,1)S(1)} %get-tuple-element.35.refs_1_, bf16[2048,2048]{1,0:T(8,128)(2,1)S(1)} %copy-done, bf16[2048,2048]{1,0:T(8,128)(2,1)S(1)} %get-tuple-element.33.psi_ref.refs_3_, ...), custom_call_target="tpu_custom_call" | custom-call | flops 2147483648 | bytes 4194304 | tf_op jit(solution)/shard_map/product/pallas_call | solution.py:343
  60.0 0.1 add_first.6
  60.1 1.3 %collective-permute-start.11 = (bf16[512,256]{1,0:T(8,128)(2,1)S(1)}, bf16[512,256]{1,0:T(8,128)(2,1)S(1)}, u32[]{:S(2)}, u32[]{:S(2)}) collective-permute-start(bf16[512,256]{1,0:T(8,128)(2,1)S(1)} %get-tuple-element.42), channel_id=1, source_target_pairs={{0,1},{1,0},{2,3},{3,2},{4,5},{5,4},{6,7},{7,6},{8,24},{9,25},{10,... | collective-permute-start | bytes 786440 | tf_op jit(solution)/shard_map/ppermute | solution.py:412
  61.4 1.6 %collective-permute-start.15 = (bf16[512,256]{1,0:T(8,128)(2,1)S(1)}, bf16[512,256]{1,0:T(8,128)(2,1)S(1)}, u32[]{:S(2)}, u32[]{:S(2)}) collective-permute-start(bf16[512,256]{1,0:T(8,128)(2,1)S(1)} %add_second.8), channel_id=1, source_target_pairs={{0,2},{1,3},{2,0},{3,1},{4,6},{5,7},{6,4},{7,5},{8,10},{9,11},{10,... | collective-permute-start | bytes 786440 | tf_op jit(solution)/shard_map/ppermute | solution.py:412
  63.0 3.5 %collective-permute-done.11.got_ref = bf16[512,256]{1,0:T(8,128)(2,1)S(1)} collective-permute-done((bf16[512,256]{1,0:T(8,128)(2,1)S(1)}, bf16[512,256]{1,0:T(8,128)(2,1)S(1)}, u32[]{:S(2)}, u32[]{:S(2)}) %collective-permute-start.11) | collective-permute-done | bytes 262176 | tf_op jit(solution)/shard_map/ppermute | solution.py:412
  66.5 0.8 %collective-permute-done.12.refs_0_ = bf16[512,256]{1,0:T(8,128)(2,1)S(1)} collective-permute-done((bf16[512,256]{1,0:T(8,128)(2,1)S(1)}, bf16[512,256]{1,0:T(8,128)(2,1)S(1)}, u32[]{:S(2)}, u32[]{:S(2)}) %collective-permute-start.12) | collective-permute-done | bytes 262176 | tf_op jit(solution)/shard_map/ppermute | solution.py:412
  67.3 0.1 add_second.7.low_ref
  67.4 3.0 %collective-permute-done.15.got_ref = bf16[512,256]{1,0:T(8,128)(2,1)S(1)} collective-permute-done((bf16[512,256]{1,0:T(8,128)(2,1)S(1)}, bf16[512,256]{1,0:T(8,128)(2,1)S(1)}, u32[]{:S(2)}, u32[]{:S(2)}) %collective-permute-start.15) | collective-permute-done | bytes 262176 | tf_op jit(solution)/shard_map/ppermute | solution.py:412
  70.4 0.8 %add_second.9 = f32[512,256]{1,0:T(8,128)} custom-call(f32[512,256]{1,0:T(8,128)S(1)} %add_second.7.low_ref, bf16[512,256]{1,0:T(8,128)(2,1)S(1)} %collective-permute-done.15.got_ref), custom_call_target="tpu_custom_call" | custom-call | flops 1 | bytes 1 | tf_op jit(solution)/shard_map/add_second/pallas_call | solution.py:385
  (13 shorter events, 0.1 us)
Async XLA Ops:
  0.0 12.2 %copy-start = (bf16[2048,2048]{1,0:T(8,128)(2,1)S(1)}, bf16[2048,2048]{1,0:T(8,128)(2,1)}, u32[]{:S(2)}) copy-start(bf16[2048,2048]{1,0:T(8,128)(2,1)} %refs_2_.13) | copy-start | bytes 25165828
  0.0 13.9 %collective-permute-start.3 = (bf16[2048,2048]{1,0:T(8,128)(2,1)}, bf16[2048,2048]{1,0:T(8,128)(2,1)}, u32[]{:S(2)}, u32[]{:S(2)}) collective-permute-start(bf16[2048,2048]{1,0:T(8,128)(2,1)} %refs_2_.13), channel_id=1, source_target_pairs={{0,8},{8,0},{16,24},{24,16},{1,9},{9,1},{17,25},{25,17},{2,10},{10... | collective-permute-start | bytes 25165832 | tf_op jit(solution)/shard_map/ppermute | solution.py:404
  9.1 4.5 %collective-permute-start = (bf16[528,128]{1,0:T(8,128)(2,1)}, bf16[528,128]{1,0:T(8,128)(2,1)S(1)}, u32[]{:S(2)}, u32[]{:S(2)}) collective-permute-start(bf16[528,128]{1,0:T(8,128)(2,1)} %get-tuple-element.26), channel_id=1, source_target_pairs={{0,8},{8,0},{16,24},{24,16},{1,9},{9,1},{17,25},{25,17},{2,10},{10... | collective-permute-start | bytes 405512 | tf_op jit(solution)/shard_map/ppermute | solution.py:404
  9.5 8.0 %collective-permute-start.1 = (bf16[528,128]{1,0:T(8,128)(2,1)}, bf16[528,128]{1,0:T(8,128)(2,1)S(1)}, u32[]{:S(2)}, u32[]{:S(2)}) collective-permute-start(bf16[528,128]{1,0:T(8,128)(2,1)} %get-tuple-element.29), channel_id=1, source_target_pairs={{0,16},{8,24},{16,0},{24,8},{1,17},{9,25},{17,1},{25,9},{2,18},{10... | collective-permute-start | bytes 405512 | tf_op jit(solution)/shard_map/ppermute | solution.py:404
  12.2 1.5 %copy-start.2 = (bf16[528,128]{1,0:T(8,128)(2,1)S(1)}, bf16[528,128]{1,0:T(8,128)(2,1)}, u32[]{:S(2)}) copy-start(bf16[528,128]{1,0:T(8,128)(2,1)} %get-tuple-element.25.own_ref) | copy-start | bytes 405508
  12.2 6.8 %collective-permute-start.2 = (bf16[528,128]{1,0:T(8,128)(2,1)}, bf16[528,128]{1,0:T(8,128)(2,1)S(1)}, u32[]{:S(2)}, u32[]{:S(2)}) collective-permute-start(bf16[528,128]{1,0:T(8,128)(2,1)} %get-tuple-element.30), channel_id=1, source_target_pairs={{0,24},{8,16},{16,8},{24,0},{1,25},{9,17},{17,9},{25,1},{2,26},{10... | collective-permute-start | bytes 405512 | tf_op jit(solution)/shard_map/ppermute | solution.py:404
  13.9 5.1 %copy-start.1 = (f32[16,128,128]{2,1,0:T(8,128)S(1)}, f32[16,128,128]{2,1,0:T(8,128)}, u32[]{:S(2)}) copy-start(f32[16,128,128]{2,1,0:T(8,128)} %base_ref.1) | copy-start | bytes 3145732
  19.7 2.7 %collective-permute-start.4 = (bf16[16,128,128]{2,1,0:T(8,128)(2,1)S(1)}, bf16[16,128,128]{2,1,0:T(8,128)(2,1)S(1)}, u32[]{:S(2)}, u32[]{:S(2)}) collective-permute-start(bf16[16,128,128]{2,1,0:T(8,128)(2,1)S(1)} %far.1.mass_ref), channel_id=1, source_target_pairs={{0,8},{8,0},{16,24},{24,16},{1,9},{9,1},{17,25},{25,17},{2,10},{10... | collective-permute-start | bytes 1572872 | tf_op jit(solution)/shard_map/ppermute | solution.py:404
  24.9 9.2 %collective-permute-start.7 = (bf16[2,512,256]{2,1,0:T(8,128)(2,1)S(1)}, bf16[2,512,256]{2,1,0:T(8,128)(2,1)S(1)}, u32[]{:S(2)}, u32[]{:S(2)}) collective-permute-start(bf16[2,512,256]{2,1,0:T(8,128)(2,1)S(1)} %get-tuple-element.36.refs_4_), channel_id=1, source_target_pairs={{0,16},{1,17},{2,18},{3,19},{4,20},{5,21},{6,22},{7,23},{8,9},{9,8... | collective-permute-start | bytes 1572872 | tf_op jit(solution)/shard_map/ppermute | solution.py:412
  29.0 13.5 %collective-permute-start.5 = (bf16[2,512,256]{2,1,0:T(8,128)(2,1)S(1)}, bf16[2,512,256]{2,1,0:T(8,128)(2,1)S(1)}, u32[]{:S(2)}, u32[]{:S(2)}) collective-permute-start(bf16[2,512,256]{2,1,0:T(8,128)(2,1)S(1)} %product.7.refs_4_), channel_id=1, source_target_pairs={{0,16},{1,17},{2,18},{3,19},{4,20},{5,21},{6,22},{7,23},{8,9},{9,8... | collective-permute-start | bytes 1572872 | tf_op jit(solution)/shard_map/ppermute | solution.py:412
  36.8 15.1 %collective-permute-start.13 = (bf16[2,512,256]{2,1,0:T(8,128)(2,1)S(1)}, bf16[2,512,256]{2,1,0:T(8,128)(2,1)S(1)}, u32[]{:S(2)}, u32[]{:S(2)}) collective-permute-start(bf16[2,512,256]{2,1,0:T(8,128)(2,1)S(1)} %product.13), channel_id=1, source_target_pairs={{0,16},{1,17},{2,18},{3,19},{4,20},{5,21},{6,22},{7,23},{8,9},{9,8... | collective-permute-start | bytes 1572872 | tf_op jit(solution)/shard_map/ppermute | solution.py:412
  38.6 9.2 %collective-permute-start.8 = (bf16[512,256]{1,0:T(8,128)(2,1)S(1)}, bf16[512,256]{1,0:T(8,128)(2,1)S(1)}, u32[]{:S(2)}, u32[]{:S(2)}) collective-permute-start(bf16[512,256]{1,0:T(8,128)(2,1)S(1)} %get-tuple-element.40), channel_id=1, source_target_pairs={{0,1},{1,0},{2,3},{3,2},{4,5},{5,4},{6,7},{7,6},{8,24},{9,25},{10,... | collective-permute-start | bytes 786440 | tf_op jit(solution)/shard_map/ppermute | solution.py:412
  45.0 14.9 %collective-permute-start.10 = (bf16[2,512,256]{2,1,0:T(8,128)(2,1)S(1)}, bf16[2,512,256]{2,1,0:T(8,128)(2,1)S(1)}, u32[]{:S(2)}, u32[]{:S(2)}) collective-permute-start(bf16[2,512,256]{2,1,0:T(8,128)(2,1)S(1)} %product.10.refs_4_), channel_id=1, source_target_pairs={{0,16},{1,17},{2,18},{3,19},{4,20},{5,21},{6,22},{7,23},{8,9},{9,8... | collective-permute-start | bytes 1572872 | tf_op jit(solution)/shard_map/ppermute | solution.py:412
  45.6 9.2 %collective-permute-start.6 = (bf16[512,256]{1,0:T(8,128)(2,1)S(1)}, bf16[512,256]{1,0:T(8,128)(2,1)S(1)}, u32[]{:S(2)}, u32[]{:S(2)}) collective-permute-start(bf16[512,256]{1,0:T(8,128)(2,1)S(1)} %get-tuple-element.38), channel_id=1, source_target_pairs={{0,1},{1,0},{2,3},{3,2},{4,5},{5,4},{6,7},{7,6},{8,24},{9,25},{10,... | collective-permute-start | bytes 786440 | tf_op jit(solution)/shard_map/ppermute | solution.py:412
  47.9 6.9 %collective-permute-start.9 = (bf16[512,256]{1,0:T(8,128)(2,1)S(1)}, bf16[512,256]{1,0:T(8,128)(2,1)S(1)}, u32[]{:S(2)}, u32[]{:S(2)}) collective-permute-start(bf16[512,256]{1,0:T(8,128)(2,1)S(1)} %add_second.5.refs_5_), channel_id=1, source_target_pairs={{0,2},{1,3},{2,0},{3,1},{4,6},{5,7},{6,4},{7,5},{8,10},{9,11},{10,... | collective-permute-start | bytes 786440 | tf_op jit(solution)/shard_map/ppermute | solution.py:412
  52.0 9.3 %collective-permute-start.14 = (bf16[512,256]{1,0:T(8,128)(2,1)S(1)}, bf16[512,256]{1,0:T(8,128)(2,1)S(1)}, u32[]{:S(2)}, u32[]{:S(2)}) collective-permute-start(bf16[512,256]{1,0:T(8,128)(2,1)S(1)} %get-tuple-element.44), channel_id=1, source_target_pairs={{0,1},{1,0},{2,3},{3,2},{4,5},{5,4},{6,7},{7,6},{8,24},{9,25},{10,... | collective-permute-start | bytes 786440 | tf_op jit(solution)/shard_map/ppermute | solution.py:412
  54.9 12.4 %collective-permute-start.12 = (bf16[512,256]{1,0:T(8,128)(2,1)S(1)}, bf16[512,256]{1,0:T(8,128)(2,1)S(1)}, u32[]{:S(2)}, u32[]{:S(2)}) collective-permute-start(bf16[512,256]{1,0:T(8,128)(2,1)S(1)} %add_second.6.refs_5_), channel_id=1, source_target_pairs={{0,4},{1,5},{2,6},{3,7},{4,0},{5,1},{6,2},{7,3},{8,12},{9,13},{10,... | collective-permute-start | bytes 786440 | tf_op jit(solution)/shard_map/ppermute | solution.py:412
  60.1 6.4 %collective-permute-start.11 = (bf16[512,256]{1,0:T(8,128)(2,1)S(1)}, bf16[512,256]{1,0:T(8,128)(2,1)S(1)}, u32[]{:S(2)}, u32[]{:S(2)}) collective-permute-start(bf16[512,256]{1,0:T(8,128)(2,1)S(1)} %get-tuple-element.42), channel_id=1, source_target_pairs={{0,1},{1,0},{2,3},{3,2},{4,5},{5,4},{6,7},{7,6},{8,24},{9,25},{10,... | collective-permute-start | bytes 786440 | tf_op jit(solution)/shard_map/ppermute | solution.py:412
  61.4 9.0 %collective-permute-start.15 = (bf16[512,256]{1,0:T(8,128)(2,1)S(1)}, bf16[512,256]{1,0:T(8,128)(2,1)S(1)}, u32[]{:S(2)}, u32[]{:S(2)}) collective-permute-start(bf16[512,256]{1,0:T(8,128)(2,1)S(1)} %add_second.8), channel_id=1, source_target_pairs={{0,2},{1,3},{2,0},{3,1},{4,6},{5,7},{6,4},{7,5},{8,10},{9,11},{10,... | collective-permute-start | bytes 786440 | tf_op jit(solution)/shard_map/ppermute | solution.py:412
